TPU v7x, 32 devices: a whole 2x2x4 slice. The times are simulated.
32 devices in a mesh: groups: 2 (over x), tm: 4 (over y, core), chan: 4 (over z).
Axes of the slice: x: 2, y: 2, z: 4, core: 2. Of those that a mesh axis runs over, the one named last changes fastest.
Arguments:
- records: bfloat16 [1536, 1024], P(('groups', 'tm'), 'chan'), parts along dimension 0, may hold values from -6 to 6
- cotangent: bfloat16 [1536, 1024], P(('groups', 'tm'), 'chan'), parts along dimension 0, may hold values from -6 to 6
- filter_weight: bfloat16 [4, 2, 1024, 1024], P(None, None, 'tm', 'chan'), may hold values from -0.125 to 0.125
- gate_weight: bfloat16 [4, 2, 1024, 1024], P(None, None, 'tm', 'chan'), may hold values from -0.125 to 0.125
- mix_weight: bfloat16 [4, 1024, 1024], P(None, 'chan', 'tm'), may hold values from -0.1875 to 0.1875
Outputs:
- output: bfloat16 [1536, 1024], P(('groups', 'tm'), 'chan'), parts along dimension 0
- input_grad: bfloat16 [1536, 1024], P(('groups', 'tm'), 'chan'), parts along dimension 0
There are 2 independent parts, one for each index of `groups`. A program takes and returns all parts, laid end to end along the dimension named above; an argument that names none is the same for every part. Nothing has to cross between parts.
All inputs are finite; a program needn't handle non-finite values.
Results may differ from a plain program's by a relative error of at most 0.018.
Values may be sent and summed in bfloat16 or wider, within the bound.
No kernel may reach another device: no remote copies, remote signals or barrier semaphores. Data moves between devices by JAX's collectives and lax.ppermute only.
A program may use at most 64 MiB of HBM per device.

v0:
```python
import jax
import jax.numpy as jnp
from jax import lax
from jax.sharding import PartitionSpec as P


def shifted(shard, axis, by):
    peers = lax.axis_size(axis)
    pairs = [(i, i + by) for i in range(peers) if 0 <= i + by < peers]
    return lax.ppermute(shard, axis, pairs)


def right_product(left, panel):
    return lax.dot_general(
        left, panel, (((1,), (1,)), ((), ())), preferred_element_type=jnp.float32
    )


def local(records, cotangent, filter_weight, gate_weight, mix_weight):
    layer_count = filter_weight.shape[0]
    tm_count = lax.axis_size("tm")
    signal = records
    stored = []
    for layer_index in range(layer_count):
        span_shards = 2**layer_index
        filt_panel, gate_panel, mix_panel = (
            lax.all_gather(filter_weight[layer_index], "tm", axis=1, tiled=True),
            lax.all_gather(gate_weight[layer_index], "tm", axis=1, tiled=True),
            lax.all_gather(mix_weight[layer_index], "tm", axis=1, tiled=True),
        )
        whole_rows = lax.all_gather(signal, "chan", axis=1, tiled=True)
        if span_shards < tm_count:
            earlier = shifted(whole_rows, "tm", span_shards)
        else:
            earlier = jnp.zeros_like(whole_rows)
        pre_filter = jnp.dot(earlier, filt_panel[0], preferred_element_type=jnp.float32) + jnp.dot(
            whole_rows, filt_panel[1], preferred_element_type=jnp.float32
        )
        pre_gate = jnp.dot(earlier, gate_panel[0], preferred_element_type=jnp.float32) + jnp.dot(
            whole_rows, gate_panel[1], preferred_element_type=jnp.float32
        )
        gated = (jnp.tanh(pre_filter) * jax.nn.sigmoid(pre_gate)).astype(jnp.bfloat16)
        mix_term = jnp.dot(gated, mix_panel, preferred_element_type=jnp.float32)
        mixed = lax.psum_scatter(
            mix_term.astype(jnp.bfloat16), "chan", scatter_dimension=1, tiled=True
        ).astype(jnp.float32)
        signal = (signal.astype(jnp.float32) + mixed).astype(jnp.bfloat16)
        stored.append((pre_filter, pre_gate, filt_panel, gate_panel, mix_panel))
    grad_now = cotangent
    for layer_index in reversed(range(layer_count)):
        span_shards = 2**layer_index
        pre_filter, pre_gate, filt_panel, gate_panel, mix_panel = stored[layer_index]
        grad_whole = lax.all_gather(grad_now, "chan", axis=1, tiled=True)
        grad_z = right_product(grad_whole, mix_panel)
        tanh_value = jnp.tanh(pre_filter)
        sig_value = jax.nn.sigmoid(pre_gate)
        grad_filt = (grad_z * sig_value * (1.0 - tanh_value * tanh_value)).astype(jnp.bfloat16)
        grad_gate = (grad_z * tanh_value * sig_value * (1.0 - sig_value)).astype(jnp.bfloat16)
        near_term = right_product(grad_filt, filt_panel[1]) + right_product(
            grad_gate, gate_panel[1]
        )
        far_term = right_product(grad_filt, filt_panel[0]) + right_product(grad_gate, gate_panel[0])
        if span_shards < tm_count:
            advanced = shifted(far_term.astype(jnp.bfloat16), "tm", -span_shards).astype(
                far_term.dtype
            )
        else:
            advanced = jnp.zeros_like(far_term)
        returned = lax.psum_scatter(
            (near_term + advanced).astype(jnp.bfloat16), "chan", scatter_dimension=1, tiled=True
        ).astype(jnp.float32)
        grad_now = (grad_now.astype(jnp.float32) + returned).astype(jnp.bfloat16)
    return (signal, grad_now)


def solution(mesh):
    return jax.shard_map(
        local,
        mesh=mesh,
        in_specs=(
            P(("groups", "tm"), "chan"),
            P(("groups", "tm"), "chan"),
            P(None, None, "tm", "chan"),
            P(None, None, "tm", "chan"),
            P(None, "chan", "tm"),
        ),
        out_specs=(P(("groups", "tm"), "chan"), P(("groups", "tm"), "chan")),
        check_vma=False,
    )
```

profile of v0, /device:TPU:0, one launch (start us, length us, event | category | flops | bytes accessed | tf_op | source)
XLA Modules:
  0.0 408.0 jit_solution(5573307418238194053)
XLA Ops:
  7.2 2.3 fusion.67
  10.7 16.4 %all_gather.60 = bf16[192,1024]{1,0:T(8,128)(2,1)S(1)} all-gather(bf16[192,256]{1,0:T(8,128)(2,1)S(1)} %copy-done.34), channel_id=1, replica_groups=mesh['groups'=2,'tm'=4,'chan'=4] {'chan'}, dimensions={1}, use_global_device_ids=true | all-gather | bytes 491520 | tf_op jit(solution)/shard_map/all_gather | solution.py:31
  29.2 7.7 %all-gather.2 = bf16[1,256,1024]{2,1,0:T(8,128)(2,1)S(1)} all-gather(bf16[1,256,256]{2,1,0:T(8,128)(2,1)S(1)} %get-tuple-element.14), channel_id=4, replica_groups=mesh['groups'=2,'tm'=4,'chan'=4] {'tm'}, dimensions={2}, use_global_device_ids=true | all-gather | bytes 655360 | tf_op jit(solution)/shard_map/all_gather | solution.py:29
  38.3 9.2 %all-gather.23.cloned.1.call-done = bf16[1,2,1024,256]{3,2,1,0:T(8,128)(2,1)} async-done(((bf16[1,2,256,256]{3,2,1,0:T(8,128)(2,1)}), bf16[1,2,1024,256]{3,2,1,0:T(8,128)(2,1)}) %all-gather.23.cloned.1.call-update) | async-done | bytes 1048592 | tf_op jit(solution)/shard_map/all_gather | solution.py:28
  54.2 7.2 %all-gather.5 = bf16[1,256,1024]{2,1,0:T(8,128)(2,1)S(1)} all-gather(bf16[1,256,256]{2,1,0:T(8,128)(2,1)S(1)} %get-tuple-element.15), channel_id=7, replica_groups=mesh['groups'=2,'tm'=4,'chan'=4] {'tm'}, dimensions={2}, use_global_device_ids=true | all-gather | bytes 655360 | tf_op jit(solution)/shard_map/all_gather | solution.py:29
  61.3 11.4 %reduce-scatter.9.cloned.1.call-done = bf16[192,256]{1,0:T(8,128)(2,1)} async-done(((bf16[192,1024]{1,0:T(8,128)(2,1)}), bf16[192,256]{1,0:T(8,128)(2,1)}) %reduce-scatter.9.cloned.1.call-update) | async-done | bytes 98320 | tf_op jit(solution)/shard_map/reduce_scatter | solution.py:44
  73.6 14.7 %all_gather.64 = bf16[192,1024]{1,0:T(8,128)(2,1)S(1)} all-gather(bf16[192,256]{1,0:T(8,128)(2,1)S(1)} %add_convert_fusion.9), channel_id=1, replica_groups=mesh['groups'=2,'tm'=4,'chan'=4] {'chan'}, dimensions={1}, use_global_device_ids=true | all-gather | bytes 491520 | tf_op jit(solution)/shard_map/all_gather | solution.py:31
  88.4 4.0 collective-permute-start.1
  92.4 2.1 fusion.46
  94.5 13.4 %all-gather.27.cloned.1.call-done = bf16[1,2,1024,256]{3,2,1,0:T(8,128)(2,1)} async-done(((bf16[1,2,256,256]{3,2,1,0:T(8,128)(2,1)}), bf16[1,2,1024,256]{3,2,1,0:T(8,128)(2,1)}) %all-gather.27.cloned.1.call-update) | async-done | bytes 1048592 | tf_op jit(solution)/shard_map/all_gather | solution.py:28
  115.5 10.2 %all-gather.11 = bf16[1,256,1024]{2,1,0:T(8,128)(2,1)S(1)} all-gather(bf16[1,256,256]{2,1,0:T(8,128)(2,1)S(1)} %copy-done.33), channel_id=13, replica_groups=mesh['groups'=2,'tm'=4,'chan'=4] {'tm'}, dimensions={2}, use_global_device_ids=true | all-gather | bytes 655360 | tf_op jit(solution)/shard_map/all_gather | solution.py:29
  125.7 7.3 %all-gather.8 = bf16[1,256,1024]{2,1,0:T(8,128)(2,1)S(1)} all-gather(bf16[1,256,256]{2,1,0:T(8,128)(2,1)S(1)} %copy-done.32), channel_id=10, replica_groups=mesh['groups'=2,'tm'=4,'chan'=4] {'tm'}, dimensions={2}, use_global_device_ids=true | all-gather | bytes 655360 | tf_op jit(solution)/shard_map/all_gather | solution.py:29
  133.0 2.0 fusion.27
  135.0 12.4 %all-gather.31.cloned.1.call-done = bf16[1,2,1024,256]{3,2,1,0:T(8,128)(2,1)} async-done(((bf16[1,2,256,256]{3,2,1,0:T(8,128)(2,1)}), bf16[1,2,1024,256]{3,2,1,0:T(8,128)(2,1)}) %all-gather.31.cloned.1.call-update) | async-done | bytes 1048592 | tf_op jit(solution)/shard_map/all_gather | solution.py:28
  147.3 2.0 fusion.26
  149.3 21.0 %reduce-scatter.11.cloned.1.call-done = bf16[192,256]{1,0:T(8,128)(2,1)} async-done(((bf16[192,1024]{1,0:T(8,128)(2,1)}), bf16[192,256]{1,0:T(8,128)(2,1)}) %reduce-scatter.11.cloned.1.call-update) | async-done | bytes 98320 | tf_op jit(solution)/shard_map/reduce_scatter | solution.py:44
  171.4 14.8 %all_gather.69 = bf16[192,1024]{1,0:T(8,128)(2,1)S(1)} all-gather(bf16[192,256]{1,0:T(8,128)(2,1)S(1)} %add_convert_fusion.8), channel_id=1, replica_groups=mesh['groups'=2,'tm'=4,'chan'=4] {'chan'}, dimensions={1}, use_global_device_ids=true | all-gather | bytes 491520 | tf_op jit(solution)/shard_map/all_gather | solution.py:31
  189.9 15.1 %all_gather.76 = bf16[192,1024]{1,0:T(8,128)(2,1)S(1)} all-gather(bf16[192,256]{1,0:T(8,128)(2,1)S(1)} %copy-done.35), channel_id=1, replica_groups=mesh['groups'=2,'tm'=4,'chan'=4] {'chan'}, dimensions={1}, use_global_device_ids=true | all-gather | bytes 491520 | tf_op jit(solution)/shard_map/all_gather | solution.py:53
  206.0 2.0 fusion.25
  208.0 2.0 fusion.24
  210.0 18.0 %reduce-scatter.13.cloned.1.call-done = bf16[192,256]{1,0:T(8,128)(2,1)} async-done(((bf16[192,1024]{1,0:T(8,128)(2,1)}), bf16[192,256]{1,0:T(8,128)(2,1)}) %reduce-scatter.13.cloned.1.call-update) | async-done | bytes 98320 | tf_op jit(solution)/shard_map/reduce_scatter | solution.py:44
  229.7 14.7 %all_gather.73 = bf16[192,1024]{1,0:T(8,128)(2,1)S(1)} all-gather(bf16[192,256]{1,0:T(8,128)(2,1)S(1)} %add_convert_fusion.7), channel_id=1, replica_groups=mesh['groups'=2,'tm'=4,'chan'=4] {'chan'}, dimensions={1}, use_global_device_ids=true | all-gather | bytes 491520 | tf_op jit(solution)/shard_map/all_gather | solution.py:31
  249.0 18.8 %reduce-scatter.17.cloned.1.call-done = bf16[192,256]{1,0:T(8,128)(2,1)} async-done(((bf16[192,1024]{1,0:T(8,128)(2,1)}), bf16[192,256]{1,0:T(8,128)(2,1)}) %reduce-scatter.17.cloned.1.call-update) | async-done | bytes 98320 | tf_op jit(solution)/shard_map/reduce_scatter | solution.py:69
  269.5 14.7 %all_gather.77 = bf16[192,1024]{1,0:T(8,128)(2,1)S(1)} all-gather(bf16[192,256]{1,0:T(8,128)(2,1)S(1)} %add_convert_fusion.5), channel_id=1, replica_groups=mesh['groups'=2,'tm'=4,'chan'=4] {'chan'}, dimensions={1}, use_global_device_ids=true | all-gather | bytes 491520 | tf_op jit(solution)/shard_map/all_gather | solution.py:53
  287.6 18.9 %reduce-scatter.19.cloned.1.call-done = bf16[192,256]{1,0:T(8,128)(2,1)} async-done(((bf16[192,1024]{1,0:T(8,128)(2,1)}), bf16[192,256]{1,0:T(8,128)(2,1)}) %reduce-scatter.19.cloned.1.call-update) | async-done | bytes 98320 | tf_op jit(solution)/shard_map/reduce_scatter | solution.py:69
  307.4 14.9 %all_gather.78 = bf16[192,1024]{1,0:T(8,128)(2,1)S(1)} all-gather(bf16[192,256]{1,0:T(8,128)(2,1)S(1)} %add_convert_fusion.4), channel_id=1, replica_groups=mesh['groups'=2,'tm'=4,'chan'=4] {'chan'}, dimensions={1}, use_global_device_ids=true | all-gather | bytes 491520 | tf_op jit(solution)/shard_map/all_gather | solution.py:53
  325.9 8.0 %collective-permute-done.2 = bf16[192,1024]{1,0:T(8,128)(2,1)S(1)} collective-permute-done((bf16[192,1024]{1,0:T(8,128)(2,1)S(1)}, bf16[192,1024]{1,0:T(8,128)(2,1)S(1)}, u32[]{:S(2)}, u32[]{:S(2)}) %collective-permute-start.2) | collective-permute-done | bytes 393248 | tf_op jit(solution)/shard_map/ppermute | solution.py:10
  337.1 15.9 %reduce-scatter.21.cloned.1.call-done = bf16[192,256]{1,0:T(8,128)(2,1)} async-done(((bf16[192,1024]{1,0:T(8,128)(2,1)}), bf16[192,256]{1,0:T(8,128)(2,1)}) %reduce-scatter.21.cloned.1.call-update) | async-done | bytes 98320 | tf_op jit(solution)/shard_map/reduce_scatter | solution.py:69
  353.9 16.0 %all_gather.79 = bf16[192,1024]{1,0:T(8,128)(2,1)S(1)} all-gather(bf16[192,256]{1,0:T(8,128)(2,1)S(1)} %add_convert_fusion.3), channel_id=1, replica_groups=mesh['groups'=2,'tm'=4,'chan'=4] {'chan'}, dimensions={1}, use_global_device_ids=true | all-gather | bytes 491520 | tf_op jit(solution)/shard_map/all_gather | solution.py:53
  373.5 2.0 collective-permute-done.3
  377.4 1.6 add_convert_fusion.6
  379.0 20.9 %reduce-scatter.23.cloned.1.call-done = bf16[192,256]{1,0:T(8,128)(2,1)} async-done(((bf16[192,1024]{1,0:T(8,128)(2,1)}), bf16[192,256]{1,0:T(8,128)(2,1)}) %reduce-scatter.23.cloned.1.call-update) | async-done | bytes 98320 | tf_op jit(solution)/shard_map/reduce_scatter | solution.py:69
  (165 shorter events, 52.0 us)
Async XLA Ops:
  7.2 29.6 %all-gather.21.cloned.1.call-start = ((), (), s32[]{:S(2)}) async-start(), calls=%async_computation.16 | async-start | bytes 1310720 | tf_op jit(solution)/shard_map/all_gather | solution.py:27
  9.6 37.9 %all-gather.23.cloned.1.call-start = ((), (), s32[]{:S(2)}) async-start(), calls=%async_computation.17 | async-start | bytes 1310720 | tf_op jit(solution)/shard_map/all_gather | solution.py:28
  10.6 17.8 %copy-start.31 = (bf16[4,256,256]{2,1,0:T(8,128)(2,1)S(1)}, bf16[4,256,256]{2,1,0:T(8,128)(2,1)}, u32[]{:S(2)}) copy-start(bf16[4,256,256]{2,1,0:T(8,128)(2,1)} %param.9) | copy-start | bytes 1572868
  10.7 62.0 %reduce-scatter.9.cloned.1.call-start = ((), (), s32[]{:S(2)}) async-start(), calls=%async_computation.8 | async-start | bytes 491520 | tf_op jit(solution)/shard_map/reduce_scatter | solution.py:44
  27.1 21.8 %collective-permute-start = (bf16[192,1024]{1,0:T(8,128)(2,1)S(1)}, bf16[192,1024]{1,0:T(8,128)(2,1)S(1)}, u32[]{:S(2)}, u32[]{:S(2)}) collective-permute-start(bf16[192,1024]{1,0:T(8,128)(2,1)S(1)} %all_gather.60), channel_id=1, source_target_pairs={{0,4},{4,8},{8,12},{1,5},{5,9},{9,13},{2,6},{6,10},{10,14},{3,7},{... | collective-permute-start | bytes 1179656 | tf_op jit(solution)/shard_map/ppermute | solution.py:10
  51.6 40.8 %all-gather.25.cloned.1.call-start = ((), (), s32[]{:S(2)}) async-start(), calls=%async_computation.18 | async-start | bytes 1310720 | tf_op jit(solution)/shard_map/all_gather | solution.py:27
  52.2 55.7 %all-gather.27.cloned.1.call-start = ((), (), s32[]{:S(2)}) async-start(), calls=%async_computation.19 | async-start | bytes 1310720 | tf_op jit(solution)/shard_map/all_gather | solution.py:28
  52.8 80.2 %all-gather.29.cloned.1.call-start = ((), (), s32[]{:S(2)}) async-start(), calls=%async_computation.20 | async-start | bytes 1310720 | tf_op jit(solution)/shard_map/all_gather | solution.py:27
  53.4 94.0 %all-gather.31.cloned.1.call-start = ((), (), s32[]{:S(2)}) async-start(), calls=%async_computation.21 | async-start | bytes 1310720 | tf_op jit(solution)/shard_map/all_gather | solution.py:28
  54.1 116.2 %reduce-scatter.11.cloned.1.call-start = ((), (), s32[]{:S(2)}) async-start(), calls=%async_computation.9 | async-start | bytes 491520 | tf_op jit(solution)/shard_map/reduce_scatter | solution.py:44
  88.4 20.9 %collective-permute-start.1 = (bf16[192,1024]{1,0:T(8,128)(2,1)S(1)}, bf16[192,1024]{1,0:T(8,128)(2,1)}, u32[]{:S(2)}, u32[]{:S(2)}) collective-permute-start(bf16[192,1024]{1,0:T(8,128)(2,1)S(1)} %all_gather.64), channel_id=1, source_target_pairs={{0,8},{4,12},{1,9},{5,13},{2,10},{6,14},{3,11},{7,15},{16,24},{20,... | collective-permute-start | bytes 1179656 | tf_op jit(solution)/shard_map/ppermute | solution.py:10
  92.4 16.9 %copy-start.1 = (bf16[1,2,1024,256]{3,2,1,0:T(8,128)(2,1)S(1)}, bf16[1,2,1024,256]{3,2,1,0:T(8,128)(2,1)}, u32[]{:S(2)}) copy-start(bf16[1,2,1024,256]{3,2,1,0:T(8,128)(2,1)} %all-gather.25.cloned.1.call-done) | copy-start | bytes 3145732
  113.8 92.2 %all-gather.33.cloned.1.call-start = ((), (), s32[]{:S(2)}) async-start(), calls=%async_computation.22 | async-start | bytes 1310720 | tf_op jit(solution)/shard_map/all_gather | solution.py:27
  114.6 93.5 %all-gather.35.cloned.1.call-start = ((), (), s32[]{:S(2)}) async-start(), calls=%async_computation.23 | async-start | bytes 1310720 | tf_op jit(solution)/shard_map/all_gather | solution.py:28
  115.1 112.9 %reduce-scatter.13.cloned.1.call-start = ((), (), s32[]{:S(2)}) async-start(), calls=%async_computation.10 | async-start | bytes 491520 | tf_op jit(solution)/shard_map/reduce_scatter | solution.py:44
  135.0 35.4 %copy-start.22 = (bf16[192,256]{1,0:T(8,128)(2,1)S(1)}, bf16[192,256]{1,0:T(8,128)(2,1)}, u32[]{:S(2)}) copy-start(bf16[192,256]{1,0:T(8,128)(2,1)} %copy-done.21) | copy-start | bytes 294916
  170.3 17.3 %copy-start.36 = (bf16[1,2,1024,256]{3,2,1,0:T(8,128)(2,1)S(1)}, bf16[1,2,1024,256]{3,2,1,0:T(8,128)(2,1)}, u32[]{:S(2)}) copy-start(bf16[1,2,1024,256]{3,2,1,0:T(8,128)(2,1)} %all-gather.31.cloned.1.call-done) | copy-start | bytes 3145732
  189.0 78.8 %reduce-scatter.17.cloned.1.call-start = ((), (), s32[]{:S(2)}) async-start(), calls=%async_computation.12 | async-start | bytes 491520 | tf_op jit(solution)/shard_map/reduce_scatter | solution.py:69
  208.0 20.0 %copy-start.24 = (bf16[192,256]{1,0:T(8,128)(2,1)S(1)}, bf16[192,256]{1,0:T(8,128)(2,1)}, u32[]{:S(2)}) copy-start(bf16[192,256]{1,0:T(8,128)(2,1)} %copy-done.23) | copy-start | bytes 294916
  228.0 17.8 %copy-start.38 = (bf16[1,2,1024,256]{3,2,1,0:T(8,128)(2,1)S(1)}, bf16[1,2,1024,256]{3,2,1,0:T(8,128)(2,1)}, u32[]{:S(2)}) copy-start(bf16[1,2,1024,256]{3,2,1,0:T(8,128)(2,1)} %all-gather.35.cloned.1.call-done) | copy-start | bytes 3145732
  249.0 57.5 %reduce-scatter.19.cloned.1.call-start = ((), (), s32[]{:S(2)}) async-start(), calls=%async_computation.13 | async-start | bytes 491520 | tf_op jit(solution)/shard_map/reduce_scatter | solution.py:69
  267.8 16.8 %copy-start.17 = (bf16[1,2,1024,256]{3,2,1,0:T(8,128)(2,1)S(1)}, bf16[1,2,1024,256]{3,2,1,0:T(8,128)(2,1)}, u32[]{:S(2)}) copy-start(bf16[1,2,1024,256]{3,2,1,0:T(8,128)(2,1)} %all-gather.29.cloned.1.call-done) | copy-start | bytes 3145732
  287.5 19.0 %copy-start.26 = (bf16[192,256]{1,0:T(8,128)(2,1)S(1)}, bf16[192,256]{1,0:T(8,128)(2,1)}, u32[]{:S(2)}) copy-start(bf16[192,256]{1,0:T(8,128)(2,1)} %copy-done.25) | copy-start | bytes 294916
  287.5 65.5 %reduce-scatter.21.cloned.1.call-start = ((), (), s32[]{:S(2)}) async-start(), calls=%async_computation.14 | async-start | bytes 491520 | tf_op jit(solution)/shard_map/reduce_scatter | solution.py:69
  306.4 15.9 %copy-start.14 = (f32[192,256]{1,0:T(8,128)S(1)}, f32[192,256]{1,0:T(8,128)}, u32[]{:S(2)}) copy-start(f32[192,256]{1,0:T(8,128)} %copy-done.13) | copy-start | bytes 589828
  306.5 15.9 %copy-start.30 = (f32[192,256]{1,0:T(8,128)S(1)}, f32[192,256]{1,0:T(8,128)}, u32[]{:S(2)}) copy-start(f32[192,256]{1,0:T(8,128)} %copy-done.29) | copy-start | bytes 589828
  324.3 9.7 %collective-permute-start.2 = (bf16[192,1024]{1,0:T(8,128)(2,1)S(1)}, bf16[192,1024]{1,0:T(8,128)(2,1)S(1)}, u32[]{:S(2)}, u32[]{:S(2)}) collective-permute-start(bf16[192,1024]{1,0:T(8,128)(2,1)S(1)} %fusion.2), channel_id=1, source_target_pairs={{8,0},{12,4},{9,1},{13,5},{10,2},{14,6},{11,3},{15,7},{24,16},{28,... | collective-permute-start | bytes 1179656 | tf_op jit(solution)/shard_map/ppermute | solution.py:10
  335.1 41.5 %reduce-scatter.15.cloned.1.call-start = ((), (), s32[]{:S(2)}) async-start(), calls=%async_computation.11 | async-start | bytes 491520 | tf_op jit(solution)/shard_map/reduce_scatter | solution.py:44
  337.0 62.9 %reduce-scatter.23.cloned.1.call-start = ((), (), s32[]{:S(2)}) async-start(), calls=%async_computation.15 | async-start | bytes 491520 | tf_op jit(solution)/shard_map/reduce_scatter | solution.py:69
  353.9 16.0 %copy-start.12 = (f32[192,256]{1,0:T(8,128)S(1)}, f32[192,256]{1,0:T(8,128)}, u32[]{:S(2)}) copy-start(f32[192,256]{1,0:T(8,128)} %copy-done.11) | copy-start | bytes 589828
  353.9 16.0 %copy-start.28 = (f32[192,256]{1,0:T(8,128)S(1)}, f32[192,256]{1,0:T(8,128)}, u32[]{:S(2)}) copy-start(f32[192,256]{1,0:T(8,128)} %copy-done.27) | copy-start | bytes 589828
  371.8 3.6 collective-permute-start.3
  (29 other events, 95.0 us)
Sparse Core Ops, SparseCore 0:
  9.7 19.4 all-gather.20
  30.7 16.7 all-gather.22
  51.7 20.9 reduce-scatter.8
  74.2 15.0 all-gather.24
  90.8 17.0 all-gather.26
  109.4 19.5 all-gather.28
  130.6 16.7 all-gather.30
  149.7 20.5 reduce-scatter.10
  171.9 14.9 all-gather.32
  188.3 16.7 all-gather.34
  207.4 20.6 reduce-scatter.12
  249.1 18.6 reduce-scatter.16
  287.6 18.7 reduce-scatter.18
  335.2 17.7 reduce-scatter.20
  355.1 19.6 reduce-scatter.14
  377.1 22.8 reduce-scatter.22
where the time goes:
time: 409 us; the launch traced here: 408 us
  waiting for transfers between devices  174 us (43%)
  blocking collectives  154 us (38%)
  matrix products  34.2 us (8%)
  local copies, waits for them, and re-layouts  14.6 us (4%)
  between operations  14.4 us (4%)
  other arithmetic  8.99 us (2%)
  starting transfers between devices  8.56 us (2%)
    reduce_scatter x4, waiting for transfers between devices, local(): lax.psum_scatter((near_term + advanced).astype(jnp.bfloat16), 'chan', sca...  74.6 us
    all_gather x4, blocking collectives, local(): grad_whole = lax.all_gather(grad_now, 'chan', axis=1, tiled=True)  60.7 us
    all_gather x4, blocking collectives, local(): whole_rows = lax.all_gather(signal, 'chan', axis=1, tiled=True)  60.6 us
    reduce_scatter x4, waiting for transfers between devices, local(): lax.psum_scatter(mix_term.astype(jnp.bfloat16), 'chan', scatter_dimension...  50.4 us
    all_gather x4, waiting for transfers between devices, local(): lax.all_gather(gate_weight[layer_index], 'tm', axis=1, tiled=True)  34.9 us
    all_gather x4, blocking collectives, local(): lax.all_gather(mix_weight[layer_index], 'tm', axis=1, tiled=True)  32.3 us
    unnamed x82, local copies, waits for them, and re-layouts  10.5 us
    ppermute x4, waiting for transfers between devices, shifted(): return lax.ppermute(shard, axis, pairs)  10 us
  transfers between devices with their start and end apart: 20, of which 12 were waited for; matrix products, arithmetic and copies ran while one was open for 8% of the time, Pallas kernels for 0%

commit v1 on v0

v1 whole, which is shorter than its diff:
```python
import functools

import jax
import jax.numpy as jnp
from jax import lax
from jax.experimental import pallas as pl
from jax.experimental.pallas import tpu as pltpu
from jax.sharding import PartitionSpec as P

BOTH = ("tm", "chan")


def dot(left, right):
    return jnp.dot(left, right, preferred_element_type=jnp.float32)


def dot_t(left, right):
    return lax.dot_general(
        left, right, (((1,), (1,)), ((), ())), preferred_element_type=jnp.float32
    )


class Blocks:
    def __init__(self, refs, kblocks, jblocks, taps, kb, half):
        self.refs, self.jblocks, self.taps, self.kb, self.half = refs, jblocks, taps, kb, half
        self.kblocks = kblocks

    def tap(self, which, i, j):
        return self.refs[0][i * self.jblocks + j, pl.ds(which * self.kb, self.kb), :]

    def mix(self, i, j):
        if len(self.refs) == 1:
            return self.refs[0][i * self.jblocks + j, pl.ds(self.taps * self.kb, self.half), :]
        return self.refs[1][i * self.jblocks + j]


def down(values, rows):
    return jnp.concatenate([jnp.zeros_like(values[:rows]), values[: values.shape[0] - rows]], axis=0)


def up(values, rows):
    return jnp.concatenate([values[rows:], jnp.zeros_like(values[:rows])], axis=0)


def total(parts):
    if len(parts) == 1:
        return parts[0][...]
    base, own, other = (part[...].astype(jnp.float32) for part in parts)
    return (base + (own + other)).astype(jnp.bfloat16)


def forward_part(blocks, x_ref, shift, fac_f, fac_g, part_ref, acc_ref):
    kb, half = blocks.kb, blocks.half
    current = blocks.taps - 1
    for j in range(blocks.jblocks):
        near = far = None
        for i in range(blocks.kblocks):
            x = x_ref[:, pl.ds(i * kb, kb)]
            term = dot(x, blocks.tap(current, i, j))
            near = term if near is None else near + term
            if blocks.taps == 2:
                term = dot(x, blocks.tap(0, i, j))
                far = term if far is None else far + term
        pre = near if far is None else near + down(far, shift)
        tanh_value = jnp.tanh(pre[:, :half])
        sig_value = jax.nn.sigmoid(pre[:, half:])
        gated = (tanh_value * sig_value).astype(jnp.bfloat16)
        fac_f[j] = sig_value * (1.0 - tanh_value * tanh_value)
        fac_g[j] = tanh_value * sig_value * (1.0 - sig_value)
        for i in range(blocks.kblocks):
            term = dot(gated, blocks.mix(i, j))
            cols = pl.ds(i * kb, kb)
            if j == 0:
                acc_ref[:, cols] = term
            else:
                acc_ref[:, cols] += term
    part_ref[...] = acc_ref[...].astype(jnp.bfloat16)


def backward_part(blocks, g_ref, shift, fac_f, fac_g, part_ref, acc_ref):
    kb = blocks.kb
    current = blocks.taps - 1
    for j in range(blocks.jblocks):
        grad_z = None
        for i in range(blocks.kblocks):
            term = dot_t(g_ref[:, pl.ds(i * kb, kb)], blocks.mix(i, j))
            grad_z = term if grad_z is None else grad_z + term
        both = jnp.concatenate([grad_z * fac_f[j], grad_z * fac_g[j]], axis=1).astype(jnp.bfloat16)
        for i in range(blocks.kblocks):
            term = dot_t(both, blocks.tap(current, i, j))
            if blocks.taps == 2:
                term = term + up(dot_t(both, blocks.tap(0, i, j)), shift)
            cols = pl.ds(i * kb, kb)
            if j == 0:
                acc_ref[:, cols] = term
            else:
                acc_ref[:, cols] += term
    part_ref[...] = acc_ref[...].astype(jnp.bfloat16)


def layer_cost(rows, weights, passes):
    return pl.CostEstimate(
        flops=2 * rows * weights * passes, bytes_accessed=2 * weights, transcendentals=rows * 1024
    )


def call(body, ins, outs, scratch, rows, weights, passes, name):
    vmem = pl.BlockSpec(memory_space=pltpu.VMEM)
    return pl.pallas_call(
        body,
        out_shape=outs,
        in_specs=[vmem] * len(ins),
        out_specs=[vmem] * len(outs),
        scratch_shapes=scratch,
        compiler_params=pltpu.CompilerParams(vmem_limit_bytes=24 * 1024 * 1024),
        cost_estimate=layer_cost(rows, weights, passes),
        name=name,
    )(*ins)


def local(records, cotangent, filter_weight, gate_weight, mix_weight):
    layers = filter_weight.shape[0]
    rows, nb = records.shape
    kb = filter_weight.shape[2]
    tm_count, chan_count = lax.axis_size("tm"), lax.axis_size("chan")
    group = lax.axis_index("groups")
    peers = tm_count * chan_count
    width = nb * chan_count
    half = nb // 2
    bf16, f32 = jnp.bfloat16, jnp.float32

    take = -(-rows // (4 * peers)) * 4
    padded = take * peers

    gathered = []
    for layer in range(layers):
        taps = 2 if 2**layer < tm_count else 1
        halves = [
            lax.dynamic_slice_in_dim(weight[layer, 2 - taps :], group * half, half, 2)
            for weight in (filter_weight, gate_weight)
        ]
        pack = jnp.concatenate(halves, axis=2).reshape(taps * kb, nb)
        mix = lax.dynamic_slice_in_dim(mix_weight[layer], group * half, half, 0)
        packs = [jnp.concatenate([pack, mix], axis=0)] if kb == nb else [pack, mix]
        gathered.append((taps, [lax.all_gather(p, BOTH, axis=0, tiled=False) for p in packs]))

    def swap(values):
        return lax.ppermute(values, "groups", [(0, 1), (1, 0)])

    both = jnp.pad(jnp.stack([records, cotangent]), ((0, 0), (0, padded - rows), (0, 0)))
    sent = both.reshape(2, peers, take, nb).transpose(1, 0, 2, 3)
    got = lax.all_to_all(sent, BOTH, split_axis=0, concat_axis=0, tiled=True)
    got = got.reshape(tm_count, chan_count, 2, take, nb).transpose(2, 0, 3, 1, 4)
    own = got.reshape(2, tm_count, take, width)
    other = swap(own)
    first, second = jnp.where(group == 0, own, other), jnp.where(group == 0, other, own)
    pair = jnp.concatenate([first, second], axis=2)
    m = tm_count * 2 * take
    signal, grad = pair.reshape(2, m, width)

    act = jax.ShapeDtypeStruct((m, width), bf16)
    fac = jax.ShapeDtypeStruct((chan_count, m, half), f32)
    scratch = [pltpu.VMEM((m, width), f32)]

    def shift_of(layer):
        return 2**layer * 2 * take

    def make_blocks(refs, taps):
        return Blocks(refs, tm_count, chan_count, taps, kb, half)

    factors = []
    parts = [signal]
    for layer in range(layers - 1):
        taps, weights = gathered[layer]

        def body(*refs, taps=taps, shift=shift_of(layer), nparts=len(parts), nw=len(weights)):
            ins, (sig, part, fac_f, fac_g, acc) = refs[: nparts + nw], refs[nparts + nw :]
            sig[...] = total(ins[:nparts])
            forward_part(make_blocks(ins[nparts:], taps), sig, shift, fac_f, fac_g, part, acc)

        elems = sum(w.size for w in weights)
        sig, part, fac_f, fac_g = call(
            body, [*parts, *weights], [act, act, fac, fac], scratch, m, elems, 1, "layer_forward"
        )
        factors.append((fac_f, fac_g))
        parts = [sig, part, swap(part)]

    taps, weights = gathered[-1]

    def last_body(*refs, taps=taps, shift=shift_of(layers - 1), nparts=len(parts), nw=len(weights)):
        ins = refs[: nparts + nw + 1]
        sig, part, gpart, fac_f, fac_g, acc = refs[nparts + nw + 1 :]
        blocks = make_blocks(ins[nparts : nparts + nw], taps)
        sig[...] = total(ins[:nparts])
        forward_part(blocks, sig, shift, fac_f, fac_g, part, acc)
        backward_part(blocks, ins[-1], shift, fac_f, fac_g, gpart, acc)

    elems = sum(w.size for w in weights)
    last_scratch = [pltpu.VMEM((chan_count, m, half), f32)] * 2 + scratch
    sig, part, gpart = call(
        last_body, [*parts, *weights, grad], [act, act, act], last_scratch, m, elems, 2, "layer_last"
    )

    def of_group(values, which):
        values = values.reshape(tm_count, 2, take, width)
        return lax.dynamic_index_in_dim(values, which, 1, keepdims=False)

    def summed(base, partial):
        arrived = swap(of_group(partial, 1 - group))
        mine = of_group(partial, group).astype(f32) + arrived.astype(f32)
        return (of_group(base, group).astype(f32) + mine).astype(bf16)

    output = summed(sig, part)
    parts = [grad, gpart, swap(gpart)]
    for layer in reversed(range(layers - 1)):
        taps, weights = gathered[layer]
        fac_f, fac_g = factors[layer]

        def body(*refs, taps=taps, shift=shift_of(layer), nw=len(weights)):
            ins, (now, part, acc) = refs[: 5 + nw], refs[5 + nw :]
            now[...] = total(ins[:3])
            backward_part(make_blocks(ins[5:], taps), now, shift, ins[3], ins[4], part, acc)

        elems = sum(w.size for w in weights)
        now, part = call(
            body, [*parts, fac_f, fac_g, *weights], [act, act], scratch, m, elems, 1, "layer_backward"
        )
        if layer:
            parts = [now, part, swap(part)]
    input_grad = summed(now, part)

    back = jnp.stack([output, input_grad]).reshape(2, tm_count, take, chan_count, nb)
    back = back.transpose(1, 3, 0, 2, 4).reshape(peers, 2, take, nb)
    back = lax.all_to_all(back, BOTH, split_axis=0, concat_axis=0, tiled=True)
    back = back.transpose(1, 0, 2, 3).reshape(2, padded, nb)[:, :rows]
    return back[0], back[1]


def solution(mesh):
    return jax.shard_map(
        local,
        mesh=mesh,
        in_specs=(
            P(("groups", "tm"), "chan"),
            P(("groups", "tm"), "chan"),
            P(None, None, "tm", "chan"),
            P(None, None, "tm", "chan"),
            P(None, "chan", "tm"),
        ),
        out_specs=(P(("groups", "tm"), "chan"), P(("groups", "tm"), "chan")),
        check_vma=False,
    )
```

time: 409 us -> 282 us (0.69)
  blocking collectives: 154 us -> 32.4 us
  matrix products: 34.2 us -> 0 us
  Pallas kernels: 0 us -> 11.3 us
  waiting for transfers between devices: 174 us -> 185 us
  local copies, waits for them, and re-layouts: 14.6 us -> 21 us
  other arithmetic: 8.99 us -> 4.21 us
  starting transfers between devices: 8.56 us -> 13.1 us
    all_gather x12 -> x0, blocking collectives: 154 us -> none  [the longest x4 60.7 us: local(): grad_whole = lax.all_gather(grad_now, 'chan', axis=1, tiled=True)]
    all_gather x8 -> x4, waiting for transfers between devices: 34.9 us -> 162 us  [local(): lax.all_gather(p, BOTH, axis=0, tiled=False)]
    reduce_scatter x8 -> x0, waiting for transfers between devices: 125 us -> none  [the longest x4 74.6 us: local(): lax.psum_scatter((near_term + advanced).astype(jnp.bfloat16), 'chan', sca...]
    dot_general x36 -> x0, matrix products: 34.2 us -> none  [the longest x16 9.03 us: right_product(): lax.dot_general(left, panel, (((1,), (1,)), ((), ())), preferred_element_...]
    all_to_all x0 -> x2, blocking collectives: none -> 32.4 us  [the longest x1 20.9 us: local(): got = lax.all_to_all(sent, BOTH, split_axis=0, concat_axis=0, tiled=True)]
    ppermute x4 -> x9, waiting for transfers between devices: 10 us -> 23.6 us  [swap(): return lax.ppermute(values, 'groups', [(0, 1), (1, 0)])]
    pallas_call x0 -> x7, Pallas kernels: none -> 11.3 us  [call(): pl.pallas_call(body, out_shape=outs, in_specs=[vmem] * len(ins), out_spec...]
    convert_element_type x8 -> x2, other arithmetic: 8.99 us -> 0.11 us  [summed(): return (of_group(base, group).astype(f32) + mine).astype(bf16)]
  transfers between devices with their start and end apart: 20 -> 13, of which waited for: 12 -> 9; matrix products, arithmetic and copies ran while one was open for 8% -> 3% of each run, Pallas kernels for 0% -> 2%
where the time goes in v1:
time: 282 us; the launch traced here: 281 us
  waiting for transfers between devices  185 us (66%)
  blocking collectives  32.4 us (11%)
  local copies, waits for them, and re-layouts  21 us (7%)
  between operations  14.1 us (5%)
  starting transfers between devices  13.1 us (5%)
  Pallas kernels  11.3 us (4%)
  other arithmetic  4.21 us (1%)
    all_gather x4, waiting for transfers between devices, local(): lax.all_gather(p, BOTH, axis=0, tiled=False)  162 us
    ppermute x9, waiting for transfers between devices, swap(): return lax.ppermute(values, 'groups', [(0, 1), (1, 0)])  23.6 us
    all_to_all x1, blocking collectives, local(): got = lax.all_to_all(sent, BOTH, split_axis=0, concat_axis=0, tiled=True)  20.9 us
    ppermute x9, starting transfers between devices, swap(): return lax.ppermute(values, 'groups', [(0, 1), (1, 0)])  12.9 us
    all_to_all x1, blocking collectives, local(): back = lax.all_to_all(back, BOTH, split_axis=0, concat_axis=0, tiled=True)  11.5 us
    unnamed x20, local copies, waits for them, and re-layouts  11.4 us
    pallas_call x7, Pallas kernels, call(): pl.pallas_call(body, out_shape=outs, in_specs=[vmem] * len(ins), out_spec...  11.3 us
  transfers between devices with their start and end apart: 13, of which 9 were waited for; matrix products, arithmetic and copies ran while one was open for 3% of the time, Pallas kernels for 2%

profile of v1, /device:TPU:0, one launch (start us, length us, event | category | flops | bytes accessed | tf_op | source)
XLA Modules:
  0.0 281.4 jit_solution(9833524949658277495)
XLA Ops:
  7.2 1.1 fusion.7
  9.4 1.1 fusion.9
  16.4 20.9 %all_to_all.10 = bf16[16,2,12,256]{3,1,2,0:T(2,128)(2,1)S(1)} all-to-all(bf16[16,2,12,256]{3,1,2,0:T(2,128)(2,1)S(1)} %copy.19), channel_id=1, replica_groups=mesh['groups'=2,'tm'=4,'chan'=4] {'tm','chan'}, dimensions={0} | all-to-all | bytes 393216 | tf_op jit(solution)/shard_map/all_to_all | solution.py:152
  37.5 1.5 collective-permute-start
  39.0 5.4 %collective-permute-done = bf16[2,4,12,1024]{3,1,2,0:T(4,128)(2,1)S(1)} collective-permute-done((bf16[2,4,12,1024]{3,1,2,0:T(4,128)(2,1)S(1)}, bf16[2,4,12,1024]{3,1,2,0:T(4,128)(2,1)S(1)}, u32[]{:S(2)}, u32[]{:S(2)}) %collective-permute-start) | collective-permute-done | bytes 196640 | tf_op jit(solution)/shard_map/ppermute | solution.py:148
  45.5 28.6 %all-gather.9.cloned.1.call-done = bf16[10240,256]{1,0:T(8,128)(2,1)} async-done(((bf16[640,256]{1,0:T(8,128)(2,1)}), bf16[10240,256]{1,0:T(8,128)(2,1)}) %all-gather.9.cloned.1.call-update) | async-done | bytes 5242896 | tf_op jit(solution)/shard_map/all_gather | solution.py:145
  74.1 2.5 copy-done
  76.6 1.5 layer_forward.3
  78.0 1.6 collective-permute-start.1
  79.6 51.4 %all-gather.11.cloned.1.call-done = bf16[10240,256]{1,0:T(8,128)(2,1)} async-done(((bf16[640,256]{1,0:T(8,128)(2,1)}), bf16[10240,256]{1,0:T(8,128)(2,1)}) %all-gather.11.cloned.1.call-update) | async-done | bytes 5242896 | tf_op jit(solution)/shard_map/all_gather | solution.py:145
  131.0 2.5 copy-done.2
  133.5 1.2 layer_forward.4
  134.7 1.5 collective-permute-start.2
  136.2 40.9 %all-gather.13.cloned.1.call-done = bf16[6144,256]{1,0:T(8,128)(2,1)} async-done(((bf16[384,256]{1,0:T(8,128)(2,1)}), bf16[6144,256]{1,0:T(8,128)(2,1)}) %all-gather.13.cloned.1.call-update) | async-done | bytes 3145744 | tf_op jit(solution)/shard_map/all_gather | solution.py:145
  177.1 1.9 copy-done.3
  180.0 1.5 collective-permute-start.3
  182.5 40.8 %all-gather.15.cloned.1.call-done = bf16[6144,256]{1,0:T(8,128)(2,1)} async-done(((bf16[384,256]{1,0:T(8,128)(2,1)}), bf16[6144,256]{1,0:T(8,128)(2,1)}) %all-gather.15.cloned.1.call-update) | async-done | bytes 3145744 | tf_op jit(solution)/shard_map/all_gather | solution.py:145
  223.3 2.0 copy-done.5
  225.3 2.1 layer_last.1
  227.4 1.5 collective-permute-start.5
  229.0 5.6 %collective-permute-done.5.refs_2_ = bf16[96,1024]{1,0:T(8,128)(2,1)S(1)} collective-permute-done((bf16[96,1024]{1,0:T(8,128)(2,1)S(1)}, bf16[96,1024]{1,0:T(8,128)(2,1)S(1)}, u32[]{:S(2)}, u32[]{:S(2)}) %collective-permute-start.5) | collective-permute-done | bytes 196640 | tf_op jit(solution)/shard_map/ppermute | solution.py:148
  234.6 1.4 layer_backward.3
  235.9 1.5 collective-permute-start.6
  237.5 4.8 %collective-permute-done.6.refs_2_ = bf16[96,1024]{1,0:T(8,128)(2,1)S(1)} collective-permute-done((bf16[96,1024]{1,0:T(8,128)(2,1)S(1)}, bf16[96,1024]{1,0:T(8,128)(2,1)S(1)}, u32[]{:S(2)}, u32[]{:S(2)}) %collective-permute-start.6) | collective-permute-done | bytes 196640 | tf_op jit(solution)/shard_map/ppermute | solution.py:148
  242.3 2.2 layer_backward.4
  244.4 1.5 collective-permute-start.7
  246.7 4.5 %collective-permute-done.7.refs_2_ = bf16[96,1024]{1,0:T(8,128)(2,1)S(1)} collective-permute-done((bf16[96,1024]{1,0:T(8,128)(2,1)S(1)}, bf16[96,1024]{1,0:T(8,128)(2,1)S(1)}, u32[]{:S(2)}, u32[]{:S(2)}) %collective-permute-start.7) | collective-permute-done | bytes 196640 | tf_op jit(solution)/shard_map/ppermute | solution.py:148
  251.2 2.5 copy-done.1
  253.7 2.0 layer_backward.5
  255.8 1.6 collective-permute-start.8
  257.5 3.3 %collective-permute-done.8 = bf16[4,12,1024]{2,1,0:T(8,128)(2,1)S(1)} collective-permute-done((bf16[4,12,1024]{2,1,0:T(8,128)(2,1)S(1)}, bf16[4,12,1024]{2,1,0:T(8,128)(2,1)S(1)}, u32[]{:S(2)}, u32[]{:S(2)}) %collective-permute-start.8) | collective-permute-done | bytes 98336 | tf_op jit(solution)/shard_map/ppermute | solution.py:148
  261.3 11.5 %all_to_all.11 = bf16[16,2,12,256]{3,1,2,0:T(2,128)(2,1)S(1)} all-to-all(bf16[16,2,12,256]{3,1,2,0:T(2,128)(2,1)S(1)} %bitcast.82), channel_id=1, replica_groups=mesh['groups'=2,'tm'=4,'chan'=4] {'tm','chan'}, dimensions={0} | all-to-all | bytes 393216 | tf_op jit(solution)/shard_map/all_to_all | solution.py:234
  (72 shorter events, 13.5 us)
Async XLA Ops:
  7.2 8.9 %copy-start.6 = (bf16[192,256]{1,0:T(8,128)(2,1)S(1)}, bf16[192,256]{1,0:T(8,128)(2,1)}, u32[]{:S(2)}) copy-start(bf16[192,256]{1,0:T(8,128)(2,1)} %param.5) | copy-start | bytes 294916
  7.2 8.9 %copy-start.7 = (bf16[192,256]{1,0:T(8,128)(2,1)S(1)}, bf16[192,256]{1,0:T(8,128)(2,1)}, u32[]{:S(2)}) copy-start(bf16[192,256]{1,0:T(8,128)(2,1)} %param.6) | copy-start | bytes 294916
  7.2 66.9 %all-gather.9.cloned.1.call-start = ((), (), s32[]{:S(2)}) async-start(), calls=%async_computation.2 | async-start | bytes 5570560 | tf_op jit(solution)/shard_map/all_gather | solution.py:145
  11.4 119.5 %all-gather.11.cloned.1.call-start = ((), (), s32[]{:S(2)}) async-start(), calls=%async_computation.3 | async-start | bytes 5570560 | tf_op jit(solution)/shard_map/all_gather | solution.py:145
  12.3 164.7 %all-gather.13.cloned.1.call-start = ((), (), s32[]{:S(2)}) async-start(), calls=%async_computation.4 | async-start | bytes 3342336 | tf_op jit(solution)/shard_map/all_gather | solution.py:145
  15.2 208.1 %all-gather.15.cloned.1.call-start = ((), (), s32[]{:S(2)}) async-start(), calls=%async_computation.5 | async-start | bytes 3342336 | tf_op jit(solution)/shard_map/all_gather | solution.py:145
  37.5 7.0 %collective-permute-start = (bf16[2,4,12,1024]{3,1,2,0:T(4,128)(2,1)S(1)}, bf16[2,4,12,1024]{3,1,2,0:T(4,128)(2,1)S(1)}, u32[]{:S(2)}, u32[]{:S(2)}) collective-permute-start(bf16[2,4,12,1024]{3,1,2,0:T(4,128)(2,1)S(1)} %reshape.84), channel_id=1, source_target_pairs={{0,16},{16,0},{1,17},{17,1},{2,18},{18,2},{3,19},{19,3},{4,20},{20... | collective-permute-start | bytes 589832 | tf_op jit(solution)/shard_map/ppermute | solution.py:148
  74.1 2.5 copy-start
  78.0 52.9 %collective-permute-start.1 = (bf16[96,1024]{1,0:T(8,128)(2,1)S(1)}, bf16[96,1024]{1,0:T(8,128)(2,1)S(1)}, u32[]{:S(2)}, u32[]{:S(2)}) collective-permute-start(bf16[96,1024]{1,0:T(8,128)(2,1)S(1)} %get-tuple-element.24.refs_1_), channel_id=1, source_target_pairs={{0,16},{16,0},{1,17},{17,1},{2,18},{18,2},{3,19},{19,3},{4,20},{20... | collective-permute-start | bytes 589832 | tf_op jit(solution)/shard_map/ppermute | solution.py:148
  131.0 2.5 copy-start.2
  134.7 42.4 %collective-permute-start.2 = (bf16[96,1024]{1,0:T(8,128)(2,1)S(1)}, bf16[96,1024]{1,0:T(8,128)(2,1)S(1)}, u32[]{:S(2)}, u32[]{:S(2)}) collective-permute-start(bf16[96,1024]{1,0:T(8,128)(2,1)S(1)} %get-tuple-element.26.refs_1_), channel_id=1, source_target_pairs={{0,16},{16,0},{1,17},{17,1},{2,18},{18,2},{3,19},{19,3},{4,20},{20... | collective-permute-start | bytes 589832 | tf_op jit(solution)/shard_map/ppermute | solution.py:148
  177.1 1.9 copy-start.3
  179.0 63.3 %slice-start = ((s8[5242880]{0:T(1024)(128)(4,1)}), s8[1048576]{0:T(1024)(128)(4,1)S(1)}, s32[]{:S(2)}) async-start(s8[5242880]{0:T(1024)(128)(4,1)} %bitcast.70), calls=%async_computation.6 | async-start | bytes 2097152
  180.0 43.3 %collective-permute-start.3 = (bf16[96,1024]{1,0:T(8,128)(2,1)S(1)}, bf16[96,1024]{1,0:T(8,128)(2,1)S(1)}, u32[]{:S(2)}, u32[]{:S(2)}) collective-permute-start(bf16[96,1024]{1,0:T(8,128)(2,1)S(1)} %get-tuple-element.28.refs_1_), channel_id=1, source_target_pairs={{0,16},{16,0},{1,17},{17,1},{2,18},{18,2},{3,19},{19,3},{4,20},{20... | collective-permute-start | bytes 589832 | tf_op jit(solution)/shard_map/ppermute | solution.py:148
  223.2 11.3 %copy-start.4 = (bf16[6144,256]{1,0:T(8,128)(2,1)S(1)}, bf16[6144,256]{1,0:T(8,128)(2,1)}, u32[]{:S(2)}) copy-start(bf16[6144,256]{1,0:T(8,128)(2,1)} %all-gather.13.cloned.1.call-done) | copy-start | bytes 9437188
  223.3 2.0 copy-start.5
  225.3 17.0 %slice-start.1 = ((s8[5242880]{0:T(1024)(128)(4,1)}), s8[4194304]{0:T(1024)(128)(4,1)S(1)}, s32[]{:S(2)}) async-start(s8[5242880]{0:T(1024)(128)(4,1)} %bitcast.70), calls=%async_computation.7 | async-start | bytes 8388608
  227.4 7.1 %collective-permute-start.5 = (bf16[96,1024]{1,0:T(8,128)(2,1)S(1)}, bf16[96,1024]{1,0:T(8,128)(2,1)S(1)}, u32[]{:S(2)}, u32[]{:S(2)}) collective-permute-start(bf16[96,1024]{1,0:T(8,128)(2,1)S(1)} %get-tuple-element.31.refs_1_), channel_id=1, source_target_pairs={{0,16},{16,0},{1,17},{17,1},{2,18},{18,2},{3,19},{19,3},{4,20},{20... | collective-permute-start | bytes 589832 | tf_op jit(solution)/shard_map/ppermute | solution.py:148
  235.9 6.3 %collective-permute-start.6 = (bf16[96,1024]{1,0:T(8,128)(2,1)S(1)}, bf16[96,1024]{1,0:T(8,128)(2,1)S(1)}, u32[]{:S(2)}, u32[]{:S(2)}) collective-permute-start(bf16[96,1024]{1,0:T(8,128)(2,1)S(1)} %get-tuple-element.35.refs_1_), channel_id=1, source_target_pairs={{0,16},{16,0},{1,17},{17,1},{2,18},{18,2},{3,19},{19,3},{4,20},{20... | collective-permute-start | bytes 589832 | tf_op jit(solution)/shard_map/ppermute | solution.py:148
  244.4 6.8 %collective-permute-start.7 = (bf16[96,1024]{1,0:T(8,128)(2,1)S(1)}, bf16[96,1024]{1,0:T(8,128)(2,1)S(1)}, u32[]{:S(2)}, u32[]{:S(2)}) collective-permute-start(bf16[96,1024]{1,0:T(8,128)(2,1)S(1)} %get-tuple-element.39.refs_1_), channel_id=1, source_target_pairs={{0,16},{16,0},{1,17},{17,1},{2,18},{18,2},{3,19},{19,3},{4,20},{20... | collective-permute-start | bytes 589832 | tf_op jit(solution)/shard_map/ppermute | solution.py:148
  246.0 11.3 %collective-permute-start.4 = (bf16[4,12,1024]{2,1,0:T(8,128)(2,1)S(1)}, bf16[4,12,1024]{2,1,0:T(8,128)(2,1)S(1)}, u32[]{:S(2)}, u32[]{:S(2)}) collective-permute-start(bf16[4,12,1024]{2,1,0:T(8,128)(2,1)S(1)} %dynamic-slice_bitcast_fusion.1), channel_id=1, source_target_pairs={{0,16},{16,0},{1,17},{17,1},{2,18},{18,2},{3,19},{19,3},{4,20},{20... | collective-permute-start | bytes 294920 | tf_op jit(solution)/shard_map/ppermute | solution.py:148
  251.2 2.5 copy-start.1
  255.8 5.0 %collective-permute-start.8 = (bf16[4,12,1024]{2,1,0:T(8,128)(2,1)S(1)}, bf16[4,12,1024]{2,1,0:T(8,128)(2,1)S(1)}, u32[]{:S(2)}, u32[]{:S(2)}) collective-permute-start(bf16[4,12,1024]{2,1,0:T(8,128)(2,1)S(1)} %dynamic-slice_bitcast_fusion), channel_id=1, source_target_pairs={{0,16},{16,0},{1,17},{17,1},{2,18},{18,2},{3,19},{19,3},{4,20},{20... | collective-permute-start | bytes 294920 | tf_op jit(solution)/shard_map/ppermute | solution.py:148
Sparse Core Ops, SparseCore 0:
  11.5 62.4 all-gather.8
  76.4 54.5 all-gather.10
  133.3 43.7 all-gather.12
  179.2 43.9 all-gather.14

commit v2 on v1

v2 whole, which is shorter than its diff:
```python
import jax
import jax.numpy as jnp
from jax import lax
from jax.experimental import pallas as pl
from jax.experimental.pallas import tpu as pltpu
from jax.sharding import PartitionSpec as P

BOTH = ("tm", "chan")
STAGES = ((0, 1), (2, 3))


def dot(left, right):
    return jnp.dot(left, right, preferred_element_type=jnp.float32)


def dot_t(left, right):
    return lax.dot_general(
        left, right, (((1,), (1,)), ((), ())), preferred_element_type=jnp.float32
    )


def exchange(values, axis, bit):
    return lax.ppermute(values, axis, [(i, i ^ bit) for i in range(lax.axis_size(axis))])


def bits_of(axis, least):
    return [1 << b for b in range(10) if least <= 1 << b < lax.axis_size(axis)]


class Piece:
    def __init__(self, array, keys, kind):
        self.array, self.keys, self.kind = array, keys, kind

    def moved(self, axis, bit):
        place = 0 if axis == "chan" else 1
        keys = [tuple(o ^ (bit if n == place else 0) for n, o in enumerate(k)) for k in self.keys]
        return Piece(exchange(self.array, axis, bit), keys, self.kind)


def merged(pieces, limit):
    if len(pieces) <= limit:
        return pieces
    joined = []
    for kind in ("full", "mine", "other"):
        same = [p for p in pieces if p.kind == kind]
        if same:
            array = jnp.concatenate([p.array for p in same], axis=0)
            joined.append(Piece(array, sum((p.keys for p in same), []), kind))
    return joined


def spread(own, group):
    limit = 16
    rows = own.shape[1]
    half = lax.dynamic_slice_in_dim(own, group * (rows // 2), rows // 2, 1)
    full = [Piece(own[None], [(0, 0)], "full")]
    mine = [Piece(half[None], [(0, 0)], "mine")]
    for bit in bits_of("chan", 2):
        mine = merged(mine + [p.moved("chan", bit) for p in mine], limit // 4)
    mine_parts = []
    for p in mine:
        if (0, 0) in p.keys:
            at = [n for n, k in enumerate(p.keys) if k != (0, 0)]
            if at:
                array = jnp.stack([p.array[n] for n in at])
                mine_parts.append(Piece(array, [p.keys[n] for n in at], "mine"))
        else:
            mine_parts.append(p)
    mine = mine_parts
    for bit in bits_of("tm", 2):
        full = merged(full + [p.moved("tm", bit) for p in full], limit // 4)
        mine = merged(mine + [p.moved("tm", bit) for p in mine], limit // 4)
    other = [
        Piece(exchange(p.array, "groups", 1), p.keys, "other") for p in mine
    ]
    pieces = full + mine + other
    if lax.axis_size("tm") > 1:
        pieces = pieces + [p.moved("tm", 1) for p in pieces]
    return merged(pieces, limit)


class Blocks:
    def __init__(self, refs, pieces, at, scratch, sems, panels, taps, kb, square):
        self.scratch, self.panels, self.taps, self.kb = scratch, panels, taps, kb
        self.square = square
        self.nb = scratch.shape[2]
        self.kblocks = scratch.shape[0] // panels
        self.copies = [[] for _ in range(panels)]
        group = lax.axis_index("groups")
        rows = scratch.shape[1]
        number = 0
        for ref, (keys, kind) in zip(refs, pieces):
            for lead, (dz, dtm) in enumerate(keys):
                target = scratch.at[dz // 2 * self.kblocks + dtm]
                if kind != "full":
                    which = group if kind == "mine" else 1 - group
                    start = pl.multiple_of(which * (rows // 2), rows // 2)
                    target = target.at[pl.ds(start, rows // 2)]
                copy = pltpu.make_async_copy(ref.at[lead, at], target, sems.at[number])
                self.copies[dz // 2].append(copy)
                number += 1

    def start(self):
        for copies in self.copies:
            for copy in copies:
                copy.start()

    def wait(self, panel):
        for copy in self.copies[panel]:
            copy.wait()

    def mat(self, which, panel, i):
        return self.scratch[panel * self.kblocks + i, pl.ds(which * self.kb, self.kb), :]

    def filt(self, tap, panel, i):
        return self.mat(tap, panel, i)

    def gate(self, tap, panel, i):
        return self.mat(self.taps + tap, panel, i)

    def mixed(self, gated, panel, i):
        mix = self.mat(2 * self.taps, panel, i)
        return dot(gated, mix) if self.square else dot_t(gated, mix)

    def unmixed(self, grad, panel, i):
        mix = self.mat(2 * self.taps, panel, i)
        return dot_t(grad, mix) if self.square else dot(grad, mix)


def down(values, rows):
    return jnp.concatenate([jnp.zeros_like(values[:rows]), values[: values.shape[0] - rows]], axis=0)


def up(values, rows):
    return jnp.concatenate([values[rows:], jnp.zeros_like(values[:rows])], axis=0)


def total(parts):
    if len(parts) == 1:
        return parts[0][...]
    base, own, other = (part[...].astype(jnp.float32) for part in parts)
    return (base + (own + other)).astype(jnp.bfloat16)


def add_to(acc_ref, cols, term, first):
    if first:
        acc_ref[:, cols] = term
    else:
        acc_ref[:, cols] += term


def forward_part(blocks, x_ref, shift, fac_f, fac_g, part_ref, acc_ref, waits=True):
    kb, taps = blocks.kb, blocks.taps
    for panel in range(blocks.panels):
        if waits:
            blocks.wait(panel)
        sums = []
        for kernel in (blocks.filt, blocks.gate):
            pre = None
            for tap in range(taps):
                value = None
                for i in range(blocks.kblocks):
                    term = dot(x_ref[:, pl.ds(i * kb, kb)], kernel(tap, panel, i))
                    value = term if value is None else value + term
                if tap < taps - 1:
                    value = down(value, shift)
                pre = value if pre is None else pre + value
            sums.append(pre)
        tanh_value = jnp.tanh(sums[0])
        sig_value = jax.nn.sigmoid(sums[1])
        gated = (tanh_value * sig_value).astype(jnp.bfloat16)
        fac_f[panel] = sig_value * (1.0 - tanh_value * tanh_value)
        fac_g[panel] = tanh_value * sig_value * (1.0 - sig_value)
        for i in range(blocks.kblocks):
            add_to(acc_ref, pl.ds(i * kb, kb), blocks.mixed(gated, panel, i), panel == 0)
    part_ref[...] = acc_ref[...].astype(jnp.bfloat16)


def backward_part(blocks, g_ref, shift, fac_f, fac_g, part_ref, acc_ref, waits=True):
    kb, taps = blocks.kb, blocks.taps
    for panel in range(blocks.panels):
        if waits:
            blocks.wait(panel)
        grad_z = None
        for i in range(blocks.kblocks):
            term = blocks.unmixed(g_ref[:, pl.ds(i * kb, kb)], panel, i)
            grad_z = term if grad_z is None else grad_z + term
        grad_f = (grad_z * fac_f[panel]).astype(jnp.bfloat16)
        grad_g = (grad_z * fac_g[panel]).astype(jnp.bfloat16)
        for i in range(blocks.kblocks):
            near = None
            for tap in range(taps):
                term = dot_t(grad_f, blocks.filt(tap, panel, i))
                term = term + dot_t(grad_g, blocks.gate(tap, panel, i))
                if tap < taps - 1:
                    term = up(term, shift)
                near = term if near is None else near + term
            add_to(acc_ref, pl.ds(i * kb, kb), near, panel == 0)
    part_ref[...] = acc_ref[...].astype(jnp.bfloat16)


def flipped(values, index, count, block):
    shape = values.shape
    for bit in [1 << b for b in range(10) if 1 << b < count]:
        split = values.reshape(*shape[:-1], count // (2 * bit), 2, bit * block)
        values = jnp.where((index & bit) != 0, split[..., ::-1, :], split).reshape(shape)
    return values


def local(records, cotangent, filter_weight, gate_weight, mix_weight):
    layers = filter_weight.shape[0]
    rows, nb = records.shape
    kb = filter_weight.shape[2]
    tm_count, chan_count = lax.axis_size("tm"), lax.axis_size("chan")
    group, tm_index = lax.axis_index("groups"), lax.axis_index("tm")
    side = lax.axis_index("chan") % 2
    peers = tm_count * chan_count
    panels = chan_count // 2
    width = nb * chan_count
    bf16, f32 = jnp.bfloat16, jnp.float32
    square = kb == nb

    take = -(-rows // (4 * peers)) * 4
    padded = take * peers

    taps_of = [2 if 2**layer < tm_count else 1 for layer in range(layers)]
    weights_of = {}
    for stage in STAGES:
        packs = []
        for layer in stage:
            taps = taps_of[layer]
            mix = mix_weight[layer] if square else mix_weight[layer].T
            mats = [filter_weight[layer, t] for t in range(2 - taps, 2)]
            mats += [gate_weight[layer, t] for t in range(2 - taps, 2)]
            packs.append(jnp.concatenate(mats + [mix], axis=0))
        if len({p.shape[0] for p in packs}) > 1:
            for layer, pack in zip(stage, packs):
                weights_of[layer] = (spread(pack[None], group), 0)
        else:
            pieces = spread(jnp.stack(packs), group)
            for at, layer in enumerate(stage):
                weights_of[layer] = (pieces, at)

    def swap(values):
        return exchange(values, "chan", 1)

    both = jnp.pad(jnp.stack([records, cotangent]), ((0, 0), (0, padded - rows), (0, 0)))
    sent = both.reshape(2, peers, take, nb).transpose(1, 0, 2, 3)
    got = lax.all_to_all(sent, BOTH, split_axis=0, concat_axis=0, tiled=True)
    got = got.reshape(tm_count, chan_count, 2, take, nb).transpose(2, 0, 3, 1, 4)
    own = flipped(got.reshape(2, tm_count, take, width), tm_index, tm_count, kb)
    other = swap(own)
    first, second = jnp.where(side == 0, own, other), jnp.where(side == 0, other, own)
    pair = jnp.concatenate([first, second], axis=2)
    m = tm_count * 2 * take
    signal, grad = pair.reshape(2, m, width)

    vmem = pl.BlockSpec(memory_space=pltpu.VMEM)
    anywhere = pl.BlockSpec(memory_space=pl.ANY)
    act = jax.ShapeDtypeStruct((m, width), bf16)
    fac = jax.ShapeDtypeStruct((panels, m, nb), f32)

    def layer_call(layer, body, arrays, outs, scratch, passes, name):
        pieces, at = weights_of[layer]
        taps = taps_of[layer]
        shift = 2**layer * 2 * take
        height = pieces[0].array.shape[2]
        copies = sum(len(p.keys) for p in pieces)
        plan = [(p.keys, p.kind) for p in pieces]
        elems = panels * tm_count * height * nb

        def kernel(*refs):
            ins, refs = refs[: len(arrays)], refs[len(arrays) :]
            piece_refs, refs = refs[: len(pieces)], refs[len(pieces) :]
            held, sems = refs[-2:]
            blocks = Blocks(piece_refs, plan, at, held, sems, panels, taps, kb, square)
            blocks.start()
            body(blocks, shift, ins, refs[: len(outs)], refs[len(outs) : -2])

        return pl.pallas_call(
            kernel,
            out_shape=outs,
            in_specs=[vmem] * len(arrays) + [anywhere] * len(pieces),
            out_specs=[vmem] * len(outs),
            scratch_shapes=[
                *scratch,
                pltpu.VMEM((panels * tm_count, height, nb), bf16),
                pltpu.SemaphoreType.DMA((copies,)),
            ],
            compiler_params=pltpu.CompilerParams(vmem_limit_bytes=32 * 1024 * 1024),
            cost_estimate=pl.CostEstimate(
                flops=2 * m * elems * passes, bytes_accessed=2 * elems, transcendentals=2 * m * nb
            ),
            name=name,
        )(*arrays, *[p.array for p in pieces])

    acc = [pltpu.VMEM((m, width), f32)]

    def forward_body(blocks, shift, ins, outs, scratch):
        sig, part, fac_f, fac_g = outs
        sig[...] = total(ins)
        forward_part(blocks, sig, shift, fac_f, fac_g, part, scratch[0])

    def last_body(blocks, shift, ins, outs, scratch):
        sig, part, gpart = outs
        fac_f, fac_g, acc_ref = scratch
        sig[...] = total(ins[:-1])
        forward_part(blocks, sig, shift, fac_f, fac_g, part, acc_ref)
        backward_part(blocks, ins[-1], shift, fac_f, fac_g, gpart, acc_ref, waits=False)

    def backward_body(blocks, shift, ins, outs, scratch):
        now, part = outs
        now[...] = total(ins[:3])
        backward_part(blocks, now, shift, ins[3], ins[4], part, scratch[0])

    factors = []
    parts = [signal]
    for layer in range(layers - 1):
        sig, part, fac_f, fac_g = layer_call(
            layer, forward_body, parts, [act, act, fac, fac], acc, 1, "layer_forward"
        )
        factors.append((fac_f, fac_g))
        parts = [sig, part, swap(part)]
    facs = [pltpu.VMEM((panels, m, nb), f32)] * 2
    sig, part, gpart = layer_call(
        layers - 1, last_body, [*parts, grad], [act, act, act], facs + acc, 2, "layer_last"
    )

    def of_side(values, which):
        values = values.reshape(tm_count, 2, take, width)
        return lax.dynamic_index_in_dim(values, which, 1, keepdims=False)

    def summed(base, partial):
        arrived = swap(of_side(partial, 1 - side))
        mine = of_side(partial, side).astype(f32) + arrived.astype(f32)
        return (of_side(base, side).astype(f32) + mine).astype(bf16)

    output = summed(sig, part)
    parts = [grad, gpart, swap(gpart)]
    for layer in reversed(range(layers - 1)):
        now, part = layer_call(
            layer, backward_body, [*parts, *factors[layer]], [act, act], acc, 1, "layer_backward"
        )
        if layer:
            parts = [now, part, swap(part)]
    input_grad = summed(now, part)

    back = flipped(jnp.stack([output, input_grad]), tm_index, tm_count, kb)
    back = back.reshape(2, tm_count, take, chan_count, nb)
    back = back.transpose(1, 3, 0, 2, 4).reshape(peers, 2, take, nb)
    back = lax.all_to_all(back, BOTH, split_axis=0, concat_axis=0, tiled=True)
    back = back.transpose(1, 0, 2, 3).reshape(2, padded, nb)[:, :rows]
    return back[0], back[1]


def solution(mesh):
    return jax.shard_map(
        local,
        mesh=mesh,
        in_specs=(
            P(("groups", "tm"), "chan"),
            P(("groups", "tm"), "chan"),
            P(None, None, "tm", "chan"),
            P(None, None, "tm", "chan"),
            P(None, "chan", "tm"),
        ),
        out_specs=(P(("groups", "tm"), "chan"), P(("groups", "tm"), "chan")),
        check_vma=False,
    )
```

time: 282 us -> 223 us (0.79)
  waiting for transfers between devices: 185 us -> 102 us
  blocking collectives: 32.4 us -> 10.9 us
  starting transfers between devices: 13.1 us -> 32.4 us
  local copies, waits for them, and re-layouts: 21 us -> 38.1 us
  Pallas kernels: 11.3 us -> 27.8 us
  between operations: 14.1 us -> 1.07 us
  other arithmetic: 4.21 us -> 9.62 us
    all_gather x4 -> x0, waiting for transfers between devices: 162 us -> none  [local(): lax.all_gather(p, BOTH, axis=0, tiled=False)]
    ppermute x9 -> x31, waiting for transfers between devices: 23.6 us -> 102 us  [exchange(): lax.ppermute(values, axis, [(i, i ^ bit) for i in range(lax.axis_size(axi...]
    all_to_all x1 -> x0, blocking collectives: 20.9 us -> none  [local(): got = lax.all_to_all(sent, BOTH, split_axis=0, concat_axis=0, tiled=True)]
    pallas_call x7, Pallas kernels: 11.3 us -> 27.8 us  [layer_call(): pl.pallas_call(kernel, out_shape=outs, in_specs=[vmem] * len(arrays) + [a...]
    ppermute x9 -> x31, starting transfers between devices: 12.9 us -> 24.9 us  [exchange(): lax.ppermute(values, axis, [(i, i ^ bit) for i in range(lax.axis_size(axi...]
    rev x0 -> x4, local copies, waits for them, and re-layouts: none -> 8.49 us  [flipped(): split[..., ::-1, :]]
    all_to_all x0 -> x1, starting transfers between devices: none -> 7.56 us  [local(): got = lax.all_to_all(sent, BOTH, split_axis=0, concat_axis=0, tiled=True)]
    slice x5 -> x0, local copies, waits for them, and re-layouts: 5.28 us -> none  [the longest x4 4.15 us: local(): weight[layer, 2 - taps:]]
  transfers between devices with their start and end apart: 13 -> 32, of which waited for: 9 -> 14; matrix products, arithmetic and copies ran while one was open for 3% -> 14% of each run, Pallas kernels for 2% -> 5%
where the time goes in v2:
time: 223 us; the launch traced here: 222 us
  waiting for transfers between devices  102 us (46%)
  local copies, waits for them, and re-layouts  38.1 us (17%)
  starting transfers between devices  32.4 us (15%)
  Pallas kernels  27.8 us (12%)
  blocking collectives  10.9 us (5%)
  other arithmetic  9.62 us (4%)
    ppermute x31, waiting for transfers between devices, exchange(): lax.ppermute(values, axis, [(i, i ^ bit) for i in range(lax.axis_size(axi...  102 us
    pallas_call x7, Pallas kernels, layer_call(): pl.pallas_call(kernel, out_shape=outs, in_specs=[vmem] * len(arrays) + [a...  27.8 us
    ppermute x31, starting transfers between devices, exchange(): lax.ppermute(values, axis, [(i, i ^ bit) for i in range(lax.axis_size(axi...  24.9 us
    all_to_all x1, blocking collectives, local(): back = lax.all_to_all(back, BOTH, split_axis=0, concat_axis=0, tiled=True)  10.9 us
    unnamed x40, local copies, waits for them, and re-layouts  9.91 us
    rev x4, local copies, waits for them, and re-layouts, flipped(): split[..., ::-1, :]  8.49 us
    all_to_all x1, starting transfers between devices, local(): got = lax.all_to_all(sent, BOTH, split_axis=0, concat_axis=0, tiled=True)  7.56 us
  transfers between devices with their start and end apart: 32, of which 14 were waited for; matrix products, arithmetic and copies ran while one was open for 14% of the time, Pallas kernels for 5%

profile of v2, /device:TPU:0, one launch (start us, length us, event | category | flops | bytes accessed | tf_op | source)
XLA Modules:
  0.0 221.6 jit_solution(7595847486653222771)
XLA Ops:
  3.5 7.6 %all-to-all-start = ((bf16[16,2,12,256]{3,1,2,0:T(2,128)(2,1)}), bf16[16,2,12,256]{3,1,2,0:T(2,128)(2,1)}, u32[]{:S(2)}, u32[]{:S(2)}) async-start(bf16[16,2,12,256]{3,1,2,0:T(2,128)(2,1)} %copy.19), calls=%async_computation | async-start | bytes 393216 | tf_op jit(solution)/shard_map/all_to_all | solution.py:249
  14.1 2.8 %collective-permute-start.2 = (bf16[1,2,640,256]{3,2,1,0:T(8,128)(2,1)}, bf16[1,2,640,256]{3,2,1,0:T(8,128)(2,1)}, u32[]{:S(2)}, u32[]{:S(2)}) collective-permute-start(bf16[1,2,640,256]{3,2,1,0:T(8,128)(2,1)} %fusion.3), channel_id=1, source_target_pairs={{0,2},{1,3},{2,0},{3,1},{4,6},{5,7},{6,4},{7,5},{8,10},{9,11},{10,... | collective-permute-start | bytes 1966088 | tf_op jit(solution)/shard_map/ppermute | solution.py:23
  23.6 1.7 copy.37
  25.2 1.7 reshape_reshape.12
  27.0 3.2 %rev.12 = bf16[2,4,12,2,2,256]{5,4,3,1,2,0:T(2,128)(2,1)} reverse(bf16[2,4,12,2,2,256]{5,4,3,1,2,0:T(2,128)(2,1)} %reshape_reshape.12), dimensions={4} | reverse | bytes 393216 | tf_op jit(solution)/shard_map/rev | solution.py:206
  30.2 26.2 %collective-permute-done.2.refs_3_.refs_5_.refs_7_ = bf16[1,2,640,256]{3,2,1,0:T(8,128)(2,1)} collective-permute-done((bf16[1,2,640,256]{3,2,1,0:T(8,128)(2,1)}, bf16[1,2,640,256]{3,2,1,0:T(8,128)(2,1)}, u32[]{:S(2)}, u32[]{:S(2)}) %collective-permute-start.2) | collective-permute-done | bytes 655392 | tf_op jit(solution)/shard_map/ppermute | solution.py:23
  57.7 1.8 broadcast_select_fusion.1
  59.5 1.7 reshape_reshape.13
  61.3 3.2 %rev.13 = bf16[2,4,12,1,2,512]{5,4,1,2,0,3:T(2,128)(2,1)} reverse(bf16[2,4,12,1,2,512]{5,4,1,2,0,3:T(2,128)(2,1)} %reshape_reshape.13), dimensions={4} | reverse | bytes 393216 | tf_op jit(solution)/shard_map/rev | solution.py:206
  65.8 1.6 broadcast_select_fusion.3
  67.4 1.8 reshape.56
  69.2 6.5 %collective-permute-done = bf16[2,4,12,1024]{3,1,2,0:T(4,128)(2,1)S(1)} collective-permute-done((bf16[2,4,12,1024]{3,1,2,0:T(4,128)(2,1)}, bf16[2,4,12,1024]{3,1,2,0:T(4,128)(2,1)S(1)}, u32[]{:S(2)}, u32[]{:S(2)}) %collective-permute-start) | collective-permute-done | bytes 196640 | tf_op jit(solution)/shard_map/ppermute | solution.py:23
  75.7 11.4 %collective-permute-done.16.refs_6_.refs_7_.refs_8_ = bf16[1,2,384,256]{3,2,1,0:T(8,128)(2,1)} collective-permute-done((bf16[1,2,384,256]{3,2,1,0:T(8,128)(2,1)}, bf16[1,2,384,256]{3,2,1,0:T(8,128)(2,1)}, u32[]{:S(2)}, u32[]{:S(2)}) %collective-permute-start.16) | collective-permute-done | bytes 393248 | tf_op jit(solution)/shard_map/ppermute | solution.py:23
  89.3 15.7 %collective-permute-done.4.refs_5_.refs_7_.refs_9_ = bf16[1,2,640,256]{3,2,1,0:T(8,128)(2,1)} collective-permute-done((bf16[1,2,640,256]{3,2,1,0:T(8,128)(2,1)}, bf16[1,2,640,256]{3,2,1,0:T(8,128)(2,1)}, u32[]{:S(2)}, u32[]{:S(2)}) %collective-permute-start.4) | collective-permute-done | bytes 655392 | tf_op jit(solution)/shard_map/ppermute | solution.py:23
  106.4 10.6 %collective-permute-done.5.refs_6_.refs_8_.refs_10_ = bf16[1,2,640,256]{3,2,1,0:T(8,128)(2,1)} collective-permute-done((bf16[1,2,640,256]{3,2,1,0:T(8,128)(2,1)}, bf16[1,2,640,256]{3,2,1,0:T(8,128)(2,1)}, u32[]{:S(2)}, u32[]{:S(2)}) %collective-permute-start.5) | collective-permute-done | bytes 655392 | tf_op jit(solution)/shard_map/ppermute | solution.py:23
  122.5 3.2 %layer_forward.3 = (bf16[96,1024]{1,0:T(8,128)(2,1)S(1)}, bf16[96,1024]{1,0:T(8,128)(2,1)S(1)}, f32[2,96,256]{2,1,0:T(8,128)S(1)}, f32[2,96,256]{2,1,0:T(8,128)S(1)}) custom-call(bf16[96,1024]{1,0:T(8,128)(2,1)S(1)} %bitcast.100, bf16[1,2,1280,256]{3,2,1,0:T(8,128)(2,1)S(1)} %fusion.refs_1_.refs_3_.refs_5_, ...), custom_call_target="tpu_custom_call" | custom-call | flops 503316480 | bytes 5242880 | tf_op jit(solution)/shard_map/layer_forward/pallas_call | solution.py:280
  127.1 2.6 %collective-permute-done.17.refs_7_.refs_8_.refs_9_ = bf16[1,2,384,256]{3,2,1,0:T(8,128)(2,1)S(1)} collective-permute-done((bf16[1,2,384,256]{3,2,1,0:T(8,128)(2,1)}, bf16[1,2,384,256]{3,2,1,0:T(8,128)(2,1)S(1)}, u32[]{:S(2)}, u32[]{:S(2)}) %collective-permute-start.17) | collective-permute-done | bytes 393248 | tf_op jit(solution)/shard_map/ppermute | solution.py:23
  131.2 6.1 %collective-permute-done.18.refs_8_.refs_9_.refs_10_ = bf16[1,2,384,256]{3,2,1,0:T(8,128)(2,1)S(1)} collective-permute-done((bf16[1,2,384,256]{3,2,1,0:T(8,128)(2,1)}, bf16[1,2,384,256]{3,2,1,0:T(8,128)(2,1)S(1)}, u32[]{:S(2)}, u32[]{:S(2)}) %collective-permute-start.18) | collective-permute-done | bytes 393248 | tf_op jit(solution)/shard_map/ppermute | solution.py:23
  137.8 3.2 %layer_forward.4 = (bf16[96,1024]{1,0:T(8,128)(2,1)S(1)}, bf16[96,1024]{1,0:T(8,128)(2,1)S(1)}, f32[2,96,256]{2,1,0:T(8,128)S(1)}, f32[2,96,256]{2,1,0:T(8,128)S(1)}) custom-call(bf16[96,1024]{1,0:T(8,128)(2,1)S(1)} %get-tuple-element.23.refs_0_, bf16[96,1024]{1,0:T(8,128)(2,1)S(1)} %get-tuple-element.24.refs_1_, ...), custom_call_target="tpu_custom_call" | custom-call | flops 503316480 | bytes 5242880 | tf_op jit(solution)/shard_map/layer_forward/pallas_call | solution.py:280
  142.5 5.3 %collective-permute-done.13.refs_2_ = bf16[96,1024]{1,0:T(8,128)(2,1)S(1)} collective-permute-done((bf16[96,1024]{1,0:T(8,128)(2,1)S(1)}, bf16[96,1024]{1,0:T(8,128)(2,1)S(1)}, u32[]{:S(2)}, u32[]{:S(2)}) %collective-permute-start.13) | collective-permute-done | bytes 196640 | tf_op jit(solution)/shard_map/ppermute | solution.py:23
  147.8 3.2 %layer_forward.5 = (bf16[96,1024]{1,0:T(8,128)(2,1)S(1)}, bf16[96,1024]{1,0:T(8,128)(2,1)S(1)}, f32[2,96,256]{2,1,0:T(8,128)S(1)}, f32[2,96,256]{2,1,0:T(8,128)S(1)}) custom-call(bf16[96,1024]{1,0:T(8,128)(2,1)S(1)} %get-tuple-element.25.refs_0_, bf16[96,1024]{1,0:T(8,128)(2,1)S(1)} %get-tuple-element.26.refs_1_, ...), custom_call_target="tpu_custom_call" | custom-call | flops 301989888 | bytes 3145728 | tf_op jit(solution)/shard_map/layer_forward/pallas_call | solution.py:280
  152.6 4.4 %collective-permute-done.25.refs_2_ = bf16[96,1024]{1,0:T(8,128)(2,1)S(1)} collective-permute-done((bf16[96,1024]{1,0:T(8,128)(2,1)S(1)}, bf16[96,1024]{1,0:T(8,128)(2,1)S(1)}, u32[]{:S(2)}, u32[]{:S(2)}) %collective-permute-start.25) | collective-permute-done | bytes 196640 | tf_op jit(solution)/shard_map/ppermute | solution.py:23
  157.1 4.5 %layer_last.1 = (bf16[96,1024]{1,0:T(8,128)(2,1)S(1)}, bf16[96,1024]{1,0:T(8,128)(2,1)S(1)}, bf16[96,1024]{1,0:T(8,128)(2,1)S(1)}) custom-call(bf16[96,1024]{1,0:T(8,128)(2,1)S(1)} %get-tuple-element.27.refs_0_, bf16[96,1024]{1,0:T(8,128)(2,1)S(1)} %get-tuple-element.28.refs_1_, bf16[96,1024]{1,0:T(8,128)(2,1)S(1)} %collective-permute-done.25.refs_2_, ...), custom_call_target="tpu_custom_call" | custom-call | flops 603979776 | bytes 3145728 | tf_op jit(solution)/shard_map/layer_last/pallas_call | solution.py:280
  164.4 4.2 %collective-permute-done.27.refs_2_ = bf16[96,1024]{1,0:T(8,128)(2,1)S(1)} collective-permute-done((bf16[96,1024]{1,0:T(8,128)(2,1)S(1)}, bf16[96,1024]{1,0:T(8,128)(2,1)S(1)}, u32[]{:S(2)}, u32[]{:S(2)}) %collective-permute-start.27) | collective-permute-done | bytes 196640 | tf_op jit(solution)/shard_map/ppermute | solution.py:23
  168.6 4.0 %layer_backward.3 = (bf16[96,1024]{1,0:T(8,128)(2,1)S(1)}, bf16[96,1024]{1,0:T(8,128)(2,1)S(1)}) custom-call(bf16[96,1024]{1,0:T(8,128)(2,1)S(1)} %bitcast.99, bf16[96,1024]{1,0:T(8,128)(2,1)S(1)} %get-tuple-element.31.refs_1_, bf16[96,1024]{1,0:T(8,128)(2,1)S(1)} %collective-permute-done.27.refs_2_, f32[2,96,256]{2,1,0:T(8,128)S(1)} %get-tuple-element.32.refs_3_, ...), custom_call_target="tpu_custom_call" | custom-call | flops 301989888 | bytes 3145728 | tf_op jit(solution)/shard_map/layer_backward/pallas_call | solution.py:280
  174.1 4.2 %collective-permute-done.28.refs_2_ = bf16[96,1024]{1,0:T(8,128)(2,1)S(1)} collective-permute-done((bf16[96,1024]{1,0:T(8,128)(2,1)S(1)}, bf16[96,1024]{1,0:T(8,128)(2,1)S(1)}, u32[]{:S(2)}, u32[]{:S(2)}) %collective-permute-start.28) | collective-permute-done | bytes 196640 | tf_op jit(solution)/shard_map/ppermute | solution.py:23
  178.4 4.6 %layer_backward.4 = (bf16[96,1024]{1,0:T(8,128)(2,1)S(1)}, bf16[96,1024]{1,0:T(8,128)(2,1)}) custom-call(bf16[96,1024]{1,0:T(8,128)(2,1)S(1)} %get-tuple-element.34.refs_0_, bf16[96,1024]{1,0:T(8,128)(2,1)S(1)} %get-tuple-element.35.refs_1_, bf16[96,1024]{1,0:T(8,128)(2,1)S(1)} %collective-permute-done.28.refs_2_, ...), custom_call_target="tpu_custom_call" | custom-call | flops 503316480 | bytes 5242880 | tf_op jit(solution)/shard_map/layer_backward/pallas_call | solution.py:280
  185.0 1.7 reshape.58
  186.7 1.6 dynamic-slice_bitcast_fusion.1
  193.1 5.3 %layer_backward.5 = (bf16[96,1024]{1,0:T(8,128)(2,1)S(1)}, bf16[96,1024]{1,0:T(8,128)(2,1)S(1)}) custom-call(bf16[96,1024]{1,0:T(8,128)(2,1)S(1)} %copy-done.12, bf16[96,1024]{1,0:T(8,128)(2,1)} %get-tuple-element.39.refs_1_, bf16[96,1024]{1,0:T(8,128)(2,1)} %collective-permute-done.29.refs_2_, f32[2,96,256]{2,1,0:T(8,128)S(1)} %copy-done.8, ...), custom_call_target="tpu_custom_call" | custom-call | flops 503316480 | bytes 5242880 | tf_op jit(solution)/shard_map/layer_backward/pallas_call | solution.py:280
  202.1 3.1 %collective-permute-done.30 = bf16[4,12,1024]{2,1,0:T(8,128)(2,1)S(1)} collective-permute-done((bf16[4,12,1024]{2,1,0:T(8,128)(2,1)S(1)}, bf16[4,12,1024]{2,1,0:T(8,128)(2,1)S(1)}, u32[]{:S(2)}, u32[]{:S(2)}) %collective-permute-start.30) | collective-permute-done | bytes 98336 | tf_op jit(solution)/shard_map/ppermute | solution.py:23
  208.5 10.9 %all_to_all.10 = bf16[16,2,12,256]{3,1,2,0:T(2,128)(2,1)S(1)} all-to-all(bf16[16,2,12,256]{3,1,2,0:T(2,128)(2,1)S(1)} %bitcast.109), channel_id=1, replica_groups=mesh['groups'=2,'tm'=4,'chan'=4] {'tm','chan'}, dimensions={0} | all-to-all | bytes 393216 | tf_op jit(solution)/shard_map/all_to_all | solution.py:351
  (127 shorter events, 51.2 us)
Async XLA Ops:
  3.5 20.1 %all-to-all-start = ((bf16[16,2,12,256]{3,1,2,0:T(2,128)(2,1)}), bf16[16,2,12,256]{3,1,2,0:T(2,128)(2,1)}, u32[]{:S(2)}, u32[]{:S(2)}) async-start(bf16[16,2,12,256]{3,1,2,0:T(2,128)(2,1)} %copy.19), calls=%async_computation | async-start | bytes 393216 | tf_op jit(solution)/shard_map/all_to_all | solution.py:249
  14.1 42.3 %collective-permute-start.2 = (bf16[1,2,640,256]{3,2,1,0:T(8,128)(2,1)}, bf16[1,2,640,256]{3,2,1,0:T(8,128)(2,1)}, u32[]{:S(2)}, u32[]{:S(2)}) collective-permute-start(bf16[1,2,640,256]{3,2,1,0:T(8,128)(2,1)} %fusion.3), channel_id=1, source_target_pairs={{0,2},{1,3},{2,0},{3,1},{4,6},{5,7},{6,4},{7,5},{8,10},{9,11},{10,... | collective-permute-start | bytes 1966088 | tf_op jit(solution)/shard_map/ppermute | solution.py:23
  17.0 72.2 %collective-permute-start.1 = (bf16[1,2,1280,256]{3,2,1,0:T(8,128)(2,1)S(1)}, bf16[1,2,1280,256]{3,2,1,0:T(8,128)(2,1)S(1)}, u32[]{:S(2)}, u32[]{:S(2)}) collective-permute-start(bf16[1,2,1280,256]{3,2,1,0:T(8,128)(2,1)S(1)} %fusion.refs_1_.refs_3_.refs_5_), channel_id=1, source_target_pairs={{0,8},{4,12},{8,0},{12,4},{1,9},{5,13},{9,1},{13,5},{2,10},{6,14},... | collective-permute-start | bytes 3932168 | tf_op jit(solution)/shard_map/ppermute | solution.py:23
  21.6 42.9 %collective-permute-start.15 = (bf16[1,2,384,256]{3,2,1,0:T(8,128)(2,1)}, bf16[1,2,384,256]{3,2,1,0:T(8,128)(2,1)}, u32[]{:S(2)}, u32[]{:S(2)}) collective-permute-start(bf16[1,2,384,256]{3,2,1,0:T(8,128)(2,1)} %fusion.5), channel_id=1, source_target_pairs={{0,2},{1,3},{2,0},{3,1},{4,6},{5,7},{6,4},{7,5},{8,10},{9,11},{10,... | collective-permute-start | bytes 1179656 | tf_op jit(solution)/shard_map/ppermute | solution.py:23
  23.3 65.2 %collective-permute-start.14 = (bf16[1,2,768,256]{3,2,1,0:T(8,128)(2,1)S(1)}, bf16[1,2,768,256]{3,2,1,0:T(8,128)(2,1)}, u32[]{:S(2)}, u32[]{:S(2)}) collective-permute-start(bf16[1,2,768,256]{3,2,1,0:T(8,128)(2,1)S(1)} %fusion.1.refs_3_.refs_4_.refs_5_), channel_id=1, source_target_pairs={{0,8},{4,12},{8,0},{12,4},{1,9},{5,13},{9,1},{13,5},{2,10},{6,14},... | collective-permute-start | bytes 2359304 | tf_op jit(solution)/shard_map/ppermute | solution.py:23
  56.4 32.2 %collective-permute-start.3 = (bf16[1,2,640,256]{3,2,1,0:T(8,128)(2,1)}, bf16[1,2,640,256]{3,2,1,0:T(8,128)(2,1)}, u32[]{:S(2)}, u32[]{:S(2)}) collective-permute-start(bf16[1,2,640,256]{3,2,1,0:T(8,128)(2,1)} %collective-permute-done.2.refs_3_.refs_5_.refs_7_), channel_id=1, source_target_pairs={{0,8},{4,12},{8,0},{12,4},{1,9},{5,13},{9,1},{13,5},{2,10},{6,14},... | collective-permute-start | bytes 1966088 | tf_op jit(solution)/shard_map/ppermute | solution.py:23
  64.5 22.6 %collective-permute-start.16 = (bf16[1,2,384,256]{3,2,1,0:T(8,128)(2,1)}, bf16[1,2,384,256]{3,2,1,0:T(8,128)(2,1)}, u32[]{:S(2)}, u32[]{:S(2)}) collective-permute-start(bf16[1,2,384,256]{3,2,1,0:T(8,128)(2,1)} %collective-permute-done.15.refs_5_.refs_6_.refs_7_), channel_id=1, source_target_pairs={{0,8},{4,12},{8,0},{12,4},{1,9},{5,13},{9,1},{13,5},{2,10},{6,14},... | collective-permute-start | bytes 1179656 | tf_op jit(solution)/shard_map/ppermute | solution.py:23
  69.2 6.5 %collective-permute-start = (bf16[2,4,12,1024]{3,1,2,0:T(4,128)(2,1)}, bf16[2,4,12,1024]{3,1,2,0:T(4,128)(2,1)S(1)}, u32[]{:S(2)}, u32[]{:S(2)}) collective-permute-start(bf16[2,4,12,1024]{3,1,2,0:T(4,128)(2,1)} %reshape.56), channel_id=1, source_target_pairs={{0,1},{1,0},{2,3},{3,2},{4,5},{5,4},{6,7},{7,6},{8,9},{9,8},{10,11... | collective-permute-start | bytes 589832 | tf_op jit(solution)/shard_map/ppermute | solution.py:23
  75.7 41.4 %collective-permute-start.6 = (bf16[1,2,1280,256]{3,2,1,0:T(8,128)(2,1)S(1)}, bf16[1,2,1280,256]{3,2,1,0:T(8,128)(2,1)}, u32[]{:S(2)}, u32[]{:S(2)}) collective-permute-start(bf16[1,2,1280,256]{3,2,1,0:T(8,128)(2,1)S(1)} %fusion.refs_1_.refs_3_.refs_5_), channel_id=1, source_target_pairs={{0,4},{4,0},{8,12},{12,8},{1,5},{5,1},{9,13},{13,9},{2,6},{6,2},{1... | collective-permute-start | bytes 3932168 | tf_op jit(solution)/shard_map/ppermute | solution.py:23
  87.0 18.0 %collective-permute-start.4 = (bf16[1,2,640,256]{3,2,1,0:T(8,128)(2,1)}, bf16[1,2,640,256]{3,2,1,0:T(8,128)(2,1)}, u32[]{:S(2)}, u32[]{:S(2)}) collective-permute-start(bf16[1,2,640,256]{3,2,1,0:T(8,128)(2,1)} %collective-permute-done.2.refs_3_.refs_5_.refs_7_), channel_id=1, source_target_pairs={{0,16},{16,0},{1,17},{17,1},{2,18},{18,2},{3,19},{19,3},{4,20},{20... | collective-permute-start | bytes 1966088 | tf_op jit(solution)/shard_map/ppermute | solution.py:23
  88.5 16.5 %collective-permute-start.8 = (bf16[1,2,640,256]{3,2,1,0:T(8,128)(2,1)}, bf16[1,2,640,256]{3,2,1,0:T(8,128)(2,1)S(1)}, u32[]{:S(2)}, u32[]{:S(2)}) collective-permute-start(bf16[1,2,640,256]{3,2,1,0:T(8,128)(2,1)} %collective-permute-done.2.refs_3_.refs_5_.refs_7_), channel_id=1, source_target_pairs={{0,4},{4,0},{8,12},{12,8},{1,5},{5,1},{9,13},{13,9},{2,6},{6,2},{1... | collective-permute-start | bytes 1966088 | tf_op jit(solution)/shard_map/ppermute | solution.py:23
  88.5 28.5 %collective-permute-start.5 = (bf16[1,2,640,256]{3,2,1,0:T(8,128)(2,1)}, bf16[1,2,640,256]{3,2,1,0:T(8,128)(2,1)}, u32[]{:S(2)}, u32[]{:S(2)}) collective-permute-start(bf16[1,2,640,256]{3,2,1,0:T(8,128)(2,1)} %collective-permute-done.3.refs_4_.refs_6_.refs_8_), channel_id=1, source_target_pairs={{0,16},{16,0},{1,17},{17,1},{2,18},{18,2},{3,19},{19,3},{4,20},{20... | collective-permute-start | bytes 1966088 | tf_op jit(solution)/shard_map/ppermute | solution.py:23
  89.1 32.0 %collective-permute-start.7 = (bf16[1,2,1280,256]{3,2,1,0:T(8,128)(2,1)S(1)}, bf16[1,2,1280,256]{3,2,1,0:T(8,128)(2,1)}, u32[]{:S(2)}, u32[]{:S(2)}) collective-permute-start(bf16[1,2,1280,256]{3,2,1,0:T(8,128)(2,1)S(1)} %collective-permute-done.1.refs_2_.refs_4_.refs_6_), channel_id=1, source_target_pairs={{0,4},{4,0},{8,12},{12,8},{1,5},{5,1},{9,13},{13,9},{2,6},{6,2},{1... | collective-permute-start | bytes 3932168 | tf_op jit(solution)/shard_map/ppermute | solution.py:23
  105.0 12.5 %collective-permute-start.9 = (bf16[1,2,640,256]{3,2,1,0:T(8,128)(2,1)}, bf16[1,2,640,256]{3,2,1,0:T(8,128)(2,1)}, u32[]{:S(2)}, u32[]{:S(2)}) collective-permute-start(bf16[1,2,640,256]{3,2,1,0:T(8,128)(2,1)} %collective-permute-done.3.refs_4_.refs_6_.refs_8_), channel_id=1, source_target_pairs={{0,4},{4,0},{8,12},{12,8},{1,5},{5,1},{9,13},{13,9},{2,6},{6,2},{1... | collective-permute-start | bytes 1966088 | tf_op jit(solution)/shard_map/ppermute | solution.py:23
  105.9 13.1 %collective-permute-start.10 = (bf16[1,2,640,256]{3,2,1,0:T(8,128)(2,1)}, bf16[1,2,640,256]{3,2,1,0:T(8,128)(2,1)}, u32[]{:S(2)}, u32[]{:S(2)}) collective-permute-start(bf16[1,2,640,256]{3,2,1,0:T(8,128)(2,1)} %collective-permute-done.4.refs_5_.refs_7_.refs_9_), channel_id=1, source_target_pairs={{0,4},{4,0},{8,12},{12,8},{1,5},{5,1},{9,13},{13,9},{2,6},{6,2},{1... | collective-permute-start | bytes 1966088 | tf_op jit(solution)/shard_map/ppermute | solution.py:23
  117.0 2.6 %collective-permute-start.11 = (bf16[1,2,640,256]{3,2,1,0:T(8,128)(2,1)}, bf16[1,2,640,256]{3,2,1,0:T(8,128)(2,1)}, u32[]{:S(2)}, u32[]{:S(2)}) collective-permute-start(bf16[1,2,640,256]{3,2,1,0:T(8,128)(2,1)} %collective-permute-done.5.refs_6_.refs_8_.refs_10_), channel_id=1, source_target_pairs={{0,4},{4,0},{8,12},{12,8},{1,5},{5,1},{9,13},{13,9},{2,6},{6,2},{1... | collective-permute-start | bytes 1966088 | tf_op jit(solution)/shard_map/ppermute | solution.py:23
  117.0 23.9 %collective-permute-start.19 = (bf16[1,2,768,256]{3,2,1,0:T(8,128)(2,1)S(1)}, bf16[1,2,768,256]{3,2,1,0:T(8,128)(2,1)S(1)}, u32[]{:S(2)}, u32[]{:S(2)}) collective-permute-start(bf16[1,2,768,256]{3,2,1,0:T(8,128)(2,1)S(1)} %fusion.1.refs_3_.refs_4_.refs_5_), channel_id=1, source_target_pairs={{0,4},{4,0},{8,12},{12,8},{1,5},{5,1},{9,13},{13,9},{2,6},{6,2},{1... | collective-permute-start | bytes 2359304 | tf_op jit(solution)/shard_map/ppermute | solution.py:23
  117.5 12.2 %collective-permute-start.17 = (bf16[1,2,384,256]{3,2,1,0:T(8,128)(2,1)}, bf16[1,2,384,256]{3,2,1,0:T(8,128)(2,1)S(1)}, u32[]{:S(2)}, u32[]{:S(2)}) collective-permute-start(bf16[1,2,384,256]{3,2,1,0:T(8,128)(2,1)} %collective-permute-done.15.refs_5_.refs_6_.refs_7_), channel_id=1, source_target_pairs={{0,16},{16,0},{1,17},{17,1},{2,18},{18,2},{3,19},{19,3},{4,20},{20... | collective-permute-start | bytes 1179656 | tf_op jit(solution)/shard_map/ppermute | solution.py:23
  119.0 12.2 %collective-permute-start.21 = (bf16[1,2,384,256]{3,2,1,0:T(8,128)(2,1)}, bf16[1,2,384,256]{3,2,1,0:T(8,128)(2,1)S(1)}, u32[]{:S(2)}, u32[]{:S(2)}) collective-permute-start(bf16[1,2,384,256]{3,2,1,0:T(8,128)(2,1)} %collective-permute-done.15.refs_5_.refs_6_.refs_7_), channel_id=1, source_target_pairs={{0,4},{4,0},{8,12},{12,8},{1,5},{5,1},{9,13},{13,9},{2,6},{6,2},{1... | collective-permute-start | bytes 1179656 | tf_op jit(solution)/shard_map/ppermute | solution.py:23
  119.6 17.6 %collective-permute-start.18 = (bf16[1,2,384,256]{3,2,1,0:T(8,128)(2,1)}, bf16[1,2,384,256]{3,2,1,0:T(8,128)(2,1)S(1)}, u32[]{:S(2)}, u32[]{:S(2)}) collective-permute-start(bf16[1,2,384,256]{3,2,1,0:T(8,128)(2,1)} %collective-permute-done.16.refs_6_.refs_7_.refs_8_), channel_id=1, source_target_pairs={{0,16},{16,0},{1,17},{17,1},{2,18},{18,2},{3,19},{19,3},{4,20},{20... | collective-permute-start | bytes 1179656 | tf_op jit(solution)/shard_map/ppermute | solution.py:23
  121.1 21.4 %collective-permute-start.20 = (bf16[1,2,768,256]{3,2,1,0:T(8,128)(2,1)}, bf16[1,2,768,256]{3,2,1,0:T(8,128)(2,1)S(1)}, u32[]{:S(2)}, u32[]{:S(2)}) collective-permute-start(bf16[1,2,768,256]{3,2,1,0:T(8,128)(2,1)} %collective-permute-done.14.refs_4_.refs_5_.refs_6_), channel_id=1, source_target_pairs={{0,4},{4,0},{8,12},{12,8},{1,5},{5,1},{9,13},{13,9},{2,6},{6,2},{1... | collective-permute-start | bytes 2359304 | tf_op jit(solution)/shard_map/ppermute | solution.py:23
  129.7 7.6 %collective-permute-start.12 = (bf16[96,1024]{1,0:T(8,128)(2,1)S(1)}, bf16[96,1024]{1,0:T(8,128)(2,1)S(1)}, u32[]{:S(2)}, u32[]{:S(2)}) collective-permute-start(bf16[96,1024]{1,0:T(8,128)(2,1)S(1)} %get-tuple-element.24.refs_1_), channel_id=1, source_target_pairs={{0,1},{1,0},{2,3},{3,2},{4,5},{5,4},{6,7},{7,6},{8,9},{9,8},{10,11... | collective-permute-start | bytes 589832 | tf_op jit(solution)/shard_map/ppermute | solution.py:23
  131.2 11.3 %collective-permute-start.22 = (bf16[1,2,384,256]{3,2,1,0:T(8,128)(2,1)}, bf16[1,2,384,256]{3,2,1,0:T(8,128)(2,1)S(1)}, u32[]{:S(2)}, u32[]{:S(2)}) collective-permute-start(bf16[1,2,384,256]{3,2,1,0:T(8,128)(2,1)} %collective-permute-done.16.refs_6_.refs_7_.refs_8_), channel_id=1, source_target_pairs={{0,4},{4,0},{8,12},{12,8},{1,5},{5,1},{9,13},{13,9},{2,6},{6,2},{1... | collective-permute-start | bytes 1179656 | tf_op jit(solution)/shard_map/ppermute | solution.py:23
  137.3 5.2 %collective-permute-start.23 = (bf16[1,2,384,256]{3,2,1,0:T(8,128)(2,1)S(1)}, bf16[1,2,384,256]{3,2,1,0:T(8,128)(2,1)S(1)}, u32[]{:S(2)}, u32[]{:S(2)}) collective-permute-start(bf16[1,2,384,256]{3,2,1,0:T(8,128)(2,1)S(1)} %collective-permute-done.17.refs_7_.refs_8_.refs_9_), channel_id=1, source_target_pairs={{0,4},{4,0},{8,12},{12,8},{1,5},{5,1},{9,13},{13,9},{2,6},{6,2},{1... | collective-permute-start | bytes 1179656 | tf_op jit(solution)/shard_map/ppermute | solution.py:23
  137.3 5.2 %collective-permute-start.24 = (bf16[1,2,384,256]{3,2,1,0:T(8,128)(2,1)S(1)}, bf16[1,2,384,256]{3,2,1,0:T(8,128)(2,1)S(1)}, u32[]{:S(2)}, u32[]{:S(2)}) collective-permute-start(bf16[1,2,384,256]{3,2,1,0:T(8,128)(2,1)S(1)} %collective-permute-done.18.refs_8_.refs_9_.refs_10_), channel_id=1, source_target_pairs={{0,4},{4,0},{8,12},{12,8},{1,5},{5,1},{9,13},{13,9},{2,6},{6,2},{1... | collective-permute-start | bytes 1179656 | tf_op jit(solution)/shard_map/ppermute | solution.py:23
  141.0 6.9 %collective-permute-start.13 = (bf16[96,1024]{1,0:T(8,128)(2,1)S(1)}, bf16[96,1024]{1,0:T(8,128)(2,1)S(1)}, u32[]{:S(2)}, u32[]{:S(2)}) collective-permute-start(bf16[96,1024]{1,0:T(8,128)(2,1)S(1)} %get-tuple-element.26.refs_1_), channel_id=1, source_target_pairs={{0,1},{1,0},{2,3},{3,2},{4,5},{5,4},{6,7},{7,6},{8,9},{9,8},{10,11... | collective-permute-start | bytes 589832 | tf_op jit(solution)/shard_map/ppermute | solution.py:23
  151.1 6.0 %collective-permute-start.25 = (bf16[96,1024]{1,0:T(8,128)(2,1)S(1)}, bf16[96,1024]{1,0:T(8,128)(2,1)S(1)}, u32[]{:S(2)}, u32[]{:S(2)}) collective-permute-start(bf16[96,1024]{1,0:T(8,128)(2,1)S(1)} %get-tuple-element.28.refs_1_), channel_id=1, source_target_pairs={{0,1},{1,0},{2,3},{3,2},{4,5},{5,4},{6,7},{7,6},{8,9},{9,8},{10,11... | collective-permute-start | bytes 589832 | tf_op jit(solution)/shard_map/ppermute | solution.py:23
  163.0 5.7 %collective-permute-start.27 = (bf16[96,1024]{1,0:T(8,128)(2,1)S(1)}, bf16[96,1024]{1,0:T(8,128)(2,1)S(1)}, u32[]{:S(2)}, u32[]{:S(2)}) collective-permute-start(bf16[96,1024]{1,0:T(8,128)(2,1)S(1)} %get-tuple-element.31.refs_1_), channel_id=1, source_target_pairs={{0,1},{1,0},{2,3},{3,2},{4,5},{5,4},{6,7},{7,6},{8,9},{9,8},{10,11... | collective-permute-start | bytes 589832 | tf_op jit(solution)/shard_map/ppermute | solution.py:23
  172.6 5.7 %collective-permute-start.28 = (bf16[96,1024]{1,0:T(8,128)(2,1)S(1)}, bf16[96,1024]{1,0:T(8,128)(2,1)S(1)}, u32[]{:S(2)}, u32[]{:S(2)}) collective-permute-start(bf16[96,1024]{1,0:T(8,128)(2,1)S(1)} %get-tuple-element.35.refs_1_), channel_id=1, source_target_pairs={{0,1},{1,0},{2,3},{3,2},{4,5},{5,4},{6,7},{7,6},{8,9},{9,8},{10,11... | collective-permute-start | bytes 589832 | tf_op jit(solution)/shard_map/ppermute | solution.py:23
  183.6 6.8 %collective-permute-start.29 = (bf16[96,1024]{1,0:T(8,128)(2,1)}, bf16[96,1024]{1,0:T(8,128)(2,1)}, u32[]{:S(2)}, u32[]{:S(2)}) collective-permute-start(bf16[96,1024]{1,0:T(8,128)(2,1)} %get-tuple-element.39.refs_1_), channel_id=1, source_target_pairs={{0,1},{1,0},{2,3},{3,2},{4,5},{5,4},{6,7},{7,6},{8,9},{9,8},{10,11... | collective-permute-start | bytes 589832 | tf_op jit(solution)/shard_map/ppermute | solution.py:23
  188.3 12.6 %collective-permute-start.26 = (bf16[4,12,1024]{2,1,0:T(8,128)(2,1)}, bf16[4,12,1024]{2,1,0:T(8,128)(2,1)}, u32[]{:S(2)}, u32[]{:S(2)}) collective-permute-start(bf16[4,12,1024]{2,1,0:T(8,128)(2,1)} %dynamic-slice_bitcast_fusion.1), channel_id=1, source_target_pairs={{0,1},{1,0},{2,3},{3,2},{4,5},{5,4},{6,7},{7,6},{8,9},{9,8},{10,11... | collective-permute-start | bytes 294920 | tf_op jit(solution)/shard_map/ppermute | solution.py:23
  200.1 5.0 %collective-permute-start.30 = (bf16[4,12,1024]{2,1,0:T(8,128)(2,1)S(1)}, bf16[4,12,1024]{2,1,0:T(8,128)(2,1)S(1)}, u32[]{:S(2)}, u32[]{:S(2)}) collective-permute-start(bf16[4,12,1024]{2,1,0:T(8,128)(2,1)S(1)} %dynamic-slice_bitcast_fusion), channel_id=1, source_target_pairs={{0,1},{1,0},{2,3},{3,2},{4,5},{5,4},{6,7},{7,6},{8,9},{9,8},{10,11... | collective-permute-start | bytes 294920 | tf_op jit(solution)/shard_map/ppermute | solution.py:23
  (18 other events, 65.4 us)

commit v3 on v2

v3 whole, which is shorter than its diff:
```python
import jax
import jax.numpy as jnp
from jax import lax
from jax.experimental import pallas as pl
from jax.experimental.pallas import tpu as pltpu
from jax.sharding import PartitionSpec as P

BOTH = ("tm", "chan")
HALVED = (0, 2)
VMEM_LIMIT = 20 * 1024 * 1024


def dot(left, right):
    return jnp.dot(left, right, preferred_element_type=jnp.float32)


def dot_t(left, right):
    return lax.dot_general(
        left, right, (((1,), (1,)), ((), ())), preferred_element_type=jnp.float32
    )


def exchange(values, axis, bit):
    return lax.ppermute(values, axis, [(i, i ^ bit) for i in range(lax.axis_size(axis))])


def bits_of(axis, least):
    return [1 << b for b in range(10) if least <= 1 << b < lax.axis_size(axis)]


class Piece:
    def __init__(self, array, keys, kind):
        self.array, self.keys, self.kind = array, keys, kind

    def moved(self, axis, bit, kind=None):
        flip = {"chan": (bit, 0), "tm": (0, bit), "groups": (0, 0)}[axis]
        keys = [(k[0] ^ flip[0], k[1] ^ flip[1]) for k in self.keys]
        return Piece(exchange(self.array, axis, bit), keys, kind or self.kind)


def merged(pieces, limit):
    if len(pieces) <= limit:
        return pieces
    joined = []
    for kind in ("full", "mine", "other"):
        same = [p for p in pieces if p.kind == kind]
        if same:
            array = jnp.concatenate([p.array for p in same], axis=0)
            joined.append(Piece(array, sum((p.keys for p in same), []), kind))
    return joined


def doubled(pieces, axis, bits, limit):
    for bit in bits:
        pieces = merged(pieces + [p.moved(axis, bit) for p in pieces], limit)
    return pieces


def packed(sources, taps_of):
    kb, nb = sources[0].shape[2:]
    shapes = []
    for taps in taps_of:
        shapes += [(1, 2 * taps + 1, kb // 2, nb), (1, 2 * taps + 1, kb, nb)]

    def kernel(*refs):
        filt, gate, mix = refs[:3]
        outs, sems = refs[3:-1], refs[-1]
        copies = []
        for n, out in enumerate(outs):
            layer, taps, rows = n // 2, taps_of[n // 2], out.shape[2]
            start = lax.axis_index("groups") * rows if n % 2 == 0 else 0
            window = pl.ds(pl.multiple_of(start, rows), rows)
            for w, ref in enumerate((filt, gate)):
                source = ref.at[layer, pl.ds(2 - taps, taps), window]
                target = out.at[0, pl.ds(w * taps, taps)]
                copies.append(pltpu.make_async_copy(source, target, sems.at[n, w]))
            copies.append(
                pltpu.make_async_copy(mix.at[layer, window], out.at[0, 2 * taps], sems.at[n, 2])
            )
        for copy in copies:
            copy.start()
        for copy in copies:
            copy.wait()

    return pl.pallas_call(
        kernel,
        out_shape=[jax.ShapeDtypeStruct(shape, jnp.bfloat16) for shape in shapes],
        in_specs=[pl.BlockSpec(memory_space=pl.ANY)] * 3,
        out_specs=[pl.BlockSpec(memory_space=pltpu.VMEM)] * len(shapes),
        scratch_shapes=[pltpu.SemaphoreType.DMA((len(shapes), 3))],
        name="pack",
    )(*sources)


class Links:
    def __init__(self, depth):
        self.depth, self.sent = depth, {}

    def move(self, piece, axis, bit, kind=None, after=()):
        sent = self.sent.setdefault(axis, [])
        waits = [*after, *sent[-self.depth :][:1]] if len(sent) >= self.depth else [*after]
        if waits:
            piece.array = lax.optimization_barrier((piece.array, *waits))[0]
        moved = piece.moved(axis, bit, kind)
        sent.append(moved.array)
        return moved


def spread(packs, taps_of, halved_layers, links):
    limit = 16 if lax.axis_size("tm") <= 4 and lax.axis_size("chan") <= 4 else 1
    high = bits_of("tm", 2)
    layers = range(len(taps_of))
    halves = [Piece(packs[2 * n], [(0, 0)], "mine") for n in layers]
    full = [[Piece(packs[2 * n + 1], [(0, 0)], "full")] for n in layers]
    zs = [[] for _ in layers]
    ys = [[] for _ in layers]
    crossed = [[] for _ in layers]
    others = [[] for _ in layers]

    def along_chan(n):
        for bit in bits_of("chan", 2):
            zs[n] = zs[n] + [links.move(p, "chan", bit) for p in [halves[n]] + zs[n]]

    def own_along_tm(n):
        for bit in high:
            if n in halved_layers:
                ys[n] = ys[n] + [links.move(p, "tm", bit) for p in [halves[n]] + ys[n]]
            else:
                full[n] = full[n] + [links.move(p, "tm", bit) for p in full[n]]

    def others_along_tm(n):
        for bit in high:
            source = merged(zs[n] + crossed[n], limit)
            crossed[n] = crossed[n] + [links.move(p, "tm", bit) for p in source]

    def along_groups(n, pieces):
        others[n] = others[n] + [links.move(p, "groups", 1, "other") for p in merged(pieces, limit)]

    steps = [(along_chan, 0), (own_along_tm, 0), (own_along_tm, 1), (along_chan, 1)]
    for step, n in steps:
        step(n)
    for n in layers:
        along_groups(n, ys[n])
        others_along_tm(n)
        along_groups(n, zs[n])
        if n + 2 < len(taps_of):
            along_chan(n + 2)
            own_along_tm(n + 2)
        along_groups(n, crossed[n])
    result = []
    for n in layers:
        pieces = merged(full[n] + ys[n] + zs[n] + crossed[n] + others[n], limit)
        if lax.axis_size("tm") > 1:
            pieces = pieces + [p.moved("tm", 1) for p in pieces]
        result.append(pieces)
    return result


class Blocks:
    def __init__(self, held, panels, taps, square):
        self.held, self.panels, self.taps, self.square = held, panels, taps, square
        self.kblocks = held.shape[0] // panels
        self.kb = held.shape[2]
        self.copies = {}

    def fill(self, refs, plan, sems):
        group = lax.axis_index("groups")
        half = self.kb // 2
        number = 0
        for ref, (keys, kind) in zip(refs, plan):
            for lead, (dz, dtm) in enumerate(keys):
                target = self.held.at[dz // 2 * self.kblocks + dtm]
                if kind != "full":
                    which = group if kind == "mine" else 1 - group
                    window = pl.ds(pl.multiple_of(which * half, half), half)
                    target = self.held.at[dz // 2 * self.kblocks + dtm, :, window]
                copy = pltpu.make_async_copy(ref.at[lead], target, sems.at[number])
                self.copies.setdefault((dz // 2, dtm), []).append(copy)
                number += 1
        for panel in range(self.panels):
            for i in range(self.kblocks):
                for copy in self.copies[panel, i]:
                    copy.start()

    def wait(self, panel, i):
        for copy in self.copies.pop((panel, i), []):
            copy.wait()

    def mat(self, which, panel, i):
        return self.held[panel * self.kblocks + i, which]

    def filt(self, tap, panel, i):
        return self.mat(tap, panel, i)

    def gate(self, tap, panel, i):
        return self.mat(self.taps + tap, panel, i)

    def mixed(self, gated, panel, i):
        mix = self.mat(2 * self.taps, panel, i)
        return dot(gated, mix) if self.square else dot_t(gated, mix)

    def unmixed(self, grad, panel, i):
        mix = self.mat(2 * self.taps, panel, i)
        return dot_t(grad, mix) if self.square else dot(grad, mix)


def down(values, rows):
    return jnp.concatenate([jnp.zeros_like(values[:rows]), values[: values.shape[0] - rows]], axis=0)


def up(values, rows):
    return jnp.concatenate([values[rows:], jnp.zeros_like(values[:rows])], axis=0)


def total(parts):
    if len(parts) == 1:
        return parts[0][...]
    base, own, other = (part[...].astype(jnp.float32) for part in parts)
    return (base + (own + other)).astype(jnp.bfloat16)


def add_to(acc_ref, cols, term, first):
    if first:
        acc_ref[:, cols] = term
    else:
        acc_ref[:, cols] += term


def forward_part(blocks, x_ref, shift, fac_f, fac_g, acc_ref):
    kb, taps = blocks.kb, blocks.taps
    for panel in range(blocks.panels):
        sums = [[None] * taps, [None] * taps]
        for i in range(blocks.kblocks):
            blocks.wait(panel, i)
            x = x_ref[:, pl.ds(i * kb, kb)]
            for n, kernel in enumerate((blocks.filt, blocks.gate)):
                for tap in range(taps):
                    term = dot(x, kernel(tap, panel, i))
                    sums[n][tap] = term if i == 0 else sums[n][tap] + term
        pre = [s[-1] if taps == 1 else s[-1] + down(s[0], shift) for s in sums]
        tanh_value = jnp.tanh(pre[0])
        sig_value = jax.nn.sigmoid(pre[1])
        gated = (tanh_value * sig_value).astype(jnp.bfloat16)
        fac_f[panel] = sig_value * (1.0 - tanh_value * tanh_value)
        fac_g[panel] = tanh_value * sig_value * (1.0 - sig_value)
        for i in range(blocks.kblocks):
            add_to(acc_ref, pl.ds(i * kb, kb), blocks.mixed(gated, panel, i), panel == 0)


def backward_part(blocks, g_ref, shift, fac_f, fac_g, acc_ref):
    kb, taps = blocks.kb, blocks.taps
    for panel in range(blocks.panels):
        grad_z = None
        for i in range(blocks.kblocks):
            term = blocks.unmixed(g_ref[:, pl.ds(i * kb, kb)], panel, i)
            grad_z = term if grad_z is None else grad_z + term
        grad_f = (grad_z * fac_f[panel]).astype(jnp.bfloat16)
        grad_g = (grad_z * fac_g[panel]).astype(jnp.bfloat16)
        for i in range(blocks.kblocks):
            near = None
            for tap in range(taps):
                term = dot_t(grad_f, blocks.filt(tap, panel, i))
                term = term + dot_t(grad_g, blocks.gate(tap, panel, i))
                if tap < taps - 1:
                    term = up(term, shift)
                near = term if near is None else near + term
            add_to(acc_ref, pl.ds(i * kb, kb), near, panel == 0)


def flipped(values, index, count, block):
    shape = values.shape
    for bit in [1 << b for b in range(10) if 1 << b < count]:
        split = values.reshape(*shape[:-1], count // (2 * bit), 2, bit * block)
        values = jnp.where((index & bit) != 0, split[..., ::-1, :], split).reshape(shape)
    return values


def local(records, cotangent, filter_weight, gate_weight, mix_weight):
    layers = filter_weight.shape[0]
    rows, nb = records.shape
    kb = filter_weight.shape[2]
    tm_count, chan_count = lax.axis_size("tm"), lax.axis_size("chan")
    tm_index = lax.axis_index("tm")
    peers = tm_count * chan_count
    panels = chan_count // 2
    width = nb * chan_count
    bf16, f32 = jnp.bfloat16, jnp.float32
    square = kb == nb

    span = -(-rows // (4 * peers)) * 8
    padded = span * peers // 2
    m = tm_count * span

    taps_of = [2 if 2**layer < tm_count else 1 for layer in range(layers)]
    mix_source = mix_weight if square else mix_weight.transpose(0, 2, 1)
    sources = (filter_weight, gate_weight, mix_source)
    pieces_of = spread(packed(sources, taps_of), taps_of, HALVED, Links(2))

    def swap(values):
        return exchange(values, "chan", 1)

    both = jnp.pad(jnp.stack([records, cotangent]), ((0, 0), (0, padded - rows), (0, 0)))
    sent = both.reshape(2, peers // 2, span, nb).transpose(1, 0, 2, 3)
    sent = jnp.broadcast_to(sent[:, None], (peers // 2, 2, 2, span, nb)).reshape(peers, 2, span, nb)
    got = lax.all_to_all(sent, BOTH, split_axis=0, concat_axis=0, tiled=True)
    if not square:
        got = got.reshape(tm_count, chan_count, 2, span, nb).transpose(2, 0, 3, 1, 4)
        got = flipped(got.reshape(2, tm_count, span, width), tm_index, tm_count, kb)
        got = got.reshape(2, tm_count, span, tm_count, kb).transpose(1, 3, 0, 2, 4)
        got = got.reshape(tm_count * tm_count, 2, span, kb)

    def place(s, i):
        return s * tm_count + ((i ^ lax.axis_index("tm")) if square else i)

    def assemble(got_ref, which, target):
        for i in range(tm_count):
            parts = [got_ref[place(s, i), which].astype(f32) for s in range(tm_count)]
            target[:, pl.ds(i * kb, kb)] = jnp.concatenate(parts, axis=0).astype(bf16)

    vmem = pl.BlockSpec(memory_space=pltpu.VMEM)
    anywhere = pl.BlockSpec(memory_space=pl.ANY)
    act = jax.ShapeDtypeStruct((m, width), bf16)
    fac = jax.ShapeDtypeStruct((panels, m, nb), f32)
    acc = [pltpu.VMEM((m, width), f32)]

    def layer_call(layer, body, arrays, held, outs, scratch, passes, name):
        taps, mats = taps_of[layer], 2 * taps_of[layer] + 1
        shift = 2**layer * span
        pieces = pieces_of[layer] if held is None else []
        copies = sum(len(p.keys) for p in pieces)
        plan = [(p.keys, p.kind) for p in pieces]
        shape = (panels * tm_count, mats, kb, nb)
        elems = panels * tm_count * mats * kb * nb
        count = len(arrays)

        def kernel(*refs):
            ins, refs = refs[:count], refs[count:]
            if held is None:
                piece_refs, refs = refs[: len(pieces)], refs[len(pieces) :]
                blocks = Blocks(refs[len(outs)], panels, taps, square)
                blocks.fill(piece_refs, plan, refs[-1])
                body(blocks, shift, ins, refs[: len(outs)], refs[len(outs) + 1 : -1])
            else:
                blocks = Blocks(refs[0], panels, taps, square)
                body(blocks, shift, ins, refs[1 : 1 + len(outs)], refs[1 + len(outs) :])

        filling = held is None
        weights = [p.array for p in pieces] if filling else [held]
        return pl.pallas_call(
            kernel,
            out_shape=[*outs, *([jax.ShapeDtypeStruct(shape, bf16)] if filling else [])],
            in_specs=[vmem] * count + [anywhere if filling else vmem] * len(weights),
            out_specs=[vmem] * (len(outs) + filling),
            scratch_shapes=[*scratch, *([pltpu.SemaphoreType.DMA((copies,))] if filling else [])],
            compiler_params=pltpu.CompilerParams(vmem_limit_bytes=VMEM_LIMIT),
            cost_estimate=pl.CostEstimate(
                flops=2 * m * elems * passes, bytes_accessed=2 * elems, transcendentals=2 * m * nb
            ),
            name=name,
        )(*arrays, *weights)

    def first_body(blocks, shift, ins, outs, scratch):
        sig, grad, part, fac_f, fac_g = outs
        assemble(ins[0], 0, sig)
        assemble(ins[0], 1, grad)
        forward_part(blocks, sig, shift, fac_f, fac_g, scratch[0])
        part[...] = scratch[0][...].astype(bf16)

    def forward_body(blocks, shift, ins, outs, scratch):
        sig, part, fac_f, fac_g = outs
        sig[...] = total(ins)
        forward_part(blocks, sig, shift, fac_f, fac_g, scratch[0])
        part[...] = scratch[0][...].astype(bf16)

    def last_body(blocks, shift, ins, outs, scratch):
        sig, part, gpart = outs
        fac_f, fac_g, acc_ref = scratch
        sig[...] = total(ins[:-1])
        forward_part(blocks, sig, shift, fac_f, fac_g, acc_ref)
        part[...] = acc_ref[...].astype(bf16)
        backward_part(blocks, ins[-1], shift, fac_f, fac_g, acc_ref)
        gpart[...] = acc_ref[...].astype(bf16)

    def backward_body(blocks, shift, ins, outs, scratch):
        now, part = outs
        now[...] = total(ins[:3])
        backward_part(blocks, now, shift, ins[3], ins[4], scratch[0])
        part[...] = scratch[0][...].astype(bf16)

    def final_body(blocks, shift, ins, outs, scratch):
        acc_ref, now = scratch
        now[...] = total(ins[:3])
        backward_part(blocks, now, shift, ins[3], ins[4], acc_ref)
        even = lax.axis_index("chan") % 2 == 0
        for i in range(tm_count):
            cols = pl.ds(i * kb, kb)
            base = now[:, cols].astype(f32)
            value = acc_ref[:, cols] + jnp.where(even, base, jnp.zeros_like(base))
            out = sum(ins[n][:, cols].astype(f32) for n in (6, 7)) + ins[5][:, cols].astype(f32)
            if square:
                out = jnp.where(even, out[:, : kb // 2], out[:, kb // 2 :])
            for s in range(tm_count):
                part = slice(s * span, (s + 1) * span)
                outs[0][place(s, i), :, :kb] = value[part].astype(bf16)
                outs[0][place(s, i), :, kb:] = out[part].astype(bf16)

    factors, helds = [], []
    sig, grad, part, fac_f, fac_g, held = layer_call(
        0, first_body, [got], None, [act, act, act, fac, fac], acc, 1, "layer_first"
    )
    for layer in range(1, layers - 1):
        factors.append((fac_f, fac_g))
        helds.append(held)
        sig, part, fac_f, fac_g, held = layer_call(
            layer, forward_body, [sig, part, swap(part)], None, [act, act, fac, fac], acc, 1, "layer_forward"
        )
    factors.append((fac_f, fac_g))
    helds.append(held)
    facs = [pltpu.VMEM((panels, m, nb), f32)] * 2
    sig, part, gpart, _ = layer_call(
        layers - 1,
        last_body,
        [sig, part, swap(part), grad],
        None,
        [act, act, act],
        facs + acc,
        2,
        "layer_last",
    )
    parts = [grad, gpart, swap(gpart)]
    output = [sig, part, swap(part)]
    for layer in reversed(range(1, layers - 1)):
        now, gpart = layer_call(
            layer,
            backward_body,
            [*parts, *factors[layer]],
            helds[layer],
            [act, act],
            acc,
            1,
            "layer_backward",
        )
        parts = [now, gpart, swap(gpart)]

    extra = kb // 2 if square else kb
    leaving = jax.ShapeDtypeStruct((tm_count * tm_count, span, kb + extra), bf16)
    back = layer_call(
        0,
        final_body,
        [*parts, *factors[0], *output],
        helds[0],
        [leaving],
        [*acc, pltpu.VMEM((m, width), bf16)],
        1,
        "layer_final",
    )[0]
    if not square:

        def regrouped(values):
            values = values.reshape(tm_count, tm_count, span, kb).transpose(0, 2, 1, 3)
            values = flipped(values.reshape(tm_count, span, width), tm_index, tm_count, kb)
            values = values.reshape(tm_count, span, chan_count, nb).transpose(0, 2, 1, 3)
            return values.reshape(peers, span, nb)

        out = regrouped(back[..., kb:])
        out = jnp.where(lax.axis_index("chan") % 2 == 0, out[..., : nb // 2], out[..., nb // 2 :])
        back = jnp.concatenate([regrouped(back[..., :kb]), out], axis=-1)
    back = lax.all_to_all(back, BOTH, split_axis=0, concat_axis=0, tiled=True)
    back = back.reshape(peers // 2, 2, span, nb + nb // 2)
    grads = back[..., :nb].astype(f32)
    input_grad = (grads[:, 0] + grads[:, 1]).astype(bf16).reshape(padded, nb)[:rows]
    output = jnp.concatenate([back[:, 0, :, nb:], back[:, 1, :, nb:]], axis=-1)
    return output.reshape(padded, nb)[:rows], input_grad


def solution(mesh):
    return jax.shard_map(
        local,
        mesh=mesh,
        in_specs=(
            P(("groups", "tm"), "chan"),
            P(("groups", "tm"), "chan"),
            P(None, None, "tm", "chan"),
            P(None, None, "tm", "chan"),
            P(None, "chan", "tm"),
        ),
        out_specs=(P(("groups", "tm"), "chan"), P(("groups", "tm"), "chan")),
        check_vma=False,
    )
```

time: 223 us -> 193 us (0.87)
  local copies, waits for them, and re-layouts: 38.1 us -> 11.3 us
  starting transfers between devices: 32.4 us -> 51.2 us
  waiting for transfers between devices: 102 us -> 90.2 us
  other arithmetic: 9.62 us -> 2.3 us
  Pallas kernels: 27.8 us -> 22.2 us
  blocking collectives: 10.9 us -> 14.3 us
    ppermute x31 -> x55, starting transfers between devices: 24.9 us -> 41.6 us  [exchange(): lax.ppermute(values, axis, [(i, i ^ bit) for i in range(lax.axis_size(axi...]
    ppermute x31 -> x55, waiting for transfers between devices: 102 us -> 90.2 us  [exchange(): lax.ppermute(values, axis, [(i, i ^ bit) for i in range(lax.axis_size(axi...]
    rev x4 -> x0, local copies, waits for them, and re-layouts: 8.49 us -> none  [flipped(): split[..., ::-1, :]]
    reshape x6 -> x0, local copies, waits for them, and re-layouts: 6.86 us -> none  [the longest x4 3.43 us: of_side(): values = values.reshape(tm_count, 2, take, width)]
    another operation x12 -> x0, local copies, waits for them, and re-layouts: 6.18 us -> none  [the longest x3 3.61 us: flipped(): split = values.reshape(*shape[:-1], count // (2 * bit), 2, bit * block)]
    pallas_call x7 -> x8, Pallas kernels: 27.8 us -> 22.2 us  [the longest x7 18.4 us: layer_call(): pl.pallas_call(kernel, out_shape=[*outs, *([jax.ShapeDtypeStruct(shape, b...]
    squeeze x7 -> x0, local copies, waits for them, and re-layouts: 4.91 us -> none  [the longest x2 1.59 us: of_side(): return lax.dynamic_index_in_dim(values, which, 1, keepdims=False)]
    select_n x5 -> x0, other arithmetic: 4.78 us -> none  [the longest x4 3.73 us: flipped(): jnp.where(index & bit != 0, split[..., ::-1, :], split).reshape(shape)]
  transfers between devices with their start and end apart: 32 -> 56, of which waited for: 14 -> 21; matrix products, arithmetic and copies ran while one was open for 14% -> 1% of each run, Pallas kernels for 5% -> 6%
where the time goes in v3:
time: 193 us; the launch traced here: 192 us
  waiting for transfers between devices  90.2 us (47%)
  starting transfers between devices  51.2 us (27%)
  Pallas kernels  22.2 us (12%)
  blocking collectives  14.3 us (7%)
  local copies, waits for them, and re-layouts  11.3 us (6%)
  other arithmetic  2.3 us (1%)
    ppermute x55, waiting for transfers between devices, exchange(): lax.ppermute(values, axis, [(i, i ^ bit) for i in range(lax.axis_size(axi...  90.2 us
    ppermute x55, starting transfers between devices, exchange(): lax.ppermute(values, axis, [(i, i ^ bit) for i in range(lax.axis_size(axi...  41.6 us
    pallas_call x7, Pallas kernels, layer_call(): pl.pallas_call(kernel, out_shape=[*outs, *([jax.ShapeDtypeStruct(shape, b...  18.4 us
    all_to_all x1, blocking collectives, local(): back = lax.all_to_all(back, BOTH, split_axis=0, concat_axis=0, tiled=True)  14.3 us
    unnamed x48, local copies, waits for them, and re-layouts  10.5 us
    all_to_all x1, starting transfers between devices, local(): got = lax.all_to_all(sent, BOTH, split_axis=0, concat_axis=0, tiled=True)  9.61 us
  transfers between devices with their start and end apart: 56, of which 21 were waited for; matrix products, arithmetic and copies ran while one was open for 1% of the time, Pallas kernels for 6%

profile of v3, /device:TPU:0, one launch (start us, length us, event | category | flops | bytes accessed | tf_op | source)
XLA Modules:
  0.0 192.5 jit_solution(7478630867468452644)
XLA Ops:
  0.6 3.8 %pack.1 = (bf16[1,5,128,256]{3,2,1,0:T(8,128)(2,1)}, bf16[1,5,256,256]{3,2,1,0:T(8,128)(2,1)}, bf16[1,5,128,256]{3,2,1,0:T(8,128)(2,1)}, bf16[1,5,256,256]{3,2,1...) custom-call(bf16[4,2,256,256]{3,2,1,0:T(8,128)(2,1)} %refs_0_.1, ...), custom_call_target="tpu_custom_call" | custom-call | tf_op jit(solution)/shard_map/pack/pallas_call | solution.py:85
  4.4 4.1 %collective-permute-start.1 = (bf16[1,5,128,256]{3,2,1,0:T(8,128)(2,1)}, bf16[1,5,128,256]{3,2,1,0:T(8,128)(2,1)S(1)}, u32[]{:S(2)}, u32[]{:S(2)}) collective-permute-start(bf16[1,5,128,256]{3,2,1,0:T(8,128)(2,1)} %get-tuple-element.50), channel_id=1, source_target_pairs={{0,2},{1,3},{2,0},{3,1},{4,6},{5,7},{6,4},{7,5},{8,10},{9,11},{10,... | collective-permute-start | bytes 983048 | tf_op jit(solution)/shard_map/ppermute | solution.py:24
  10.4 20.9 %collective-permute-done.1.refs_3_ = bf16[1,5,128,256]{3,2,1,0:T(8,128)(2,1)S(1)} collective-permute-done((bf16[1,5,128,256]{3,2,1,0:T(8,128)(2,1)}, bf16[1,5,128,256]{3,2,1,0:T(8,128)(2,1)S(1)}, u32[]{:S(2)}, u32[]{:S(2)}) %collective-permute-start.1) | collective-permute-done | bytes 327712 | tf_op jit(solution)/shard_map/ppermute | solution.py:24
  31.3 1.9 collective-permute-start.2
  34.7 8.0 %collective-permute-done.15.refs_5_ = bf16[1,5,128,256]{3,2,1,0:T(8,128)(2,1)} collective-permute-done((bf16[1,5,128,256]{3,2,1,0:T(8,128)(2,1)}, bf16[1,5,128,256]{3,2,1,0:T(8,128)(2,1)}, u32[]{:S(2)}, u32[]{:S(2)}) %collective-permute-start.15) | collective-permute-done | bytes 327712 | tf_op jit(solution)/shard_map/ppermute | solution.py:24
  42.7 1.9 collective-permute-start.14
  46.0 1.6 collective-permute-start.4
  47.6 6.8 %collective-permute-done.41.refs_6_ = bf16[1,3,128,256]{3,2,1,0:T(8,128)(2,1)S(1)} collective-permute-done((bf16[1,3,128,256]{3,2,1,0:T(8,128)(2,1)}, bf16[1,3,128,256]{3,2,1,0:T(8,128)(2,1)S(1)}, u32[]{:S(2)}, u32[]{:S(2)}) %collective-permute-start.41) | collective-permute-done | bytes 196640 | tf_op jit(solution)/shard_map/ppermute | solution.py:24
  60.9 3.1 %collective-permute-start.26 = (bf16[1,3,128,256]{3,2,1,0:T(8,128)(2,1)}, bf16[1,3,128,256]{3,2,1,0:T(8,128)(2,1)}, u32[]{:S(2)}, u32[]{:S(2)}) collective-permute-start(bf16[1,3,128,256]{3,2,1,0:T(8,128)(2,1)} %get-tuple-element.66), channel_id=1, source_target_pairs={{0,8},{4,12},{8,0},{12,4},{1,9},{5,13},{9,1},{13,5},{2,10},{6,14},... | collective-permute-start | bytes 589832 | tf_op jit(solution)/shard_map/ppermute | solution.py:24
  64.1 5.9 %collective-permute-done.26.refs_4_ = bf16[1,3,128,256]{3,2,1,0:T(8,128)(2,1)} collective-permute-done((bf16[1,3,128,256]{3,2,1,0:T(8,128)(2,1)}, bf16[1,3,128,256]{3,2,1,0:T(8,128)(2,1)}, u32[]{:S(2)}, u32[]{:S(2)}) %collective-permute-start.26) | collective-permute-done | bytes 196640 | tf_op jit(solution)/shard_map/ppermute | solution.py:24
  70.6 4.7 %collective-permute-done.17.refs_7_ = bf16[1,5,128,256]{3,2,1,0:T(8,128)(2,1)} collective-permute-done((bf16[1,5,128,256]{3,2,1,0:T(8,128)(2,1)}, bf16[1,5,128,256]{3,2,1,0:T(8,128)(2,1)}, u32[]{:S(2)}, u32[]{:S(2)}) %collective-permute-start.17) | collective-permute-done | bytes 327712 | tf_op jit(solution)/shard_map/ppermute | solution.py:24
  77.0 9.6 %all-to-all-start = ((bf16[16,2,24,256]{3,2,1,0:T(8,128)(2,1)}), bf16[16,2,24,256]{3,2,1,0:T(8,128)(2,1)S(1)}, u32[]{:S(2)}, u32[]{:S(2)}) async-start(bf16[16,2,24,256]{3,2,1,0:T(8,128)(2,1)} %bitcast.9), calls=%async_computation | async-start | bytes 786432 | tf_op jit(solution)/shard_map/all_to_all | solution.py:305
  88.2 1.9 collective-permute-start.28
  91.2 3.4 %collective-permute-done.29.refs_7_ = bf16[1,3,128,256]{3,2,1,0:T(8,128)(2,1)S(1)} collective-permute-done((bf16[1,3,128,256]{3,2,1,0:T(8,128)(2,1)}, bf16[1,3,128,256]{3,2,1,0:T(8,128)(2,1)S(1)}, u32[]{:S(2)}, u32[]{:S(2)}) %collective-permute-start.29) | collective-permute-done | bytes 196640 | tf_op jit(solution)/shard_map/ppermute | solution.py:24
  94.6 2.0 %collective-permute-start.40 = (bf16[1,3,256,256]{3,2,1,0:T(8,128)(2,1)}, bf16[1,3,256,256]{3,2,1,0:T(8,128)(2,1)}, u32[]{:S(2)}, u32[]{:S(2)}) collective-permute-start(bf16[1,3,256,256]{3,2,1,0:T(8,128)(2,1)} %get-tuple-element.74.refs_4_), channel_id=1, source_target_pairs={{0,8},{4,12},{8,0},{12,4},{1,9},{5,13},{9,1},{13,5},{2,10},{6,14},... | collective-permute-start | bytes 1179656 | tf_op jit(solution)/shard_map/ppermute | solution.py:24
  96.6 1.7 collective-permute-done.28.refs_6_
  98.3 1.6 collective-permute-done.33.refs_11_
  108.0 3.2 %layer_first.1 = (bf16[96,1024]{1,0:T(8,128)(2,1)S(1)}, bf16[96,1024]{1,0:T(8,128)(2,1)S(1)}, bf16[96,1024]{1,0:T(8,128)(2,1)S(1)}, f32[2,96,256]{2,1,0:T(8,128)...) custom-call(bf16[16,2,24,256]{3,2,1,0:T(8,128)(2,1)S(1)} %all-to-all-done.refs_0_, ...), custom_call_target="tpu_custom_call" | custom-call | flops 503316480 | bytes 5242880 | tf_op jit(solution)/shard_map/layer_first/pallas_call | solution.py:349
  111.2 2.5 %collective-permute-start.13 = (bf16[96,1024]{1,0:T(8,128)(2,1)S(1)}, bf16[96,1024]{1,0:T(8,128)(2,1)S(1)}, u32[]{:S(2)}, u32[]{:S(2)}) collective-permute-start(bf16[96,1024]{1,0:T(8,128)(2,1)S(1)} %get-tuple-element.55.refs_1_), channel_id=1, source_target_pairs={{0,1},{1,0},{2,3},{3,2},{4,5},{5,4},{6,7},{7,6},{8,9},{9,8},{10,11... | collective-permute-start | bytes 589832 | tf_op jit(solution)/shard_map/ppermute | solution.py:24
  115.4 3.7 %collective-permute-done.13.refs_2_ = bf16[96,1024]{1,0:T(8,128)(2,1)S(1)} collective-permute-done((bf16[96,1024]{1,0:T(8,128)(2,1)S(1)}, bf16[96,1024]{1,0:T(8,128)(2,1)S(1)}, u32[]{:S(2)}, u32[]{:S(2)}) %collective-permute-start.13) | collective-permute-done | bytes 196640 | tf_op jit(solution)/shard_map/ppermute | solution.py:24
  121.2 3.0 %layer_forward.2 = (bf16[96,1024]{1,0:T(8,128)(2,1)S(1)}, bf16[96,1024]{1,0:T(8,128)(2,1)S(1)}, f32[2,96,256]{2,1,0:T(8,128)S(1)}, f32[2,96,256]{2,1,0:T(8,128)S(1)}, bf16[8,5,256,256]{3,2,1,0:T(8,128)(2,1)S(1)}) custom-call(bf16[96,1024]{1,0:T(8,128)(2,1)S(1)} %get-tuple-element.54.refs_0_, bf16[96,1024]{1,0:T(8,128)(2,1)S(1)} %get-tuple-element.55.refs_1_, ...), custom_call_target="tpu_custom_call" | custom-call | flops 503316480 | bytes 5242880 | tf_op jit(solution)/shard_map/layer_forward/pallas_call | solution.py:349
  130.2 2.8 %collective-permute-done.25.refs_2_ = bf16[96,1024]{1,0:T(8,128)(2,1)S(1)} collective-permute-done((bf16[96,1024]{1,0:T(8,128)(2,1)S(1)}, bf16[96,1024]{1,0:T(8,128)(2,1)S(1)}, u32[]{:S(2)}, u32[]{:S(2)}) %collective-permute-start.25) | collective-permute-done | bytes 196640 | tf_op jit(solution)/shard_map/ppermute | solution.py:24
  133.0 2.6 %layer_forward.3 = (bf16[96,1024]{1,0:T(8,128)(2,1)S(1)}, bf16[96,1024]{1,0:T(8,128)(2,1)S(1)}, f32[2,96,256]{2,1,0:T(8,128)S(1)}, f32[2,96,256]{2,1,0:T(8,128)S(1)}, bf16[8,3,256,256]{3,2,1,0:T(8,128)(2,1)S(1)}) custom-call(bf16[96,1024]{1,0:T(8,128)(2,1)S(1)} %get-tuple-element.61.refs_0_, bf16[96,1024]{1,0:T(8,128)(2,1)S(1)} %get-tuple-element.62.refs_1_, ...), custom_call_target="tpu_custom_call" | custom-call | flops 301989888 | bytes 3145728 | tf_op jit(solution)/shard_map/layer_forward/pallas_call | solution.py:349
  136.3 3.3 %collective-permute-done.43.refs_8_ = bf16[1,3,128,256]{3,2,1,0:T(8,128)(2,1)S(1)} collective-permute-done((bf16[1,3,128,256]{3,2,1,0:T(8,128)(2,1)S(1)}, bf16[1,3,128,256]{3,2,1,0:T(8,128)(2,1)S(1)}, u32[]{:S(2)}, u32[]{:S(2)}) %collective-permute-start.43) | collective-permute-done | bytes 196640 | tf_op jit(solution)/shard_map/ppermute | solution.py:24
  141.1 5.9 %collective-permute-done.39.refs_2_ = bf16[96,1024]{1,0:T(8,128)(2,1)S(1)} collective-permute-done((bf16[96,1024]{1,0:T(8,128)(2,1)S(1)}, bf16[96,1024]{1,0:T(8,128)(2,1)S(1)}, u32[]{:S(2)}, u32[]{:S(2)}) %collective-permute-start.39) | collective-permute-done | bytes 196640 | tf_op jit(solution)/shard_map/ppermute | solution.py:24
  146.9 4.1 %layer_last.1 = (bf16[96,1024]{1,0:T(8,128)(2,1)S(1)}, bf16[96,1024]{1,0:T(8,128)(2,1)S(1)}, bf16[96,1024]{1,0:T(8,128)(2,1)S(1)}, bf16[8,3,256,256]{3,2,1,0:T(8,128)(2,1)}) custom-call(bf16[96,1024]{1,0:T(8,128)(2,1)S(1)} %get-tuple-element.71.refs_0_, bf16[96,1024]{1,0:T(8,128)(2,1)S(1)} %get-tuple-element.72.refs_1_, ...), custom_call_target="tpu_custom_call" | custom-call | flops 603979776 | bytes 3145728 | tf_op jit(solution)/shard_map/layer_last/pallas_call | solution.py:349
  151.6 6.0 %collective-permute-done.51.refs_2_ = bf16[96,1024]{1,0:T(8,128)(2,1)S(1)} collective-permute-done((bf16[96,1024]{1,0:T(8,128)(2,1)S(1)}, bf16[96,1024]{1,0:T(8,128)(2,1)S(1)}, u32[]{:S(2)}, u32[]{:S(2)}) %collective-permute-start.51) | collective-permute-done | bytes 196640 | tf_op jit(solution)/shard_map/ppermute | solution.py:24
  161.1 5.7 %collective-permute-done.52.refs_2_ = bf16[96,1024]{1,0:T(8,128)(2,1)S(1)} collective-permute-done((bf16[96,1024]{1,0:T(8,128)(2,1)S(1)}, bf16[96,1024]{1,0:T(8,128)(2,1)S(1)}, u32[]{:S(2)}, u32[]{:S(2)}) %collective-permute-start.52) | collective-permute-done | bytes 196640 | tf_op jit(solution)/shard_map/ppermute | solution.py:24
  166.9 2.1 %layer_backward.3 = (bf16[96,1024]{1,0:T(8,128)(2,1)S(1)}, bf16[96,1024]{1,0:T(8,128)(2,1)S(1)}) custom-call(bf16[96,1024]{1,0:T(8,128)(2,1)S(1)} %get-tuple-element.84.refs_0_, bf16[96,1024]{1,0:T(8,128)(2,1)S(1)} %get-tuple-element.85.refs_1_, bf16[96,1024]{1,0:T(8,128)(2,1)S(1)} %collective-permute-done.52.refs_2_, ...), custom_call_target="tpu_custom_call" | custom-call | flops 503316480 | bytes 5242880 | tf_op jit(solution)/shard_map/layer_backward/pallas_call | solution.py:349
  170.7 4.0 %collective-permute-done.53.refs_2_ = bf16[96,1024]{1,0:T(8,128)(2,1)S(1)} collective-permute-done((bf16[96,1024]{1,0:T(8,128)(2,1)S(1)}, bf16[96,1024]{1,0:T(8,128)(2,1)S(1)}, u32[]{:S(2)}, u32[]{:S(2)}) %collective-permute-start.53) | collective-permute-done | bytes 196640 | tf_op jit(solution)/shard_map/ppermute | solution.py:24
  174.7 2.1 %layer_final.1 = bf16[16,24,384]{2,1,0:T(8,128)(2,1)S(1)} custom-call(bf16[96,1024]{1,0:T(8,128)(2,1)S(1)} %get-tuple-element.89.refs_0_, bf16[96,1024]{1,0:T(8,128)(2,1)S(1)} %get-tuple-element.90.refs_1_, bf16[96,1024]{1,0:T(8,128)(2,1)S(1)} %collective-permute-done.53.refs_2_, f32[2,96,256]{2,1,0:T(8,128)S(1)} %get-tuple-element.91.refs_3_, ...), custom_call_target="tpu_custom_call" | custom-call | flops 503316480 | bytes 5242880 | tf_op jit(solution)/shard_map/layer_final/pallas_call | solution.py:349
  176.7 14.3 %all_to_all.10 = bf16[16,24,384]{2,1,0:T(8,128)(2,1)S(1)} all-to-all(bf16[16,24,384]{2,1,0:T(8,128)(2,1)S(1)} %layer_final.1), channel_id=1, replica_groups=mesh['groups'=2,'tm'=4,'chan'=4] {'tm','chan'}, dimensions={0} | all-to-all | bytes 589824 | tf_op jit(solution)/shard_map/all_to_all | solution.py:468
  (144 shorter events, 43.3 us)
Async XLA Ops:
  4.4 26.9 %collective-permute-start.1 = (bf16[1,5,128,256]{3,2,1,0:T(8,128)(2,1)}, bf16[1,5,128,256]{3,2,1,0:T(8,128)(2,1)S(1)}, u32[]{:S(2)}, u32[]{:S(2)}) collective-permute-start(bf16[1,5,128,256]{3,2,1,0:T(8,128)(2,1)} %get-tuple-element.50), channel_id=1, source_target_pairs={{0,2},{1,3},{2,0},{3,1},{4,6},{5,7},{6,4},{7,5},{8,10},{9,11},{10,... | collective-permute-start | bytes 983048 | tf_op jit(solution)/shard_map/ppermute | solution.py:24
  8.5 22.8 %collective-permute-start = (bf16[1,5,128,256]{3,2,1,0:T(8,128)(2,1)}, bf16[1,5,128,256]{3,2,1,0:T(8,128)(2,1)S(1)}, u32[]{:S(2)}, u32[]{:S(2)}) collective-permute-start(bf16[1,5,128,256]{3,2,1,0:T(8,128)(2,1)} %get-tuple-element.50), channel_id=1, source_target_pairs={{0,8},{4,12},{8,0},{12,4},{1,9},{5,13},{9,1},{13,5},{2,10},{6,14},... | collective-permute-start | bytes 983048 | tf_op jit(solution)/shard_map/ppermute | solution.py:24
  10.1 32.6 %collective-permute-start.15 = (bf16[1,5,128,256]{3,2,1,0:T(8,128)(2,1)}, bf16[1,5,128,256]{3,2,1,0:T(8,128)(2,1)}, u32[]{:S(2)}, u32[]{:S(2)}) collective-permute-start(bf16[1,5,128,256]{3,2,1,0:T(8,128)(2,1)} %get-tuple-element.57), channel_id=1, source_target_pairs={{0,2},{1,3},{2,0},{3,1},{4,6},{5,7},{6,4},{7,5},{8,10},{9,11},{10,... | collective-permute-start | bytes 983048 | tf_op jit(solution)/shard_map/ppermute | solution.py:24
  10.4 34.1 %collective-permute-start.32 = (bf16[1,3,256,256]{3,2,1,0:T(8,128)(2,1)}, bf16[1,3,256,256]{3,2,1,0:T(8,128)(2,1)S(1)}, u32[]{:S(2)}, u32[]{:S(2)}) collective-permute-start(bf16[1,3,256,256]{3,2,1,0:T(8,128)(2,1)} %get-tuple-element.63.refs_3_), channel_id=1, source_target_pairs={{0,4},{4,0},{8,12},{12,8},{1,5},{5,1},{9,13},{13,9},{2,6},{6,2},{1... | collective-permute-start | bytes 1179656 | tf_op jit(solution)/shard_map/ppermute | solution.py:24
  31.3 14.7 %collective-permute-start.27 = (bf16[1,3,128,256]{3,2,1,0:T(8,128)(2,1)}, bf16[1,3,128,256]{3,2,1,0:T(8,128)(2,1)S(1)}, u32[]{:S(2)}, u32[]{:S(2)}) collective-permute-start(bf16[1,3,128,256]{3,2,1,0:T(8,128)(2,1)} %get-tuple-element.66), channel_id=1, source_target_pairs={{0,2},{1,3},{2,0},{3,1},{4,6},{5,7},{6,4},{7,5},{8,10},{9,11},{10,... | collective-permute-start | bytes 589832 | tf_op jit(solution)/shard_map/ppermute | solution.py:24
  31.3 23.0 %collective-permute-start.2 = (bf16[1,5,128,256]{3,2,1,0:T(8,128)(2,1)S(1)}, bf16[1,5,128,256]{3,2,1,0:T(8,128)(2,1)}, u32[]{:S(2)}, u32[]{:S(2)}) collective-permute-start(bf16[1,5,128,256]{3,2,1,0:T(8,128)(2,1)S(1)} %collective-permute-done.1.refs_3_), channel_id=1, source_target_pairs={{0,8},{4,12},{8,0},{12,4},{1,9},{5,13},{9,1},{13,5},{2,10},{6,14},... | collective-permute-start | bytes 983048 | tf_op jit(solution)/shard_map/ppermute | solution.py:24
  33.2 21.9 %collective-permute-start.3 = (bf16[1,5,128,256]{3,2,1,0:T(8,128)(2,1)S(1)}, bf16[1,5,128,256]{3,2,1,0:T(8,128)(2,1)}, u32[]{:S(2)}, u32[]{:S(2)}) collective-permute-start(bf16[1,5,128,256]{3,2,1,0:T(8,128)(2,1)S(1)} %collective-permute-done.refs_2_), channel_id=1, source_target_pairs={{0,16},{16,0},{1,17},{17,1},{2,18},{18,2},{3,19},{19,3},{4,20},{20... | collective-permute-start | bytes 983048 | tf_op jit(solution)/shard_map/ppermute | solution.py:24
  42.7 17.0 %collective-permute-start.14 = (bf16[1,5,256,256]{3,2,1,0:T(8,128)(2,1)}, bf16[1,5,256,256]{3,2,1,0:T(8,128)(2,1)S(1)}, u32[]{:S(2)}, u32[]{:S(2)}) collective-permute-start(bf16[1,5,256,256]{3,2,1,0:T(8,128)(2,1)} %get-tuple-element.56.refs_3_), channel_id=1, source_target_pairs={{0,8},{4,12},{8,0},{12,4},{1,9},{5,13},{9,1},{13,5},{2,10},{6,14},... | collective-permute-start | bytes 1966088 | tf_op jit(solution)/shard_map/ppermute | solution.py:24
  44.5 9.8 %collective-permute-start.41 = (bf16[1,3,128,256]{3,2,1,0:T(8,128)(2,1)}, bf16[1,3,128,256]{3,2,1,0:T(8,128)(2,1)S(1)}, u32[]{:S(2)}, u32[]{:S(2)}) collective-permute-start(bf16[1,3,128,256]{3,2,1,0:T(8,128)(2,1)} %get-tuple-element.76), channel_id=1, source_target_pairs={{0,2},{1,3},{2,0},{3,1},{4,6},{5,7},{6,4},{7,5},{8,10},{9,11},{10,... | collective-permute-start | bytes 589832 | tf_op jit(solution)/shard_map/ppermute | solution.py:24
  46.0 9.8 %collective-permute-start.4 = (bf16[1,5,128,256]{3,2,1,0:T(8,128)(2,1)S(1)}, bf16[1,5,128,256]{3,2,1,0:T(8,128)(2,1)}, u32[]{:S(2)}, u32[]{:S(2)}) collective-permute-start(bf16[1,5,128,256]{3,2,1,0:T(8,128)(2,1)S(1)} %collective-permute-done.1.refs_3_), channel_id=1, source_target_pairs={{0,16},{16,0},{1,17},{17,1},{2,18},{18,2},{3,19},{19,3},{4,20},{20... | collective-permute-start | bytes 983048 | tf_op jit(solution)/shard_map/ppermute | solution.py:24
  58.1 11.9 %collective-permute-start.5 = (bf16[1,5,128,256]{3,2,1,0:T(8,128)(2,1)}, bf16[1,5,128,256]{3,2,1,0:T(8,128)(2,1)}, u32[]{:S(2)}, u32[]{:S(2)}) collective-permute-start(bf16[1,5,128,256]{3,2,1,0:T(8,128)(2,1)} %collective-permute-done.2.refs_4_), channel_id=1, source_target_pairs={{0,16},{16,0},{1,17},{17,1},{2,18},{18,2},{3,19},{19,3},{4,20},{20... | collective-permute-start | bytes 983048 | tf_op jit(solution)/shard_map/ppermute | solution.py:24
  59.7 15.5 %collective-permute-start.17 = (bf16[1,5,128,256]{3,2,1,0:T(8,128)(2,1)}, bf16[1,5,128,256]{3,2,1,0:T(8,128)(2,1)}, u32[]{:S(2)}, u32[]{:S(2)}) collective-permute-start(bf16[1,5,128,256]{3,2,1,0:T(8,128)(2,1)} %collective-permute-done.15.refs_5_), channel_id=1, source_target_pairs={{0,16},{16,0},{1,17},{17,1},{2,18},{18,2},{3,19},{19,3},{4,20},{20... | collective-permute-start | bytes 983048 | tf_op jit(solution)/shard_map/ppermute | solution.py:24
  64.0 22.6 %collective-permute-start.16 = (bf16[1,5,128,256]{3,2,1,0:T(8,128)(2,1)}, bf16[1,5,128,256]{3,2,1,0:T(8,128)(2,1)}, u32[]{:S(2)}, u32[]{:S(2)}) collective-permute-start(bf16[1,5,128,256]{3,2,1,0:T(8,128)(2,1)} %collective-permute-done.15.refs_5_), channel_id=1, source_target_pairs={{0,8},{4,12},{8,0},{12,4},{1,9},{5,13},{9,1},{13,5},{2,10},{6,14},... | collective-permute-start | bytes 983048 | tf_op jit(solution)/shard_map/ppermute | solution.py:24
  64.1 24.1 %collective-permute-start.9 = (bf16[1,5,128,256]{3,2,1,0:T(8,128)(2,1)}, bf16[1,5,128,256]{3,2,1,0:T(8,128)(2,1)}, u32[]{:S(2)}, u32[]{:S(2)}) collective-permute-start(bf16[1,5,128,256]{3,2,1,0:T(8,128)(2,1)} %collective-permute-done.2.refs_4_), channel_id=1, source_target_pairs={{0,4},{4,0},{8,12},{12,8},{1,5},{5,1},{9,13},{13,9},{2,6},{6,2},{1... | collective-permute-start | bytes 983048 | tf_op jit(solution)/shard_map/ppermute | solution.py:24
  70.1 20.6 %collective-permute-start.21 = (bf16[1,5,128,256]{3,2,1,0:T(8,128)(2,1)}, bf16[1,5,128,256]{3,2,1,0:T(8,128)(2,1)}, u32[]{:S(2)}, u32[]{:S(2)}) collective-permute-start(bf16[1,5,128,256]{3,2,1,0:T(8,128)(2,1)} %collective-permute-done.15.refs_5_), channel_id=1, source_target_pairs={{0,4},{4,0},{8,12},{12,8},{1,5},{5,1},{9,13},{13,9},{2,6},{6,2},{1... | collective-permute-start | bytes 983048 | tf_op jit(solution)/shard_map/ppermute | solution.py:24
  70.1 20.0 %collective-permute-start.11 = (bf16[1,5,128,256]{3,2,1,0:T(8,128)(2,1)}, bf16[1,5,128,256]{3,2,1,0:T(8,128)(2,1)}, u32[]{:S(2)}, u32[]{:S(2)}) collective-permute-start(bf16[1,5,128,256]{3,2,1,0:T(8,128)(2,1)} %collective-permute-done.4.refs_6_), channel_id=1, source_target_pairs={{0,4},{4,0},{8,12},{12,8},{1,5},{5,1},{9,13},{13,9},{2,6},{6,2},{1... | collective-permute-start | bytes 983048 | tf_op jit(solution)/shard_map/ppermute | solution.py:24
  75.2 14.9 %collective-permute-start.10 = (bf16[1,5,128,256]{3,2,1,0:T(8,128)(2,1)}, bf16[1,5,128,256]{3,2,1,0:T(8,128)(2,1)}, u32[]{:S(2)}, u32[]{:S(2)}) collective-permute-start(bf16[1,5,128,256]{3,2,1,0:T(8,128)(2,1)} %collective-permute-done.3.refs_5_), channel_id=1, source_target_pairs={{0,4},{4,0},{8,12},{12,8},{1,5},{5,1},{9,13},{13,9},{2,6},{6,2},{1... | collective-permute-start | bytes 983048 | tf_op jit(solution)/shard_map/ppermute | solution.py:24
  77.0 25.0 %all-to-all-start = ((bf16[16,2,24,256]{3,2,1,0:T(8,128)(2,1)}), bf16[16,2,24,256]{3,2,1,0:T(8,128)(2,1)S(1)}, u32[]{:S(2)}, u32[]{:S(2)}) async-start(bf16[16,2,24,256]{3,2,1,0:T(8,128)(2,1)} %bitcast.9), calls=%async_computation | async-start | bytes 786432 | tf_op jit(solution)/shard_map/all_to_all | solution.py:305
  88.2 10.1 %collective-permute-start.28 = (bf16[1,3,128,256]{3,2,1,0:T(8,128)(2,1)}, bf16[1,3,128,256]{3,2,1,0:T(8,128)(2,1)S(1)}, u32[]{:S(2)}, u32[]{:S(2)}) collective-permute-start(bf16[1,3,128,256]{3,2,1,0:T(8,128)(2,1)} %copy-done.14), channel_id=1, source_target_pairs={{0,8},{4,12},{8,0},{12,4},{1,9},{5,13},{9,1},{13,5},{2,10},{6,14},... | collective-permute-start | bytes 589832 | tf_op jit(solution)/shard_map/ppermute | solution.py:24
  90.1 10.6 %collective-permute-start.12 = (bf16[1,5,128,256]{3,2,1,0:T(8,128)(2,1)}, bf16[1,5,128,256]{3,2,1,0:T(8,128)(2,1)S(1)}, u32[]{:S(2)}, u32[]{:S(2)}) collective-permute-start(bf16[1,5,128,256]{3,2,1,0:T(8,128)(2,1)} %collective-permute-done.5.refs_7_), channel_id=1, source_target_pairs={{0,4},{4,0},{8,12},{12,8},{1,5},{5,1},{9,13},{13,9},{2,6},{6,2},{1... | collective-permute-start | bytes 983048 | tf_op jit(solution)/shard_map/ppermute | solution.py:24
  90.1 24.7 %collective-permute-start.20 = (bf16[1,5,256,256]{3,2,1,0:T(8,128)(2,1)S(1)}, bf16[1,5,256,256]{3,2,1,0:T(8,128)(2,1)}, u32[]{:S(2)}, u32[]{:S(2)}) collective-permute-start(bf16[1,5,256,256]{3,2,1,0:T(8,128)(2,1)S(1)} %collective-permute-done.14.refs_4_), channel_id=1, source_target_pairs={{0,4},{4,0},{8,12},{12,8},{1,5},{5,1},{9,13},{13,9},{2,6},{6,2},{1... | collective-permute-start | bytes 1966088 | tf_op jit(solution)/shard_map/ppermute | solution.py:24
  90.6 11.2 %collective-permute-start.18 = (bf16[1,5,128,256]{3,2,1,0:T(8,128)(2,1)}, bf16[1,5,128,256]{3,2,1,0:T(8,128)(2,1)}, u32[]{:S(2)}, u32[]{:S(2)}) collective-permute-start(bf16[1,5,128,256]{3,2,1,0:T(8,128)(2,1)} %collective-permute-done.16.refs_6_), channel_id=1, source_target_pairs={{0,16},{16,0},{1,17},{17,1},{2,18},{18,2},{3,19},{19,3},{4,20},{20... | collective-permute-start | bytes 983048 | tf_op jit(solution)/shard_map/ppermute | solution.py:24
  94.6 16.6 %collective-permute-start.40 = (bf16[1,3,256,256]{3,2,1,0:T(8,128)(2,1)}, bf16[1,3,256,256]{3,2,1,0:T(8,128)(2,1)}, u32[]{:S(2)}, u32[]{:S(2)}) collective-permute-start(bf16[1,3,256,256]{3,2,1,0:T(8,128)(2,1)} %get-tuple-element.74.refs_4_), channel_id=1, source_target_pairs={{0,8},{4,12},{8,0},{12,4},{1,9},{5,13},{9,1},{13,5},{2,10},{6,14},... | collective-permute-start | bytes 1179656 | tf_op jit(solution)/shard_map/ppermute | solution.py:24
  100.6 13.1 %collective-permute-start.22 = (bf16[1,5,128,256]{3,2,1,0:T(8,128)(2,1)}, bf16[1,5,128,256]{3,2,1,0:T(8,128)(2,1)}, u32[]{:S(2)}, u32[]{:S(2)}) collective-permute-start(bf16[1,5,128,256]{3,2,1,0:T(8,128)(2,1)} %collective-permute-done.16.refs_6_), channel_id=1, source_target_pairs={{0,4},{4,0},{8,12},{12,8},{1,5},{5,1},{9,13},{13,9},{2,6},{6,2},{1... | collective-permute-start | bytes 983048 | tf_op jit(solution)/shard_map/ppermute | solution.py:24
  101.5 13.4 %collective-permute-start.23 = (bf16[1,5,128,256]{3,2,1,0:T(8,128)(2,1)}, bf16[1,5,128,256]{3,2,1,0:T(8,128)(2,1)}, u32[]{:S(2)}, u32[]{:S(2)}) collective-permute-start(bf16[1,5,128,256]{3,2,1,0:T(8,128)(2,1)} %collective-permute-done.17.refs_7_), channel_id=1, source_target_pairs={{0,4},{4,0},{8,12},{12,8},{1,5},{5,1},{9,13},{13,9},{2,6},{6,2},{1... | collective-permute-start | bytes 983048 | tf_op jit(solution)/shard_map/ppermute | solution.py:24
  101.8 18.4 %collective-permute-start.24 = (bf16[1,5,128,256]{3,2,1,0:T(8,128)(2,1)}, bf16[1,5,128,256]{3,2,1,0:T(8,128)(2,1)}, u32[]{:S(2)}, u32[]{:S(2)}) collective-permute-start(bf16[1,5,128,256]{3,2,1,0:T(8,128)(2,1)} %collective-permute-done.18.refs_8_), channel_id=1, source_target_pairs={{0,4},{4,0},{8,12},{12,8},{1,5},{5,1},{9,13},{13,9},{2,6},{6,2},{1... | collective-permute-start | bytes 983048 | tf_op jit(solution)/shard_map/ppermute | solution.py:24
  113.7 10.6 %collective-permute-start.31 = (bf16[1,3,128,256]{3,2,1,0:T(8,128)(2,1)S(1)}, bf16[1,3,128,256]{3,2,1,0:T(8,128)(2,1)S(1)}, u32[]{:S(2)}, u32[]{:S(2)}) collective-permute-start(bf16[1,3,128,256]{3,2,1,0:T(8,128)(2,1)S(1)} %copy-done.19), channel_id=1, source_target_pairs={{0,16},{16,0},{1,17},{17,1},{2,18},{18,2},{3,19},{19,3},{4,20},{20... | collective-permute-start | bytes 589832 | tf_op jit(solution)/shard_map/ppermute | solution.py:24
  114.9 10.0 %collective-permute-start.36 = (bf16[1,3,128,256]{3,2,1,0:T(8,128)(2,1)S(1)}, bf16[1,3,128,256]{3,2,1,0:T(8,128)(2,1)S(1)}, u32[]{:S(2)}, u32[]{:S(2)}) collective-permute-start(bf16[1,3,128,256]{3,2,1,0:T(8,128)(2,1)S(1)} %copy-done.17), channel_id=1, source_target_pairs={{0,4},{4,0},{8,12},{12,8},{1,5},{5,1},{9,13},{13,9},{2,6},{6,2},{1... | collective-permute-start | bytes 589832 | tf_op jit(solution)/shard_map/ppermute | solution.py:24
  124.9 10.8 %collective-permute-start.45 = (bf16[1,3,256,256]{3,2,1,0:T(8,128)(2,1)S(1)}, bf16[1,3,256,256]{3,2,1,0:T(8,128)(2,1)S(1)}, u32[]{:S(2)}, u32[]{:S(2)}) collective-permute-start(bf16[1,3,256,256]{3,2,1,0:T(8,128)(2,1)S(1)} %copy-done.3), channel_id=1, source_target_pairs={{0,4},{4,0},{8,12},{12,8},{1,5},{5,1},{9,13},{13,9},{2,6},{6,2},{1... | collective-permute-start | bytes 1179656 | tf_op jit(solution)/shard_map/ppermute | solution.py:24
  128.1 12.1 %collective-permute-start.46 = (bf16[1,3,256,256]{3,2,1,0:T(8,128)(2,1)}, bf16[1,3,256,256]{3,2,1,0:T(8,128)(2,1)S(1)}, u32[]{:S(2)}, u32[]{:S(2)}) collective-permute-start(bf16[1,3,256,256]{3,2,1,0:T(8,128)(2,1)} %collective-permute-done.40.refs_5_), channel_id=1, source_target_pairs={{0,4},{4,0},{8,12},{12,8},{1,5},{5,1},{9,13},{13,9},{2,6},{6,2},{1... | collective-permute-start | bytes 1179656 | tf_op jit(solution)/shard_map/ppermute | solution.py:24
  129.0 10.6 %collective-permute-start.43 = (bf16[1,3,128,256]{3,2,1,0:T(8,128)(2,1)S(1)}, bf16[1,3,128,256]{3,2,1,0:T(8,128)(2,1)S(1)}, u32[]{:S(2)}, u32[]{:S(2)}) collective-permute-start(bf16[1,3,128,256]{3,2,1,0:T(8,128)(2,1)S(1)} %copy-done.23), channel_id=1, source_target_pairs={{0,16},{16,0},{1,17},{17,1},{2,18},{18,2},{3,19},{19,3},{4,20},{20... | collective-permute-start | bytes 589832 | tf_op jit(solution)/shard_map/ppermute | solution.py:24
  159.6 11.1 %collective-permute-start.54 = (bf16[96,1024]{1,0:T(8,128)(2,1)S(1)}, bf16[96,1024]{1,0:T(8,128)(2,1)S(1)}, u32[]{:S(2)}, u32[]{:S(2)}) collective-permute-start(bf16[96,1024]{1,0:T(8,128)(2,1)S(1)} %get-tuple-element.94.refs_6_), channel_id=1, source_target_pairs={{0,1},{1,0},{2,3},{3,2},{4,5},{5,4},{6,7},{7,6},{8,9},{9,8},{10,11... | collective-permute-start | bytes 589832 | tf_op jit(solution)/shard_map/ppermute | solution.py:24
  (48 other events, 394.9 us)

commit v4 on v3

--- a/solution.py
+++ b/solution.py
@@ -8,6 +8,7 @@
 BOTH = ("tm", "chan")
 HALVED = (0, 2)
 VMEM_LIMIT = 20 * 1024 * 1024
+DEPTHS = {"chan": 1, "tm": 2, "groups": 2}
 
 
 def dot(left, right):
@@ -93,12 +94,12 @@
 
 
 class Links:
-    def __init__(self, depth):
-        self.depth, self.sent = depth, {}
+    def __init__(self, depths):
+        self.depths, self.sent = depths, {}
 
     def move(self, piece, axis, bit, kind=None, after=()):
-        sent = self.sent.setdefault(axis, [])
-        waits = [*after, *sent[-self.depth :][:1]] if len(sent) >= self.depth else [*after]
+        sent, depth = self.sent.setdefault(axis, []), self.depths[axis]
+        waits = [*after, *(sent[-depth:][:1] if len(sent) >= depth else [])]
         if waits:
             piece.array = lax.optimization_barrier((piece.array, *waits))[0]
         moved = piece.moved(axis, bit, kind)
@@ -106,54 +107,60 @@
         return moved
 
 
-def spread(packs, taps_of, halved_layers, links):
-    limit = 16 if lax.axis_size("tm") <= 4 and lax.axis_size("chan") <= 4 else 1
-    high = bits_of("tm", 2)
-    layers = range(len(taps_of))
-    halves = [Piece(packs[2 * n], [(0, 0)], "mine") for n in layers]
-    full = [[Piece(packs[2 * n + 1], [(0, 0)], "full")] for n in layers]
-    zs = [[] for _ in layers]
-    ys = [[] for _ in layers]
-    crossed = [[] for _ in layers]
-    others = [[] for _ in layers]
-
-    def along_chan(n):
+class Weights:
+    def __init__(self, packs, taps_of, halved, depths):
+        self.limit = 16 if lax.axis_size("tm") <= 4 and lax.axis_size("chan") <= 4 else 1
+        self.links, self.halved, self.high = Links(depths), halved, bits_of("tm", 2)
+        count = len(taps_of)
+        self.halves = [Piece(packs[2 * n], [(0, 0)], "mine") for n in range(count)]
+        self.full = [[Piece(packs[2 * n + 1], [(0, 0)], "full")] for n in range(count)]
+        self.zs, self.ys, self.crossed, self.others = ([[] for _ in range(count)] for _ in range(4))
+
+    def along_chan(self, n, after=()):
         for bit in bits_of("chan", 2):
-            zs[n] = zs[n] + [links.move(p, "chan", bit) for p in [halves[n]] + zs[n]]
-
-    def own_along_tm(n):
-        for bit in high:
-            if n in halved_layers:
-                ys[n] = ys[n] + [links.move(p, "tm", bit) for p in [halves[n]] + ys[n]]
+            sources = [self.halves[n]] + self.zs[n]
+            self.zs[n] = self.zs[n] + [self.links.move(p, "chan", bit, None, after) for p in sources]
+
+    def own_along_tm(self, n, after=()):
+        for bit in self.high:
+            if n in self.halved:
+                sources = [self.halves[n]] + self.ys[n]
+                self.ys[n] = self.ys[n] + [self.links.move(p, "tm", bit, None, after) for p in sources]
             else:
-                full[n] = full[n] + [links.move(p, "tm", bit) for p in full[n]]
-
-    def others_along_tm(n):
-        for bit in high:
-            source = merged(zs[n] + crossed[n], limit)
-            crossed[n] = crossed[n] + [links.move(p, "tm", bit) for p in source]
-
-    def along_groups(n, pieces):
-        others[n] = others[n] + [links.move(p, "groups", 1, "other") for p in merged(pieces, limit)]
-
-    steps = [(along_chan, 0), (own_along_tm, 0), (own_along_tm, 1), (along_chan, 1)]
-    for step, n in steps:
-        step(n)
-    for n in layers:
-        along_groups(n, ys[n])
-        others_along_tm(n)
-        along_groups(n, zs[n])
-        if n + 2 < len(taps_of):
-            along_chan(n + 2)
-            own_along_tm(n + 2)
-        along_groups(n, crossed[n])
-    result = []
-    for n in layers:
-        pieces = merged(full[n] + ys[n] + zs[n] + crossed[n] + others[n], limit)
+                moved = [self.links.move(p, "tm", bit, None, after) for p in self.full[n]]
+                self.full[n] = self.full[n] + moved
+
+    def others_along_tm(self, n, after=()):
+        for bit in self.high:
+            sources = merged(self.zs[n] + self.crossed[n], self.limit)
+            self.crossed[n] = self.crossed[n] + [
+                self.links.move(p, "tm", bit, None, after) for p in sources
+            ]
+
+    def along_groups(self, n, pieces, after=()):
+        for p in merged(pieces, self.limit):
+            self.others[n].append(self.links.move(p, "groups", 1, "other", after))
+
+    def begin(self, after):
+        self.along_chan(0)
+        self.own_along_tm(0)
+        self.own_along_tm(1)
+        self.along_chan(1, after)
+
+    def layer(self, n, after=()):
+        self.along_groups(n, self.ys[n])
+        self.others_along_tm(n)
+        self.along_groups(n, self.zs[n])
+        if n + 2 < len(self.full):
+            self.along_chan(n + 2)
+            self.own_along_tm(n + 2, after)
+        self.along_groups(n, self.crossed[n])
+        pieces = merged(
+            self.full[n] + self.ys[n] + self.zs[n] + self.crossed[n] + self.others[n], self.limit
+        )
         if lax.axis_size("tm") > 1:
             pieces = pieces + [p.moved("tm", 1) for p in pieces]
-        result.append(pieces)
-    return result
+        return pieces
 
 
 class Blocks:
@@ -294,7 +301,7 @@
     taps_of = [2 if 2**layer < tm_count else 1 for layer in range(layers)]
     mix_source = mix_weight if square else mix_weight.transpose(0, 2, 1)
     sources = (filter_weight, gate_weight, mix_source)
-    pieces_of = spread(packed(sources, taps_of), taps_of, HALVED, Links(2))
+    weights = Weights(packed(sources, taps_of), taps_of, HALVED, DEPTHS)
 
     def swap(values):
         return exchange(values, "chan", 1)
@@ -303,6 +310,7 @@
     sent = both.reshape(2, peers // 2, span, nb).transpose(1, 0, 2, 3)
     sent = jnp.broadcast_to(sent[:, None], (peers // 2, 2, 2, span, nb)).reshape(peers, 2, span, nb)
     got = lax.all_to_all(sent, BOTH, split_axis=0, concat_axis=0, tiled=True)
+    weights.begin([got])
     if not square:
         got = got.reshape(tm_count, chan_count, 2, span, nb).transpose(2, 0, 3, 1, 4)
         got = flipped(got.reshape(2, tm_count, span, width), tm_index, tm_count, kb)
@@ -318,7 +326,6 @@
             target[:, pl.ds(i * kb, kb)] = jnp.concatenate(parts, axis=0).astype(bf16)
 
     vmem = pl.BlockSpec(memory_space=pltpu.VMEM)
-    anywhere = pl.BlockSpec(memory_space=pl.ANY)
     act = jax.ShapeDtypeStruct((m, width), bf16)
     fac = jax.ShapeDtypeStruct((panels, m, nb), f32)
     acc = [pltpu.VMEM((m, width), f32)]
@@ -326,7 +333,7 @@
     def layer_call(layer, body, arrays, held, outs, scratch, passes, name):
         taps, mats = taps_of[layer], 2 * taps_of[layer] + 1
         shift = 2**layer * span
-        pieces = pieces_of[layer] if held is None else []
+        pieces = weights.layer(layer, arrays[1:2]) if held is None else []
         copies = sum(len(p.keys) for p in pieces)
         plan = [(p.keys, p.kind) for p in pieces]
         shape = (panels * tm_count, mats, kb, nb)
@@ -345,11 +352,11 @@
                 body(blocks, shift, ins, refs[1 : 1 + len(outs)], refs[1 + len(outs) :])
 
         filling = held is None
-        weights = [p.array for p in pieces] if filling else [held]
+        blocks_in = [p.array for p in pieces] if filling else [held]
         return pl.pallas_call(
             kernel,
             out_shape=[*outs, *([jax.ShapeDtypeStruct(shape, bf16)] if filling else [])],
-            in_specs=[vmem] * count + [anywhere if filling else vmem] * len(weights),
+            in_specs=[vmem] * count + [pl.BlockSpec(memory_space=pltpu.HBM if filling else pltpu.VMEM)] * len(blocks_in),
             out_specs=[vmem] * (len(outs) + filling),
             scratch_shapes=[*scratch, *([pltpu.SemaphoreType.DMA((copies,))] if filling else [])],
             compiler_params=pltpu.CompilerParams(vmem_limit_bytes=VMEM_LIMIT),
@@ -357,7 +364,7 @@
                 flops=2 * m * elems * passes, bytes_accessed=2 * elems, transcendentals=2 * m * nb
             ),
             name=name,
-        )(*arrays, *weights)
+        )(*arrays, *blocks_in)
 
     def first_body(blocks, shift, ins, outs, scratch):
         sig, grad, part, fac_f, fac_g = outs

time: 193 us -> 178 us (0.922)
  starting transfers between devices: 51.2 us -> 39.4 us
  local copies, waits for them, and re-layouts: 11.3 us -> 1.91 us
  waiting for transfers between devices: 90.2 us -> 95.6 us
    unnamed x48 -> x8, local copies, waits for them, and re-layouts: 10.5 us -> 1.1 us
    all_to_all x1, starting transfers between devices: 9.61 us -> 3.55 us  [local(): got = lax.all_to_all(sent, BOTH, split_axis=0, concat_axis=0, tiled=True)]
    ppermute x55, starting transfers between devices: 41.6 us -> 35.9 us  [exchange(): lax.ppermute(values, axis, [(i, i ^ bit) for i in range(lax.axis_size(axi...]
    ppermute x55, waiting for transfers between devices: 90.2 us -> 95.6 us  [exchange(): lax.ppermute(values, axis, [(i, i ^ bit) for i in range(lax.axis_size(axi...]
  transfers between devices with their start and end apart: 56 -> 56, of which waited for: 21 -> 26; matrix products, arithmetic and copies ran while one was open for 1% -> 1% of each run, Pallas kernels for 6% -> 6%
where the time goes in v4:
time: 178 us; the launch traced here: 177 us
  waiting for transfers between devices  95.6 us (54%)
  starting transfers between devices  39.4 us (22%)
  Pallas kernels  22.1 us (12%)
  blocking collectives  15 us (8%)
  other arithmetic  2.3 us (1%)
  local copies, waits for them, and re-layouts  1.91 us (1%)
    ppermute x55, waiting for transfers between devices, exchange(): lax.ppermute(values, axis, [(i, i ^ bit) for i in range(lax.axis_size(axi...  95.6 us
    ppermute x55, starting transfers between devices, exchange(): lax.ppermute(values, axis, [(i, i ^ bit) for i in range(lax.axis_size(axi...  35.9 us
    pallas_call x7, Pallas kernels, layer_call(): pl.pallas_call(kernel, out_shape=[*outs, *([jax.ShapeDtypeStruct(shape, b...  18.3 us
    all_to_all x1, blocking collectives, local(): back = lax.all_to_all(back, BOTH, split_axis=0, concat_axis=0, tiled=True)  15 us
    pallas_call x1, Pallas kernels, packed(): pl.pallas_call(kernel, out_shape=[jax.ShapeDtypeStruct(shape, jnp.bfloat1...  3.77 us
  transfers between devices with their start and end apart: 56, of which 26 were waited for; matrix products, arithmetic and copies ran while one was open for 1% of the time, Pallas kernels for 6%

profile of v4, /device:TPU:0, one launch (start us, length us, event | category | flops | bytes accessed | tf_op | source)
XLA Modules:
  0.0 177.2 jit_solution(4193360369465908908)
XLA Ops:
  0.6 3.8 %pack.1 = (bf16[1,5,128,256]{3,2,1,0:T(8,128)(2,1)}, bf16[1,5,256,256]{3,2,1,0:T(8,128)(2,1)}, bf16[1,5,128,256]{3,2,1,0:T(8,128)(2,1)}, bf16[1,5,256,256]{3,2,1...) custom-call(bf16[4,2,256,256]{3,2,1,0:T(8,128)(2,1)} %refs_0_.1, ...), custom_call_target="tpu_custom_call" | custom-call | tf_op jit(solution)/shard_map/pack/pallas_call | solution.py:86
  4.4 3.0 %collective-permute-start = (bf16[1,5,128,256]{3,2,1,0:T(8,128)(2,1)}, bf16[1,5,128,256]{3,2,1,0:T(8,128)(2,1)S(1)}, u32[]{:S(2)}, u32[]{:S(2)}) collective-permute-start(bf16[1,5,128,256]{3,2,1,0:T(8,128)(2,1)} %get-tuple-element.51), channel_id=1, source_target_pairs={{0,8},{4,12},{8,0},{12,4},{1,9},{5,13},{9,1},{13,5},{2,10},{6,14},... | collective-permute-start | bytes 983048 | tf_op jit(solution)/shard_map/ppermute | solution.py:25
  7.5 2.6 %collective-permute-start.1 = (bf16[1,5,128,256]{3,2,1,0:T(8,128)(2,1)}, bf16[1,5,128,256]{3,2,1,0:T(8,128)(2,1)}, u32[]{:S(2)}, u32[]{:S(2)}) collective-permute-start(bf16[1,5,128,256]{3,2,1,0:T(8,128)(2,1)} %get-tuple-element.51), channel_id=1, source_target_pairs={{0,2},{1,3},{2,0},{3,1},{4,6},{5,7},{6,4},{7,5},{8,10},{9,11},{10,... | collective-permute-start | bytes 983048 | tf_op jit(solution)/shard_map/ppermute | solution.py:25
  11.8 3.6 %all-to-all-start = ((bf16[16,2,24,256]{3,2,1,0:T(8,128)(2,1)}), bf16[16,2,24,256]{3,2,1,0:T(8,128)(2,1)S(1)}, u32[]{:S(2)}, u32[]{:S(2)}) async-start(bf16[16,2,24,256]{3,2,1,0:T(8,128)(2,1)} %bitcast.3), calls=%async_computation | async-start | bytes 786432 | tf_op jit(solution)/shard_map/all_to_all | solution.py:312
  15.7 14.6 %collective-permute-done.1.refs_3_ = bf16[1,5,128,256]{3,2,1,0:T(8,128)(2,1)} collective-permute-done((bf16[1,5,128,256]{3,2,1,0:T(8,128)(2,1)}, bf16[1,5,128,256]{3,2,1,0:T(8,128)(2,1)}, u32[]{:S(2)}, u32[]{:S(2)}) %collective-permute-start.1) | collective-permute-done | bytes 327712 | tf_op jit(solution)/shard_map/ppermute | solution.py:25
  30.8 1.6 collective-permute-start.3
  32.3 1.5 collective-permute-start.14
  34.4 6.6 %collective-permute-done.2.refs_4_ = bf16[1,5,128,256]{3,2,1,0:T(8,128)(2,1)} collective-permute-done((bf16[1,5,128,256]{3,2,1,0:T(8,128)(2,1)}, bf16[1,5,128,256]{3,2,1,0:T(8,128)(2,1)}, u32[]{:S(2)}, u32[]{:S(2)}) %collective-permute-start.2) | collective-permute-done | bytes 327712 | tf_op jit(solution)/shard_map/ppermute | solution.py:25
  41.5 3.5 %collective-permute-done.4.refs_6_ = bf16[1,5,128,256]{3,2,1,0:T(8,128)(2,1)} collective-permute-done((bf16[1,5,128,256]{3,2,1,0:T(8,128)(2,1)}, bf16[1,5,128,256]{3,2,1,0:T(8,128)(2,1)}, u32[]{:S(2)}, u32[]{:S(2)}) %collective-permute-start.4) | collective-permute-done | bytes 327712 | tf_op jit(solution)/shard_map/ppermute | solution.py:25
  45.1 1.5 collective-permute-start.5
  47.2 5.2 %collective-permute-done.14.refs_4_ = bf16[1,5,256,256]{3,2,1,0:T(8,128)(2,1)S(1)} collective-permute-done((bf16[1,5,256,256]{3,2,1,0:T(8,128)(2,1)}, bf16[1,5,256,256]{3,2,1,0:T(8,128)(2,1)S(1)}, u32[]{:S(2)}, u32[]{:S(2)}) %collective-permute-start.14) | collective-permute-done | bytes 655392 | tf_op jit(solution)/shard_map/ppermute | solution.py:25
  52.4 1.6 collective-permute-done.5.refs_7_
  54.0 8.2 %collective-permute-done.15.refs_5_ = bf16[1,5,128,256]{3,2,1,0:T(8,128)(2,1)S(1)} collective-permute-done((bf16[1,5,128,256]{3,2,1,0:T(8,128)(2,1)}, bf16[1,5,128,256]{3,2,1,0:T(8,128)(2,1)S(1)}, u32[]{:S(2)}, u32[]{:S(2)}) %collective-permute-start.15) | collective-permute-done | bytes 327712 | tf_op jit(solution)/shard_map/ppermute | solution.py:25
  62.9 6.8 %collective-permute-done.26.refs_4_ = bf16[1,3,128,256]{3,2,1,0:T(8,128)(2,1)S(1)} collective-permute-done((bf16[1,3,128,256]{3,2,1,0:T(8,128)(2,1)}, bf16[1,3,128,256]{3,2,1,0:T(8,128)(2,1)S(1)}, u32[]{:S(2)}, u32[]{:S(2)}) %collective-permute-start.26) | collective-permute-done | bytes 196640 | tf_op jit(solution)/shard_map/ppermute | solution.py:25
  71.2 2.8 %collective-permute-done.27.refs_5_ = bf16[1,3,128,256]{3,2,1,0:T(8,128)(2,1)S(1)} collective-permute-done((bf16[1,3,128,256]{3,2,1,0:T(8,128)(2,1)}, bf16[1,3,128,256]{3,2,1,0:T(8,128)(2,1)S(1)}, u32[]{:S(2)}, u32[]{:S(2)}) %collective-permute-start.27) | collective-permute-done | bytes 196640 | tf_op jit(solution)/shard_map/ppermute | solution.py:25
  75.2 3.9 %collective-permute-done.17.refs_7_ = bf16[1,5,128,256]{3,2,1,0:T(8,128)(2,1)S(1)} collective-permute-done((bf16[1,5,128,256]{3,2,1,0:T(8,128)(2,1)S(1)}, bf16[1,5,128,256]{3,2,1,0:T(8,128)(2,1)S(1)}, u32[]{:S(2)}, u32[]{:S(2)}) %collective-permute-start.17) | collective-permute-done | bytes 327712 | tf_op jit(solution)/shard_map/ppermute | solution.py:25
  80.2 3.0 %layer_first.1 = (bf16[96,1024]{1,0:T(8,128)(2,1)S(1)}, bf16[96,1024]{1,0:T(8,128)(2,1)S(1)}, bf16[96,1024]{1,0:T(8,128)(2,1)S(1)}, f32[2,96,256]{2,1,0:T(8,128)...) custom-call(bf16[16,2,24,256]{3,2,1,0:T(8,128)(2,1)S(1)} %all-to-all-done.refs_0_, ...), custom_call_target="tpu_custom_call" | custom-call | flops 503316480 | bytes 5242880 | tf_op jit(solution)/shard_map/layer_first/pallas_call | solution.py:356
  85.0 1.5 collective-permute-start.29
  89.5 3.2 %collective-permute-done.13.refs_2_ = bf16[96,1024]{1,0:T(8,128)(2,1)S(1)} collective-permute-done((bf16[96,1024]{1,0:T(8,128)(2,1)S(1)}, bf16[96,1024]{1,0:T(8,128)(2,1)S(1)}, u32[]{:S(2)}, u32[]{:S(2)}) %collective-permute-start.13) | collective-permute-done | bytes 196640 | tf_op jit(solution)/shard_map/ppermute | solution.py:25
  97.2 3.4 %collective-permute-done.40.refs_5_ = bf16[1,3,256,256]{3,2,1,0:T(8,128)(2,1)S(1)} collective-permute-done((bf16[1,3,256,256]{3,2,1,0:T(8,128)(2,1)S(1)}, bf16[1,3,256,256]{3,2,1,0:T(8,128)(2,1)S(1)}, u32[]{:S(2)}, u32[]{:S(2)}) %collective-permute-start.40) | collective-permute-done | bytes 393248 | tf_op jit(solution)/shard_map/ppermute | solution.py:25
  103.3 4.7 %collective-permute-done.42.refs_7_ = bf16[1,3,128,256]{3,2,1,0:T(8,128)(2,1)S(1)} collective-permute-done((bf16[1,3,128,256]{3,2,1,0:T(8,128)(2,1)S(1)}, bf16[1,3,128,256]{3,2,1,0:T(8,128)(2,1)S(1)}, u32[]{:S(2)}, u32[]{:S(2)}) %collective-permute-start.42) | collective-permute-done | bytes 196640 | tf_op jit(solution)/shard_map/ppermute | solution.py:25
  108.8 2.8 %layer_forward.2 = (bf16[96,1024]{1,0:T(8,128)(2,1)S(1)}, bf16[96,1024]{1,0:T(8,128)(2,1)S(1)}, f32[2,96,256]{2,1,0:T(8,128)S(1)}, f32[2,96,256]{2,1,0:T(8,128)S(1)}, bf16[8,5,256,256]{3,2,1,0:T(8,128)(2,1)S(1)}) custom-call(bf16[96,1024]{1,0:T(8,128)(2,1)S(1)} %get-tuple-element.55.refs_0_, bf16[96,1024]{1,0:T(8,128)(2,1)S(1)} %get-tuple-element.56.refs_1_, ...), custom_call_target="tpu_custom_call" | custom-call | flops 503316480 | bytes 5242880 | tf_op jit(solution)/shard_map/layer_forward/pallas_call | solution.py:356
  114.8 3.9 %collective-permute-done.25.refs_2_ = bf16[96,1024]{1,0:T(8,128)(2,1)S(1)} collective-permute-done((bf16[96,1024]{1,0:T(8,128)(2,1)S(1)}, bf16[96,1024]{1,0:T(8,128)(2,1)S(1)}, u32[]{:S(2)}, u32[]{:S(2)}) %collective-permute-start.25) | collective-permute-done | bytes 196640 | tf_op jit(solution)/shard_map/ppermute | solution.py:25
  118.7 2.7 %layer_forward.3 = (bf16[96,1024]{1,0:T(8,128)(2,1)S(1)}, bf16[96,1024]{1,0:T(8,128)(2,1)S(1)}, f32[2,96,256]{2,1,0:T(8,128)S(1)}, f32[2,96,256]{2,1,0:T(8,128)S(1)}, bf16[8,3,256,256]{3,2,1,0:T(8,128)(2,1)S(1)}) custom-call(bf16[96,1024]{1,0:T(8,128)(2,1)S(1)} %get-tuple-element.63.refs_0_, bf16[96,1024]{1,0:T(8,128)(2,1)S(1)} %get-tuple-element.64.refs_1_, ...), custom_call_target="tpu_custom_call" | custom-call | flops 301989888 | bytes 3145728 | tf_op jit(solution)/shard_map/layer_forward/pallas_call | solution.py:356
  125.0 5.9 %collective-permute-done.39.refs_2_ = bf16[96,1024]{1,0:T(8,128)(2,1)S(1)} collective-permute-done((bf16[96,1024]{1,0:T(8,128)(2,1)S(1)}, bf16[96,1024]{1,0:T(8,128)(2,1)S(1)}, u32[]{:S(2)}, u32[]{:S(2)}) %collective-permute-start.39) | collective-permute-done | bytes 196640 | tf_op jit(solution)/shard_map/ppermute | solution.py:25
  130.8 4.3 %layer_last.1 = (bf16[96,1024]{1,0:T(8,128)(2,1)S(1)}, bf16[96,1024]{1,0:T(8,128)(2,1)S(1)}, bf16[96,1024]{1,0:T(8,128)(2,1)S(1)}, bf16[8,3,256,256]{3,2,1,0:T(8,128)(2,1)}) custom-call(bf16[96,1024]{1,0:T(8,128)(2,1)S(1)} %get-tuple-element.73.refs_0_, bf16[96,1024]{1,0:T(8,128)(2,1)S(1)} %get-tuple-element.74.refs_1_, ...), custom_call_target="tpu_custom_call" | custom-call | flops 603979776 | bytes 3145728 | tf_op jit(solution)/shard_map/layer_last/pallas_call | solution.py:356
  136.3 5.4 %collective-permute-done.51.refs_2_ = bf16[96,1024]{1,0:T(8,128)(2,1)S(1)} collective-permute-done((bf16[96,1024]{1,0:T(8,128)(2,1)S(1)}, bf16[96,1024]{1,0:T(8,128)(2,1)S(1)}, u32[]{:S(2)}, u32[]{:S(2)}) %collective-permute-start.51) | collective-permute-done | bytes 196640 | tf_op jit(solution)/shard_map/ppermute | solution.py:25
  145.2 5.7 %collective-permute-done.52.refs_2_ = bf16[96,1024]{1,0:T(8,128)(2,1)S(1)} collective-permute-done((bf16[96,1024]{1,0:T(8,128)(2,1)S(1)}, bf16[96,1024]{1,0:T(8,128)(2,1)S(1)}, u32[]{:S(2)}, u32[]{:S(2)}) %collective-permute-start.52) | collective-permute-done | bytes 196640 | tf_op jit(solution)/shard_map/ppermute | solution.py:25
  150.9 2.0 %layer_backward.3 = (bf16[96,1024]{1,0:T(8,128)(2,1)S(1)}, bf16[96,1024]{1,0:T(8,128)(2,1)S(1)}) custom-call(bf16[96,1024]{1,0:T(8,128)(2,1)S(1)} %get-tuple-element.86.refs_0_, bf16[96,1024]{1,0:T(8,128)(2,1)S(1)} %get-tuple-element.87.refs_1_, bf16[96,1024]{1,0:T(8,128)(2,1)S(1)} %collective-permute-done.52.refs_2_, ...), custom_call_target="tpu_custom_call" | custom-call | flops 503316480 | bytes 5242880 | tf_op jit(solution)/shard_map/layer_backward/pallas_call | solution.py:356
  154.8 4.0 %collective-permute-done.53.refs_2_ = bf16[96,1024]{1,0:T(8,128)(2,1)S(1)} collective-permute-done((bf16[96,1024]{1,0:T(8,128)(2,1)S(1)}, bf16[96,1024]{1,0:T(8,128)(2,1)S(1)}, u32[]{:S(2)}, u32[]{:S(2)}) %collective-permute-start.53) | collective-permute-done | bytes 196640 | tf_op jit(solution)/shard_map/ppermute | solution.py:25
  158.7 2.1 %layer_final.1 = bf16[16,24,384]{2,1,0:T(8,128)(2,1)S(1)} custom-call(bf16[96,1024]{1,0:T(8,128)(2,1)S(1)} %get-tuple-element.91.refs_0_, bf16[96,1024]{1,0:T(8,128)(2,1)S(1)} %get-tuple-element.92.refs_1_, bf16[96,1024]{1,0:T(8,128)(2,1)S(1)} %collective-permute-done.53.refs_2_, f32[2,96,256]{2,1,0:T(8,128)S(1)} %get-tuple-element.93.refs_3_, ...), custom_call_target="tpu_custom_call" | custom-call | flops 503316480 | bytes 5242880 | tf_op jit(solution)/shard_map/layer_final/pallas_call | solution.py:356
  160.8 15.0 %all_to_all.10 = bf16[16,24,384]{2,1,0:T(8,128)(2,1)S(1)} all-to-all(bf16[16,24,384]{2,1,0:T(8,128)(2,1)S(1)} %layer_final.1), channel_id=1, replica_groups=mesh['groups'=2,'tm'=4,'chan'=4] {'tm','chan'}, dimensions={0} | all-to-all | bytes 589824 | tf_op jit(solution)/shard_map/all_to_all | solution.py:475
  (104 shorter events, 36.0 us)
Async XLA Ops:
  4.4 11.3 %collective-permute-start = (bf16[1,5,128,256]{3,2,1,0:T(8,128)(2,1)}, bf16[1,5,128,256]{3,2,1,0:T(8,128)(2,1)S(1)}, u32[]{:S(2)}, u32[]{:S(2)}) collective-permute-start(bf16[1,5,128,256]{3,2,1,0:T(8,128)(2,1)} %get-tuple-element.51), channel_id=1, source_target_pairs={{0,8},{4,12},{8,0},{12,4},{1,9},{5,13},{9,1},{13,5},{2,10},{6,14},... | collective-permute-start | bytes 983048 | tf_op jit(solution)/shard_map/ppermute | solution.py:25
  7.5 22.8 %collective-permute-start.1 = (bf16[1,5,128,256]{3,2,1,0:T(8,128)(2,1)}, bf16[1,5,128,256]{3,2,1,0:T(8,128)(2,1)}, u32[]{:S(2)}, u32[]{:S(2)}) collective-permute-start(bf16[1,5,128,256]{3,2,1,0:T(8,128)(2,1)} %get-tuple-element.51), channel_id=1, source_target_pairs={{0,2},{1,3},{2,0},{3,1},{4,6},{5,7},{6,4},{7,5},{8,10},{9,11},{10,... | collective-permute-start | bytes 983048 | tf_op jit(solution)/shard_map/ppermute | solution.py:25
  11.8 29.7 %all-to-all-start = ((bf16[16,2,24,256]{3,2,1,0:T(8,128)(2,1)}), bf16[16,2,24,256]{3,2,1,0:T(8,128)(2,1)S(1)}, u32[]{:S(2)}, u32[]{:S(2)}) async-start(bf16[16,2,24,256]{3,2,1,0:T(8,128)(2,1)} %bitcast.3), calls=%async_computation | async-start | bytes 786432 | tf_op jit(solution)/shard_map/all_to_all | solution.py:312
  15.4 18.5 %collective-permute-start.32 = (bf16[1,3,256,256]{3,2,1,0:T(8,128)(2,1)}, bf16[1,3,256,256]{3,2,1,0:T(8,128)(2,1)S(1)}, u32[]{:S(2)}, u32[]{:S(2)}) collective-permute-start(bf16[1,3,256,256]{3,2,1,0:T(8,128)(2,1)} %get-tuple-element.65.refs_3_), channel_id=1, source_target_pairs={{0,4},{4,0},{8,12},{12,8},{1,5},{5,1},{9,13},{13,9},{2,6},{6,2},{1... | collective-permute-start | bytes 1179656 | tf_op jit(solution)/shard_map/ppermute | solution.py:25
  30.3 10.7 %collective-permute-start.2 = (bf16[1,5,128,256]{3,2,1,0:T(8,128)(2,1)}, bf16[1,5,128,256]{3,2,1,0:T(8,128)(2,1)}, u32[]{:S(2)}, u32[]{:S(2)}) collective-permute-start(bf16[1,5,128,256]{3,2,1,0:T(8,128)(2,1)} %collective-permute-done.1.refs_3_), channel_id=1, source_target_pairs={{0,8},{4,12},{8,0},{12,4},{1,9},{5,13},{9,1},{13,5},{2,10},{6,14},... | collective-permute-start | bytes 983048 | tf_op jit(solution)/shard_map/ppermute | solution.py:25
  30.8 10.2 %collective-permute-start.3 = (bf16[1,5,128,256]{3,2,1,0:T(8,128)(2,1)S(1)}, bf16[1,5,128,256]{3,2,1,0:T(8,128)(2,1)}, u32[]{:S(2)}, u32[]{:S(2)}) collective-permute-start(bf16[1,5,128,256]{3,2,1,0:T(8,128)(2,1)S(1)} %collective-permute-done.refs_2_), channel_id=1, source_target_pairs={{0,16},{16,0},{1,17},{17,1},{2,18},{18,2},{3,19},{19,3},{4,20},{20... | collective-permute-start | bytes 983048 | tf_op jit(solution)/shard_map/ppermute | solution.py:25
  32.3 14.3 %collective-permute-start.6 = (bf16[1,5,256,256]{3,2,1,0:T(8,128)(2,1)}, bf16[1,5,256,256]{3,2,1,0:T(8,128)(2,1)S(1)}, u32[]{:S(2)}, u32[]{:S(2)}) collective-permute-start(bf16[1,5,256,256]{3,2,1,0:T(8,128)(2,1)} %get-tuple-element.50.refs_1_), channel_id=1, source_target_pairs={{0,4},{4,0},{8,12},{12,8},{1,5},{5,1},{9,13},{13,9},{2,6},{6,2},{1... | collective-permute-start | bytes 1966088 | tf_op jit(solution)/shard_map/ppermute | solution.py:25
  32.3 20.0 %collective-permute-start.14 = (bf16[1,5,256,256]{3,2,1,0:T(8,128)(2,1)}, bf16[1,5,256,256]{3,2,1,0:T(8,128)(2,1)S(1)}, u32[]{:S(2)}, u32[]{:S(2)}) collective-permute-start(bf16[1,5,256,256]{3,2,1,0:T(8,128)(2,1)} %get-tuple-element.57.refs_3_), channel_id=1, source_target_pairs={{0,8},{4,12},{8,0},{12,4},{1,9},{5,13},{9,1},{13,5},{2,10},{6,14},... | collective-permute-start | bytes 1966088 | tf_op jit(solution)/shard_map/ppermute | solution.py:25
  33.8 11.2 %collective-permute-start.4 = (bf16[1,5,128,256]{3,2,1,0:T(8,128)(2,1)}, bf16[1,5,128,256]{3,2,1,0:T(8,128)(2,1)}, u32[]{:S(2)}, u32[]{:S(2)}) collective-permute-start(bf16[1,5,128,256]{3,2,1,0:T(8,128)(2,1)} %collective-permute-done.1.refs_3_), channel_id=1, source_target_pairs={{0,16},{16,0},{1,17},{17,1},{2,18},{18,2},{3,19},{19,3},{4,20},{20... | collective-permute-start | bytes 983048 | tf_op jit(solution)/shard_map/ppermute | solution.py:25
  45.1 8.9 %collective-permute-start.5 = (bf16[1,5,128,256]{3,2,1,0:T(8,128)(2,1)}, bf16[1,5,128,256]{3,2,1,0:T(8,128)(2,1)S(1)}, u32[]{:S(2)}, u32[]{:S(2)}) collective-permute-start(bf16[1,5,128,256]{3,2,1,0:T(8,128)(2,1)} %collective-permute-done.2.refs_4_), channel_id=1, source_target_pairs={{0,16},{16,0},{1,17},{17,1},{2,18},{18,2},{3,19},{19,3},{4,20},{20... | collective-permute-start | bytes 983048 | tf_op jit(solution)/shard_map/ppermute | solution.py:25
  46.6 15.6 %collective-permute-start.15 = (bf16[1,5,128,256]{3,2,1,0:T(8,128)(2,1)}, bf16[1,5,128,256]{3,2,1,0:T(8,128)(2,1)S(1)}, u32[]{:S(2)}, u32[]{:S(2)}) collective-permute-start(bf16[1,5,128,256]{3,2,1,0:T(8,128)(2,1)} %get-tuple-element.59), channel_id=1, source_target_pairs={{0,2},{1,3},{2,0},{3,1},{4,6},{5,7},{6,4},{7,5},{8,10},{9,11},{10,... | collective-permute-start | bytes 983048 | tf_op jit(solution)/shard_map/ppermute | solution.py:25
  46.6 15.6 %collective-permute-start.9 = (bf16[1,5,128,256]{3,2,1,0:T(8,128)(2,1)}, bf16[1,5,128,256]{3,2,1,0:T(8,128)(2,1)S(1)}, u32[]{:S(2)}, u32[]{:S(2)}) collective-permute-start(bf16[1,5,128,256]{3,2,1,0:T(8,128)(2,1)} %collective-permute-done.2.refs_4_), channel_id=1, source_target_pairs={{0,4},{4,0},{8,12},{12,8},{1,5},{5,1},{9,13},{13,9},{2,6},{6,2},{1... | collective-permute-start | bytes 983048 | tf_op jit(solution)/shard_map/ppermute | solution.py:25
  46.7 16.0 %collective-permute-start.11 = (bf16[1,5,128,256]{3,2,1,0:T(8,128)(2,1)}, bf16[1,5,128,256]{3,2,1,0:T(8,128)(2,1)S(1)}, u32[]{:S(2)}, u32[]{:S(2)}) collective-permute-start(bf16[1,5,128,256]{3,2,1,0:T(8,128)(2,1)} %collective-permute-done.4.refs_6_), channel_id=1, source_target_pairs={{0,4},{4,0},{8,12},{12,8},{1,5},{5,1},{9,13},{13,9},{2,6},{6,2},{1... | collective-permute-start | bytes 983048 | tf_op jit(solution)/shard_map/ppermute | solution.py:25
  52.4 10.3 %collective-permute-start.10 = (bf16[1,5,128,256]{3,2,1,0:T(8,128)(2,1)}, bf16[1,5,128,256]{3,2,1,0:T(8,128)(2,1)S(1)}, u32[]{:S(2)}, u32[]{:S(2)}) collective-permute-start(bf16[1,5,128,256]{3,2,1,0:T(8,128)(2,1)} %collective-permute-done.3.refs_5_), channel_id=1, source_target_pairs={{0,4},{4,0},{8,12},{12,8},{1,5},{5,1},{9,13},{13,9},{2,6},{6,2},{1... | collective-permute-start | bytes 983048 | tf_op jit(solution)/shard_map/ppermute | solution.py:25
  54.0 31.0 %collective-permute-start.19 = (bf16[1,5,256,256]{3,2,1,0:T(8,128)(2,1)}, bf16[1,5,256,256]{3,2,1,0:T(8,128)(2,1)S(1)}, u32[]{:S(2)}, u32[]{:S(2)}) collective-permute-start(bf16[1,5,256,256]{3,2,1,0:T(8,128)(2,1)} %get-tuple-element.57.refs_3_), channel_id=1, source_target_pairs={{0,4},{4,0},{8,12},{12,8},{1,5},{5,1},{9,13},{13,9},{2,6},{6,2},{1... | collective-permute-start | bytes 1966088 | tf_op jit(solution)/shard_map/ppermute | solution.py:25
  62.2 24.3 %collective-permute-start.20 = (bf16[1,5,256,256]{3,2,1,0:T(8,128)(2,1)S(1)}, bf16[1,5,256,256]{3,2,1,0:T(8,128)(2,1)S(1)}, u32[]{:S(2)}, u32[]{:S(2)}) collective-permute-start(bf16[1,5,256,256]{3,2,1,0:T(8,128)(2,1)S(1)} %collective-permute-done.14.refs_4_), channel_id=1, source_target_pairs={{0,4},{4,0},{8,12},{12,8},{1,5},{5,1},{9,13},{13,9},{2,6},{6,2},{1... | collective-permute-start | bytes 1966088 | tf_op jit(solution)/shard_map/ppermute | solution.py:25
  62.6 11.4 %collective-permute-start.27 = (bf16[1,3,128,256]{3,2,1,0:T(8,128)(2,1)}, bf16[1,3,128,256]{3,2,1,0:T(8,128)(2,1)S(1)}, u32[]{:S(2)}, u32[]{:S(2)}) collective-permute-start(bf16[1,3,128,256]{3,2,1,0:T(8,128)(2,1)} %get-tuple-element.68), channel_id=1, source_target_pairs={{0,2},{1,3},{2,0},{3,1},{4,6},{5,7},{6,4},{7,5},{8,10},{9,11},{10,... | collective-permute-start | bytes 589832 | tf_op jit(solution)/shard_map/ppermute | solution.py:25
  62.7 12.5 %collective-permute-start.12 = (bf16[1,5,128,256]{3,2,1,0:T(8,128)(2,1)S(1)}, bf16[1,5,128,256]{3,2,1,0:T(8,128)(2,1)S(1)}, u32[]{:S(2)}, u32[]{:S(2)}) collective-permute-start(bf16[1,5,128,256]{3,2,1,0:T(8,128)(2,1)S(1)} %collective-permute-done.5.refs_7_), channel_id=1, source_target_pairs={{0,4},{4,0},{8,12},{12,8},{1,5},{5,1},{9,13},{13,9},{2,6},{6,2},{1... | collective-permute-start | bytes 983048 | tf_op jit(solution)/shard_map/ppermute | solution.py:25
  69.7 9.3 %collective-permute-start.17 = (bf16[1,5,128,256]{3,2,1,0:T(8,128)(2,1)S(1)}, bf16[1,5,128,256]{3,2,1,0:T(8,128)(2,1)S(1)}, u32[]{:S(2)}, u32[]{:S(2)}) collective-permute-start(bf16[1,5,128,256]{3,2,1,0:T(8,128)(2,1)S(1)} %collective-permute-done.15.refs_5_), channel_id=1, source_target_pairs={{0,16},{16,0},{1,17},{17,1},{2,18},{18,2},{3,19},{19,3},{4,20},{20... | collective-permute-start | bytes 983048 | tf_op jit(solution)/shard_map/ppermute | solution.py:25
  74.0 9.7 %collective-permute-start.16 = (bf16[1,5,128,256]{3,2,1,0:T(8,128)(2,1)S(1)}, bf16[1,5,128,256]{3,2,1,0:T(8,128)(2,1)S(1)}, u32[]{:S(2)}, u32[]{:S(2)}) collective-permute-start(bf16[1,5,128,256]{3,2,1,0:T(8,128)(2,1)S(1)} %collective-permute-done.15.refs_5_), channel_id=1, source_target_pairs={{0,8},{4,12},{8,0},{12,4},{1,9},{5,13},{9,1},{13,5},{2,10},{6,14},... | collective-permute-start | bytes 983048 | tf_op jit(solution)/shard_map/ppermute | solution.py:25
  75.1 11.9 %collective-permute-start.21 = (bf16[1,5,128,256]{3,2,1,0:T(8,128)(2,1)S(1)}, bf16[1,5,128,256]{3,2,1,0:T(8,128)(2,1)S(1)}, u32[]{:S(2)}, u32[]{:S(2)}) collective-permute-start(bf16[1,5,128,256]{3,2,1,0:T(8,128)(2,1)S(1)} %collective-permute-done.15.refs_5_), channel_id=1, source_target_pairs={{0,4},{4,0},{8,12},{12,8},{1,5},{5,1},{9,13},{13,9},{2,6},{6,2},{1... | collective-permute-start | bytes 983048 | tf_op jit(solution)/shard_map/ppermute | solution.py:25
  79.1 9.6 %collective-permute-start.41 = (bf16[1,3,128,256]{3,2,1,0:T(8,128)(2,1)}, bf16[1,3,128,256]{3,2,1,0:T(8,128)(2,1)S(1)}, u32[]{:S(2)}, u32[]{:S(2)}) collective-permute-start(bf16[1,3,128,256]{3,2,1,0:T(8,128)(2,1)} %get-tuple-element.78), channel_id=1, source_target_pairs={{0,2},{1,3},{2,0},{3,1},{4,6},{5,7},{6,4},{7,5},{8,10},{9,11},{10,... | collective-permute-start | bytes 589832 | tf_op jit(solution)/shard_map/ppermute | solution.py:25
  83.7 9.1 %collective-permute-start.13 = (bf16[96,1024]{1,0:T(8,128)(2,1)S(1)}, bf16[96,1024]{1,0:T(8,128)(2,1)S(1)}, u32[]{:S(2)}, u32[]{:S(2)}) collective-permute-start(bf16[96,1024]{1,0:T(8,128)(2,1)S(1)} %get-tuple-element.56.refs_1_), channel_id=1, source_target_pairs={{0,1},{1,0},{2,3},{3,2},{4,5},{5,4},{6,7},{7,6},{8,9},{9,8},{10,11... | collective-permute-start | bytes 589832 | tf_op jit(solution)/shard_map/ppermute | solution.py:25
  87.0 10.2 %collective-permute-start.18 = (bf16[1,5,128,256]{3,2,1,0:T(8,128)(2,1)S(1)}, bf16[1,5,128,256]{3,2,1,0:T(8,128)(2,1)S(1)}, u32[]{:S(2)}, u32[]{:S(2)}) collective-permute-start(bf16[1,5,128,256]{3,2,1,0:T(8,128)(2,1)S(1)} %collective-permute-done.16.refs_6_), channel_id=1, source_target_pairs={{0,16},{16,0},{1,17},{17,1},{2,18},{18,2},{3,19},{19,3},{4,20},{20... | collective-permute-start | bytes 983048 | tf_op jit(solution)/shard_map/ppermute | solution.py:25
  88.6 11.9 %collective-permute-start.40 = (bf16[1,3,256,256]{3,2,1,0:T(8,128)(2,1)S(1)}, bf16[1,3,256,256]{3,2,1,0:T(8,128)(2,1)S(1)}, u32[]{:S(2)}, u32[]{:S(2)}) collective-permute-start(bf16[1,3,256,256]{3,2,1,0:T(8,128)(2,1)S(1)} %copy-done.3), channel_id=1, source_target_pairs={{0,8},{4,12},{8,0},{12,4},{1,9},{5,13},{9,1},{13,5},{2,10},{6,14},... | collective-permute-start | bytes 1179656 | tf_op jit(solution)/shard_map/ppermute | solution.py:25
  97.2 11.3 %collective-permute-start.24 = (bf16[1,5,128,256]{3,2,1,0:T(8,128)(2,1)S(1)}, bf16[1,5,128,256]{3,2,1,0:T(8,128)(2,1)S(1)}, u32[]{:S(2)}, u32[]{:S(2)}) collective-permute-start(bf16[1,5,128,256]{3,2,1,0:T(8,128)(2,1)S(1)} %collective-permute-done.18.refs_8_), channel_id=1, source_target_pairs={{0,4},{4,0},{8,12},{12,8},{1,5},{5,1},{9,13},{13,9},{2,6},{6,2},{1... | collective-permute-start | bytes 983048 | tf_op jit(solution)/shard_map/ppermute | solution.py:25
  102.8 9.9 %collective-permute-start.38 = (bf16[1,3,128,256]{3,2,1,0:T(8,128)(2,1)S(1)}, bf16[1,3,128,256]{3,2,1,0:T(8,128)(2,1)S(1)}, u32[]{:S(2)}, u32[]{:S(2)}) collective-permute-start(bf16[1,3,128,256]{3,2,1,0:T(8,128)(2,1)S(1)} %collective-permute-done.31.refs_9_), channel_id=1, source_target_pairs={{0,4},{4,0},{8,12},{12,8},{1,5},{5,1},{9,13},{13,9},{2,6},{6,2},{1... | collective-permute-start | bytes 589832 | tf_op jit(solution)/shard_map/ppermute | solution.py:25
  108.0 13.4 %collective-permute-start.45 = (bf16[1,3,256,256]{3,2,1,0:T(8,128)(2,1)S(1)}, bf16[1,3,256,256]{3,2,1,0:T(8,128)(2,1)S(1)}, u32[]{:S(2)}, u32[]{:S(2)}) collective-permute-start(bf16[1,3,256,256]{3,2,1,0:T(8,128)(2,1)S(1)} %copy-done.3), channel_id=1, source_target_pairs={{0,4},{4,0},{8,12},{12,8},{1,5},{5,1},{9,13},{13,9},{2,6},{6,2},{1... | collective-permute-start | bytes 1179656 | tf_op jit(solution)/shard_map/ppermute | solution.py:25
  108.5 15.0 %collective-permute-start.46 = (bf16[1,3,256,256]{3,2,1,0:T(8,128)(2,1)S(1)}, bf16[1,3,256,256]{3,2,1,0:T(8,128)(2,1)S(1)}, u32[]{:S(2)}, u32[]{:S(2)}) collective-permute-start(bf16[1,3,256,256]{3,2,1,0:T(8,128)(2,1)S(1)} %collective-permute-done.40.refs_5_), channel_id=1, source_target_pairs={{0,4},{4,0},{8,12},{12,8},{1,5},{5,1},{9,13},{13,9},{2,6},{6,2},{1... | collective-permute-start | bytes 1179656 | tf_op jit(solution)/shard_map/ppermute | solution.py:25
  112.7 9.3 %collective-permute-start.44 = (bf16[1,3,128,256]{3,2,1,0:T(8,128)(2,1)S(1)}, bf16[1,3,128,256]{3,2,1,0:T(8,128)(2,1)S(1)}, u32[]{:S(2)}, u32[]{:S(2)}) collective-permute-start(bf16[1,3,128,256]{3,2,1,0:T(8,128)(2,1)S(1)} %collective-permute-done.42.refs_7_), channel_id=1, source_target_pairs={{0,16},{16,0},{1,17},{17,1},{2,18},{18,2},{3,19},{19,3},{4,20},{20... | collective-permute-start | bytes 589832 | tf_op jit(solution)/shard_map/ppermute | solution.py:25
  113.5 10.0 %collective-permute-start.43 = (bf16[1,3,128,256]{3,2,1,0:T(8,128)(2,1)S(1)}, bf16[1,3,128,256]{3,2,1,0:T(8,128)(2,1)S(1)}, u32[]{:S(2)}, u32[]{:S(2)}) collective-permute-start(bf16[1,3,128,256]{3,2,1,0:T(8,128)(2,1)S(1)} %collective-permute-done.41.refs_6_), channel_id=1, source_target_pairs={{0,16},{16,0},{1,17},{17,1},{2,18},{18,2},{3,19},{19,3},{4,20},{20... | collective-permute-start | bytes 589832 | tf_op jit(solution)/shard_map/ppermute | solution.py:25
  144.4 10.4 %collective-permute-start.54 = (bf16[96,1024]{1,0:T(8,128)(2,1)S(1)}, bf16[96,1024]{1,0:T(8,128)(2,1)S(1)}, u32[]{:S(2)}, u32[]{:S(2)}) collective-permute-start(bf16[96,1024]{1,0:T(8,128)(2,1)S(1)} %get-tuple-element.96.refs_6_), channel_id=1, source_target_pairs={{0,1},{1,0},{2,3},{3,2},{4,5},{5,4},{6,7},{7,6},{8,9},{9,8},{10,11... | collective-permute-start | bytes 589832 | tf_op jit(solution)/shard_map/ppermute | solution.py:25
  (28 other events, 366.0 us)

commit v5 on v4

--- a/solution.py
+++ b/solution.py
@@ -6,9 +6,8 @@
 from jax.sharding import PartitionSpec as P
 
 BOTH = ("tm", "chan")
-HALVED = (0, 2)
+HALVED = ()
 VMEM_LIMIT = 20 * 1024 * 1024
-DEPTHS = {"chan": 1, "tm": 2, "groups": 2}
 
 
 def dot(left, right):
@@ -51,33 +50,32 @@
     return joined
 
 
-def doubled(pieces, axis, bits, limit):
-    for bit in bits:
-        pieces = merged(pieces + [p.moved(axis, bit) for p in pieces], limit)
-    return pieces
-
-
-def packed(sources, taps_of):
+def packed(sources, taps_of, stages):
     kb, nb = sources[0].shape[2:]
-    shapes = []
-    for taps in taps_of:
-        shapes += [(1, 2 * taps + 1, kb // 2, nb), (1, 2 * taps + 1, kb, nb)]
+    places, shapes = [], []
+    for stage in stages:
+        for rows in (kb // 2, kb):
+            at = 0
+            for layer in stage:
+                places.append((len(shapes), layer, at))
+                at += 2 * taps_of[layer] + 1
+            shapes.append((1, at, rows, nb))
 
     def kernel(*refs):
         filt, gate, mix = refs[:3]
         outs, sems = refs[3:-1], refs[-1]
         copies = []
-        for n, out in enumerate(outs):
-            layer, taps, rows = n // 2, taps_of[n // 2], out.shape[2]
+        for number, (n, layer, at) in enumerate(places):
+            out, taps = outs[n], taps_of[layer]
+            rows = out.shape[2]
             start = lax.axis_index("groups") * rows if n % 2 == 0 else 0
             window = pl.ds(pl.multiple_of(start, rows), rows)
             for w, ref in enumerate((filt, gate)):
                 source = ref.at[layer, pl.ds(2 - taps, taps), window]
-                target = out.at[0, pl.ds(w * taps, taps)]
-                copies.append(pltpu.make_async_copy(source, target, sems.at[n, w]))
-            copies.append(
-                pltpu.make_async_copy(mix.at[layer, window], out.at[0, 2 * taps], sems.at[n, 2])
-            )
+                target = out.at[0, pl.ds(at + w * taps, taps)]
+                copies.append(pltpu.make_async_copy(source, target, sems.at[number, w]))
+            target = out.at[0, at + 2 * taps]
+            copies.append(pltpu.make_async_copy(mix.at[layer, window], target, sems.at[number, 2]))
         for copy in copies:
             copy.start()
         for copy in copies:
@@ -88,30 +86,22 @@
         out_shape=[jax.ShapeDtypeStruct(shape, jnp.bfloat16) for shape in shapes],
         in_specs=[pl.BlockSpec(memory_space=pl.ANY)] * 3,
         out_specs=[pl.BlockSpec(memory_space=pltpu.VMEM)] * len(shapes),
-        scratch_shapes=[pltpu.SemaphoreType.DMA((len(shapes), 3))],
+        scratch_shapes=[pltpu.SemaphoreType.DMA((len(places), 3))],
         name="pack",
     )(*sources)
 
 
-class Links:
-    def __init__(self, depths):
-        self.depths, self.sent = depths, {}
-
-    def move(self, piece, axis, bit, kind=None, after=()):
-        sent, depth = self.sent.setdefault(axis, []), self.depths[axis]
-        waits = [*after, *(sent[-depth:][:1] if len(sent) >= depth else [])]
-        if waits:
-            piece.array = lax.optimization_barrier((piece.array, *waits))[0]
-        moved = piece.moved(axis, bit, kind)
-        sent.append(moved.array)
-        return moved
+def ordered(piece, axis, bit, kind=None, after=()):
+    if after:
+        piece.array = lax.optimization_barrier((piece.array, *after))[0]
+    return piece.moved(axis, bit, kind)
 
 
 class Weights:
-    def __init__(self, packs, taps_of, halved, depths):
+    def __init__(self, packs, halved):
         self.limit = 16 if lax.axis_size("tm") <= 4 and lax.axis_size("chan") <= 4 else 1
-        self.links, self.halved, self.high = Links(depths), halved, bits_of("tm", 2)
-        count = len(taps_of)
+        self.halved, self.high = halved, bits_of("tm", 2)
+        count = len(packs) // 2
         self.halves = [Piece(packs[2 * n], [(0, 0)], "mine") for n in range(count)]
         self.full = [[Piece(packs[2 * n + 1], [(0, 0)], "full")] for n in range(count)]
         self.zs, self.ys, self.crossed, self.others = ([[] for _ in range(count)] for _ in range(4))
@@ -119,47 +109,65 @@
     def along_chan(self, n, after=()):
         for bit in bits_of("chan", 2):
             sources = [self.halves[n]] + self.zs[n]
-            self.zs[n] = self.zs[n] + [self.links.move(p, "chan", bit, None, after) for p in sources]
+            self.zs[n] = self.zs[n] + [ordered(p, "chan", bit, None, after) for p in sources]
 
     def own_along_tm(self, n, after=()):
         for bit in self.high:
             if n in self.halved:
                 sources = [self.halves[n]] + self.ys[n]
-                self.ys[n] = self.ys[n] + [self.links.move(p, "tm", bit, None, after) for p in sources]
+                self.ys[n] = self.ys[n] + [ordered(p, "tm", bit, None, after) for p in sources]
             else:
-                moved = [self.links.move(p, "tm", bit, None, after) for p in self.full[n]]
+                moved = [ordered(p, "tm", bit, None, after) for p in self.full[n]]
                 self.full[n] = self.full[n] + moved
 
     def others_along_tm(self, n, after=()):
         for bit in self.high:
             sources = merged(self.zs[n] + self.crossed[n], self.limit)
             self.crossed[n] = self.crossed[n] + [
-                self.links.move(p, "tm", bit, None, after) for p in sources
+                ordered(p, "tm", bit, None, after) for p in sources
             ]
 
     def along_groups(self, n, pieces, after=()):
         for p in merged(pieces, self.limit):
-            self.others[n].append(self.links.move(p, "groups", 1, "other", after))
-
-    def begin(self, after):
+            self.others[n].append(ordered(p, "groups", 1, "other", after))
+
+    def send(self, exchange_rows):
+        def arrays(*lists):
+            return [p.array for pieces in lists for p in pieces]
+
         self.along_chan(0)
         self.own_along_tm(0)
-        self.own_along_tm(1)
-        self.along_chan(1, after)
-
-    def layer(self, n, after=()):
-        self.along_groups(n, self.ys[n])
-        self.others_along_tm(n)
-        self.along_groups(n, self.zs[n])
-        if n + 2 < len(self.full):
-            self.along_chan(n + 2)
-            self.own_along_tm(n + 2, after)
-        self.along_groups(n, self.crossed[n])
-        pieces = merged(
-            self.full[n] + self.ys[n] + self.zs[n] + self.crossed[n] + self.others[n], self.limit
-        )
+        ended = arrays(self.zs[0], self.ys[0], self.full[0][1:])
+        self.others_along_tm(0, ended)
+        self.along_groups(0, self.zs[0] + self.ys[0], ended)
+        self.along_chan(1, ended)
+        ended = arrays(self.crossed[0], self.others[0], self.zs[1])
+        rows = exchange_rows(ended)
+        self.along_groups(0, self.crossed[0], ended)
+        self.others_along_tm(1, ended)
+        ended = arrays(self.others[0])
+        self.along_groups(1, self.zs[1], ended)
+        self.own_along_tm(1, ended)
+        ended = arrays(self.crossed[1])
+        rows = lax.optimization_barrier((rows, *ended))[0]
+        return rows, self.stage(0)
+
+    def own_halves(self, after):
+        self.along_groups(1, self.ys[1], after)
+
+    def middle(self):
+        return [p.array for p in self.ys[1] + self.full[1][1:] + self.others[1]]
+
+    def finish(self, before, after):
+        first = [p.array for p in self.ys[1] + self.full[1][1:] + self.others[1]]
+        self.along_groups(1, self.crossed[1], [*before, *first])
+        return self.stage(1, after)
+
+    def stage(self, n, after=()):
+        pieces = self.full[n] + self.ys[n] + self.zs[n] + self.crossed[n] + self.others[n]
+        pieces = merged(pieces, self.limit)
         if lax.axis_size("tm") > 1:
-            pieces = pieces + [p.moved("tm", 1) for p in pieces]
+            pieces = pieces + [ordered(p, "tm", 1, None, after) for p in pieces]
         return pieces
 
 
@@ -170,7 +178,7 @@
         self.kb = held.shape[2]
         self.copies = {}
 
-    def fill(self, refs, plan, sems):
+    def fill(self, refs, plan, at, sems):
         group = lax.axis_index("groups")
         half = self.kb // 2
         number = 0
@@ -181,7 +189,8 @@
                     which = group if kind == "mine" else 1 - group
                     window = pl.ds(pl.multiple_of(which * half, half), half)
                     target = self.held.at[dz // 2 * self.kblocks + dtm, :, window]
-                copy = pltpu.make_async_copy(ref.at[lead], target, sems.at[number])
+                mats = pl.ds(at, self.held.shape[1])
+                copy = pltpu.make_async_copy(ref.at[lead, mats], target, sems.at[number])
                 self.copies.setdefault((dz // 2, dtm), []).append(copy)
                 number += 1
         for panel in range(self.panels):
@@ -301,7 +310,9 @@
     taps_of = [2 if 2**layer < tm_count else 1 for layer in range(layers)]
     mix_source = mix_weight if square else mix_weight.transpose(0, 2, 1)
     sources = (filter_weight, gate_weight, mix_source)
-    weights = Weights(packed(sources, taps_of), taps_of, HALVED, DEPTHS)
+    early = (layers + 1) // 2
+    stages = [range(early), range(early, layers)]
+    weights = Weights(packed(sources, taps_of, stages), HALVED)
 
     def swap(values):
         return exchange(values, "chan", 1)
@@ -309,8 +320,13 @@
     both = jnp.pad(jnp.stack([records, cotangent]), ((0, 0), (0, padded - rows), (0, 0)))
     sent = both.reshape(2, peers // 2, span, nb).transpose(1, 0, 2, 3)
     sent = jnp.broadcast_to(sent[:, None], (peers // 2, 2, 2, span, nb)).reshape(peers, 2, span, nb)
-    got = lax.all_to_all(sent, BOTH, split_axis=0, concat_axis=0, tiled=True)
-    weights.begin([got])
+
+    def exchange_rows(after):
+        ready = lax.optimization_barrier((sent, *after))[0]
+        return lax.all_to_all(ready, BOTH, split_axis=0, concat_axis=0, tiled=True)
+
+    got, pieces = weights.send(exchange_rows)
+    pieces_of = [pieces]
     if not square:
         got = got.reshape(tm_count, chan_count, 2, span, nb).transpose(2, 0, 3, 1, 4)
         got = flipped(got.reshape(2, tm_count, span, width), tm_index, tm_count, kb)
@@ -333,7 +349,8 @@
     def layer_call(layer, body, arrays, held, outs, scratch, passes, name):
         taps, mats = taps_of[layer], 2 * taps_of[layer] + 1
         shift = 2**layer * span
-        pieces = weights.layer(layer, arrays[1:2]) if held is None else []
+        pieces = pieces_of[layer // early] if held is None else []
+        at = sum(2 * taps_of[n] + 1 for n in range(layer // early * early, layer))
         copies = sum(len(p.keys) for p in pieces)
         plan = [(p.keys, p.kind) for p in pieces]
         shape = (panels * tm_count, mats, kb, nb)
@@ -345,7 +362,7 @@
             if held is None:
                 piece_refs, refs = refs[: len(pieces)], refs[len(pieces) :]
                 blocks = Blocks(refs[len(outs)], panels, taps, square)
-                blocks.fill(piece_refs, plan, refs[-1])
+                blocks.fill(piece_refs, plan, at, refs[-1])
                 body(blocks, shift, ins, refs[: len(outs)], refs[len(outs) + 1 : -1])
             else:
                 blocks = Blocks(refs[0], panels, taps, square)
@@ -356,7 +373,7 @@
         return pl.pallas_call(
             kernel,
             out_shape=[*outs, *([jax.ShapeDtypeStruct(shape, bf16)] if filling else [])],
-            in_specs=[vmem] * count + [pl.BlockSpec(memory_space=pltpu.HBM if filling else pltpu.VMEM)] * len(blocks_in),
+            in_specs=[vmem] * count + [pl.BlockSpec(memory_space=pl.ANY if filling else pltpu.VMEM)] * len(blocks_in),
             out_specs=[vmem] * (len(outs) + filling),
             scratch_shapes=[*scratch, *([pltpu.SemaphoreType.DMA((copies,))] if filling else [])],
             compiler_params=pltpu.CompilerParams(vmem_limit_bytes=VMEM_LIMIT),
@@ -415,11 +432,17 @@
     sig, grad, part, fac_f, fac_g, held = layer_call(
         0, first_body, [got], None, [act, act, act, fac, fac], acc, 1, "layer_first"
     )
+    weights.own_halves([part])
     for layer in range(1, layers - 1):
+        arrived = swap(part)
+        if layer == 1:
+            arrived = lax.optimization_barrier((arrived, *weights.middle()))[0]
+        if layer == early:
+            pieces_of.append(weights.finish([part], [arrived]))
         factors.append((fac_f, fac_g))
         helds.append(held)
         sig, part, fac_f, fac_g, held = layer_call(
-            layer, forward_body, [sig, part, swap(part)], None, [act, act, fac, fac], acc, 1, "layer_forward"
+            layer, forward_body, [sig, part, arrived], None, [act, act, fac, fac], acc, 1, "layer_forward"
         )
     factors.append((fac_f, fac_g))
     helds.append(held)

time: 178 us -> 169 us (0.949)
  starting transfers between devices: 39.4 us -> 27.8 us
    ppermute x55 -> x29, starting transfers between devices: 35.9 us -> 23.6 us  [exchange(): lax.ppermute(values, axis, [(i, i ^ bit) for i in range(lax.axis_size(axi...]
    ppermute x55 -> x29, waiting for transfers between devices: 95.6 us -> 95.3 us  [exchange(): lax.ppermute(values, axis, [(i, i ^ bit) for i in range(lax.axis_size(axi...]
  transfers between devices with their start and end apart: 56 -> 30, of which waited for: 26 -> 13; matrix products, arithmetic and copies ran while one was open for 1% -> 1% of each run, Pallas kernels for 6% -> 4%
where the time goes in v5:
time: 169 us; the launch traced here: 168 us
  waiting for transfers between devices  96.7 us (57%)
  starting transfers between devices  27.8 us (16%)
  Pallas kernels  22.7 us (13%)
  blocking collectives  14.5 us (9%)
  local copies, waits for them, and re-layouts  3.22 us (2%)
  other arithmetic  2.31 us (1%)
    ppermute x29, waiting for transfers between devices, exchange(): lax.ppermute(values, axis, [(i, i ^ bit) for i in range(lax.axis_size(axi...  95.3 us
    ppermute x29, starting transfers between devices, exchange(): lax.ppermute(values, axis, [(i, i ^ bit) for i in range(lax.axis_size(axi...  23.6 us
    pallas_call x7, Pallas kernels, layer_call(): pl.pallas_call(kernel, out_shape=[*outs, *([jax.ShapeDtypeStruct(shape, b...  18.9 us
    all_to_all x1, blocking collectives, local(): back = lax.all_to_all(back, BOTH, split_axis=0, concat_axis=0, tiled=True)  14.5 us
    all_to_all x1, starting transfers between devices, exchange_rows(): return lax.all_to_all(ready, BOTH, split_axis=0, concat_axis=0, tiled=True)  4.22 us
    pallas_call x1, Pallas kernels, packed(): pl.pallas_call(kernel, out_shape=[jax.ShapeDtypeStruct(shape, jnp.bfloat1...  3.79 us
  transfers between devices with their start and end apart: 30, of which 13 were waited for; matrix products, arithmetic and copies ran while one was open for 1% of the time, Pallas kernels for 4%

profile of v5, /device:TPU:0, one launch (start us, length us, event | category | flops | bytes accessed | tf_op | source)
XLA Modules:
  0.0 168.0 jit_solution(11817166536023659308)
XLA Ops:
  0.6 3.8 %pack.1 = (bf16[1,10,128,256]{3,2,1,0:T(8,128)(2,1)}, bf16[1,10,256,256]{3,2,1,0:T(8,128)(2,1)}, bf16[1,6,128,256]{3,2,1,0:T(8,128)(2,1)}, bf16[1,6,256,256]{3,2,1,0:T(8,128)(2,1)}) custom-call(bf16[4,2,256,256]{3,2,1,0:T(8,128)(2,1)} %refs_0_.1, bf16[4,2,256,256]{3,2,1,0:T(8,128)(2,1)} %refs_1_.1, bf16[4,256,256]{2,1,0:T(8,128)(2,1)} %refs_2_.1), custom_call_target="tpu_custom_call" | custom-call | tf_op jit(solution)/shard_map/pack/pallas_call | solution.py:84
  4.4 3.0 %collective-permute-start.1 = (bf16[1,10,256,256]{3,2,1,0:T(8,128)(2,1)}, bf16[1,10,256,256]{3,2,1,0:T(8,128)(2,1)S(1)}, u32[]{:S(2)}, u32[]{:S(2)}) collective-permute-start(bf16[1,10,256,256]{3,2,1,0:T(8,128)(2,1)} %get-tuple-element.47.refs_1_.refs_3_), channel_id=1, source_target_pairs={{0,8},{4,12},{8,0},{12,4},{1,9},{5,13},{9,1},{13,5},{2,10},{6,14},... | collective-permute-start | bytes 3932168 | tf_op jit(solution)/shard_map/ppermute | solution.py:24
  7.5 2.6 %collective-permute-start = (bf16[1,10,128,256]{3,2,1,0:T(8,128)(2,1)}, bf16[1,10,128,256]{3,2,1,0:T(8,128)(2,1)S(1)}, u32[]{:S(2)}, u32[]{:S(2)}) collective-permute-start(bf16[1,10,128,256]{3,2,1,0:T(8,128)(2,1)} %get-tuple-element.46), channel_id=1, source_target_pairs={{0,2},{1,3},{2,0},{3,1},{4,6},{5,7},{6,4},{7,5},{8,10},{9,11},{10,... | collective-permute-start | bytes 1966088 | tf_op jit(solution)/shard_map/ppermute | solution.py:24
  10.0 28.8 %collective-permute-done.refs_3_.refs_5_ = bf16[1,10,128,256]{3,2,1,0:T(8,128)(2,1)S(1)} collective-permute-done((bf16[1,10,128,256]{3,2,1,0:T(8,128)(2,1)}, bf16[1,10,128,256]{3,2,1,0:T(8,128)(2,1)S(1)}, u32[]{:S(2)}, u32[]{:S(2)}) %collective-permute-start) | collective-permute-done | bytes 655392 | tf_op jit(solution)/shard_map/ppermute | solution.py:24
  38.8 1.5 collective-permute-start.3
  40.8 1.5 collective-permute-start.4
  42.3 17.6 %collective-permute-done.4.refs_5_.refs_6_ = bf16[1,6,128,256]{3,2,1,0:T(8,128)(2,1)} collective-permute-done((bf16[1,6,128,256]{3,2,1,0:T(8,128)(2,1)}, bf16[1,6,128,256]{3,2,1,0:T(8,128)(2,1)}, u32[]{:S(2)}, u32[]{:S(2)}) %collective-permute-start.4) | collective-permute-done | bytes 393248 | tf_op jit(solution)/shard_map/ppermute | solution.py:24
  60.4 1.5 collective-permute-start.5
  63.8 4.2 %all-to-all-start = ((bf16[16,2,24,256]{3,2,1,0:T(8,128)(2,1)}), bf16[16,2,24,256]{3,2,1,0:T(8,128)(2,1)}, u32[]{:S(2)}, u32[]{:S(2)}) async-start(bf16[16,2,24,256]{3,2,1,0:T(8,128)(2,1)} %bitcast.9), calls=%async_computation | async-start | bytes 786432 | tf_op jit(solution)/shard_map/all_to_all | solution.py:326
  68.5 8.9 %collective-permute-done.6.refs_6_.refs_8_ = bf16[1,10,128,256]{3,2,1,0:T(8,128)(2,1)} collective-permute-done((bf16[1,10,128,256]{3,2,1,0:T(8,128)(2,1)}, bf16[1,10,128,256]{3,2,1,0:T(8,128)(2,1)}, u32[]{:S(2)}, u32[]{:S(2)}) %collective-permute-start.6) | collective-permute-done | bytes 655392 | tf_op jit(solution)/shard_map/ppermute | solution.py:24
  77.3 1.6 collective-permute-start.14
  83.3 4.1 %layer_first.1 = (bf16[96,1024]{1,0:T(8,128)(2,1)S(1)}, bf16[96,1024]{1,0:T(8,128)(2,1)S(1)}, bf16[96,1024]{1,0:T(8,128)(2,1)S(1)}, f32[2,96,256]{2,1,0:T(8,128)...) custom-call(bf16[16,2,24,256]{3,2,1,0:T(8,128)(2,1)} %all-to-all-done.refs_0_, ...), custom_call_target="tpu_custom_call" | custom-call | flops 503316480 | bytes 5242880 | tf_op jit(solution)/shard_map/layer_first/pallas_call | solution.py:373
  87.5 2.9 %collective-permute-done.15.refs_7_.refs_8_ = bf16[1,6,128,256]{3,2,1,0:T(8,128)(2,1)} collective-permute-done((bf16[1,6,128,256]{3,2,1,0:T(8,128)(2,1)}, bf16[1,6,128,256]{3,2,1,0:T(8,128)(2,1)}, u32[]{:S(2)}, u32[]{:S(2)}) %collective-permute-start.15) | collective-permute-done | bytes 393248 | tf_op jit(solution)/shard_map/ppermute | solution.py:24
  90.4 7.1 %collective-permute-done.14.refs_4_.refs_5_ = bf16[1,6,256,256]{3,2,1,0:T(8,128)(2,1)S(1)} collective-permute-done((bf16[1,6,256,256]{3,2,1,0:T(8,128)(2,1)}, bf16[1,6,256,256]{3,2,1,0:T(8,128)(2,1)S(1)}, u32[]{:S(2)}, u32[]{:S(2)}) %collective-permute-start.14) | collective-permute-done | bytes 786464 | tf_op jit(solution)/shard_map/ppermute | solution.py:24
  97.6 3.0 %layer_forward.2 = (bf16[96,1024]{1,0:T(8,128)(2,1)S(1)}, bf16[96,1024]{1,0:T(8,128)(2,1)S(1)}, f32[2,96,256]{2,1,0:T(8,128)S(1)}, f32[2,96,256]{2,1,0:T(8,128)S(1)}, bf16[8,5,256,256]{3,2,1,0:T(8,128)(2,1)S(1)}) custom-call(bf16[96,1024]{1,0:T(8,128)(2,1)S(1)} %get-tuple-element.57.refs_0_, bf16[96,1024]{1,0:T(8,128)(2,1)S(1)} %get-tuple-element.58.refs_1_, ...), custom_call_target="tpu_custom_call" | custom-call | flops 503316480 | bytes 5242880 | tf_op jit(solution)/shard_map/layer_forward/pallas_call | solution.py:373
  101.5 5.7 %collective-permute-done.16.refs_2_ = bf16[96,1024]{1,0:T(8,128)(2,1)S(1)} collective-permute-done((bf16[96,1024]{1,0:T(8,128)(2,1)S(1)}, bf16[96,1024]{1,0:T(8,128)(2,1)S(1)}, u32[]{:S(2)}, u32[]{:S(2)}) %collective-permute-start.16) | collective-permute-done | bytes 196640 | tf_op jit(solution)/shard_map/ppermute | solution.py:24
  108.2 3.5 %collective-permute-done.17.refs_8_.refs_9_ = bf16[1,6,128,256]{3,2,1,0:T(8,128)(2,1)S(1)} collective-permute-done((bf16[1,6,128,256]{3,2,1,0:T(8,128)(2,1)}, bf16[1,6,128,256]{3,2,1,0:T(8,128)(2,1)S(1)}, u32[]{:S(2)}, u32[]{:S(2)}) %collective-permute-start.17) | collective-permute-done | bytes 393248 | tf_op jit(solution)/shard_map/ppermute | solution.py:24
  112.2 1.9 %collective-permute-done.22.refs_13_.refs_14_ = bf16[1,6,128,256]{3,2,1,0:T(8,128)(2,1)S(1)} collective-permute-done((bf16[1,6,128,256]{3,2,1,0:T(8,128)(2,1)}, bf16[1,6,128,256]{3,2,1,0:T(8,128)(2,1)S(1)}, u32[]{:S(2)}, u32[]{:S(2)}) %collective-permute-start.22) | collective-permute-done | bytes 393248 | tf_op jit(solution)/shard_map/ppermute | solution.py:24
  114.1 2.5 %layer_forward.3 = (bf16[96,1024]{1,0:T(8,128)(2,1)S(1)}, bf16[96,1024]{1,0:T(8,128)(2,1)S(1)}, f32[2,96,256]{2,1,0:T(8,128)S(1)}, f32[2,96,256]{2,1,0:T(8,128)S(1)}, bf16[8,3,256,256]{3,2,1,0:T(8,128)(2,1)S(1)}) custom-call(bf16[96,1024]{1,0:T(8,128)(2,1)S(1)} %get-tuple-element.63.refs_0_, bf16[96,1024]{1,0:T(8,128)(2,1)S(1)} %get-tuple-element.64.refs_1_, ...), custom_call_target="tpu_custom_call" | custom-call | flops 301989888 | bytes 3145728 | tf_op jit(solution)/shard_map/layer_forward/pallas_call | solution.py:373
  116.6 1.7 %collective-permute-start.24 = (bf16[96,1024]{1,0:T(8,128)(2,1)S(1)}, bf16[96,1024]{1,0:T(8,128)(2,1)S(1)}, u32[]{:S(2)}, u32[]{:S(2)}) collective-permute-start(bf16[96,1024]{1,0:T(8,128)(2,1)S(1)} %get-tuple-element.73.refs_1_), channel_id=1, source_target_pairs={{0,1},{1,0},{2,3},{3,2},{4,5},{5,4},{6,7},{7,6},{8,9},{9,8},{10,11... | collective-permute-start | bytes 589832 | tf_op jit(solution)/shard_map/ppermute | solution.py:24
  118.3 5.3 %collective-permute-done.24.refs_2_ = bf16[96,1024]{1,0:T(8,128)(2,1)S(1)} collective-permute-done((bf16[96,1024]{1,0:T(8,128)(2,1)S(1)}, bf16[96,1024]{1,0:T(8,128)(2,1)S(1)}, u32[]{:S(2)}, u32[]{:S(2)}) %collective-permute-start.24) | collective-permute-done | bytes 196640 | tf_op jit(solution)/shard_map/ppermute | solution.py:24
  123.6 3.7 %layer_last.1 = (bf16[96,1024]{1,0:T(8,128)(2,1)S(1)}, bf16[96,1024]{1,0:T(8,128)(2,1)S(1)}, bf16[96,1024]{1,0:T(8,128)(2,1)S(1)}, bf16[8,3,256,256]{3,2,1,0:T(8,128)(2,1)}) custom-call(bf16[96,1024]{1,0:T(8,128)(2,1)S(1)} %get-tuple-element.72.refs_0_, bf16[96,1024]{1,0:T(8,128)(2,1)S(1)} %get-tuple-element.73.refs_1_, ...), custom_call_target="tpu_custom_call" | custom-call | flops 603979776 | bytes 3145728 | tf_op jit(solution)/shard_map/layer_last/pallas_call | solution.py:373
  127.4 1.7 %collective-permute-start.25 = (bf16[96,1024]{1,0:T(8,128)(2,1)S(1)}, bf16[96,1024]{1,0:T(8,128)(2,1)S(1)}, u32[]{:S(2)}, u32[]{:S(2)}) collective-permute-start(bf16[96,1024]{1,0:T(8,128)(2,1)S(1)} %get-tuple-element.74.refs_1_), channel_id=1, source_target_pairs={{0,1},{1,0},{2,3},{3,2},{4,5},{5,4},{6,7},{7,6},{8,9},{9,8},{10,11... | collective-permute-start | bytes 589832 | tf_op jit(solution)/shard_map/ppermute | solution.py:24
  129.1 4.4 %collective-permute-done.25.refs_2_ = bf16[96,1024]{1,0:T(8,128)(2,1)S(1)} collective-permute-done((bf16[96,1024]{1,0:T(8,128)(2,1)S(1)}, bf16[96,1024]{1,0:T(8,128)(2,1)S(1)}, u32[]{:S(2)}, u32[]{:S(2)}) %collective-permute-start.25) | collective-permute-done | bytes 196640 | tf_op jit(solution)/shard_map/ppermute | solution.py:24
  133.5 1.4 layer_backward.2
  134.9 1.8 %collective-permute-start.26 = (bf16[96,1024]{1,0:T(8,128)(2,1)S(1)}, bf16[96,1024]{1,0:T(8,128)(2,1)S(1)}, u32[]{:S(2)}, u32[]{:S(2)}) collective-permute-start(bf16[96,1024]{1,0:T(8,128)(2,1)S(1)} %get-tuple-element.79.refs_1_), channel_id=1, source_target_pairs={{0,1},{1,0},{2,3},{3,2},{4,5},{5,4},{6,7},{7,6},{8,9},{9,8},{10,11... | collective-permute-start | bytes 589832 | tf_op jit(solution)/shard_map/ppermute | solution.py:24
  137.0 5.3 %collective-permute-done.26.refs_2_ = bf16[96,1024]{1,0:T(8,128)(2,1)S(1)} collective-permute-done((bf16[96,1024]{1,0:T(8,128)(2,1)S(1)}, bf16[96,1024]{1,0:T(8,128)(2,1)S(1)}, u32[]{:S(2)}, u32[]{:S(2)}) %collective-permute-start.26) | collective-permute-done | bytes 196640 | tf_op jit(solution)/shard_map/ppermute | solution.py:24
  142.3 2.0 %layer_backward.3 = (bf16[96,1024]{1,0:T(8,128)(2,1)S(1)}, bf16[96,1024]{1,0:T(8,128)(2,1)S(1)}) custom-call(bf16[96,1024]{1,0:T(8,128)(2,1)S(1)} %get-tuple-element.78.refs_0_, bf16[96,1024]{1,0:T(8,128)(2,1)S(1)} %get-tuple-element.79.refs_1_, bf16[96,1024]{1,0:T(8,128)(2,1)S(1)} %collective-permute-done.26.refs_2_, ...), custom_call_target="tpu_custom_call" | custom-call | flops 503316480 | bytes 5242880 | tf_op jit(solution)/shard_map/layer_backward/pallas_call | solution.py:373
  144.3 1.8 %collective-permute-start.27 = (bf16[96,1024]{1,0:T(8,128)(2,1)S(1)}, bf16[96,1024]{1,0:T(8,128)(2,1)S(1)}, u32[]{:S(2)}, u32[]{:S(2)}) collective-permute-start(bf16[96,1024]{1,0:T(8,128)(2,1)S(1)} %get-tuple-element.84.refs_1_), channel_id=1, source_target_pairs={{0,1},{1,0},{2,3},{3,2},{4,5},{5,4},{6,7},{7,6},{8,9},{9,8},{10,11... | collective-permute-start | bytes 589832 | tf_op jit(solution)/shard_map/ppermute | solution.py:24
  146.1 4.0 %collective-permute-done.27.refs_2_ = bf16[96,1024]{1,0:T(8,128)(2,1)S(1)} collective-permute-done((bf16[96,1024]{1,0:T(8,128)(2,1)S(1)}, bf16[96,1024]{1,0:T(8,128)(2,1)S(1)}, u32[]{:S(2)}, u32[]{:S(2)}) %collective-permute-start.27) | collective-permute-done | bytes 196640 | tf_op jit(solution)/shard_map/ppermute | solution.py:24
  150.1 2.1 %layer_final.1 = bf16[16,24,384]{2,1,0:T(8,128)(2,1)S(1)} custom-call(bf16[96,1024]{1,0:T(8,128)(2,1)S(1)} %get-tuple-element.83.refs_0_, bf16[96,1024]{1,0:T(8,128)(2,1)S(1)} %get-tuple-element.84.refs_1_, bf16[96,1024]{1,0:T(8,128)(2,1)S(1)} %collective-permute-done.27.refs_2_, f32[2,96,256]{2,1,0:T(8,128)S(1)} %get-tuple-element.85.refs_3_, ...), custom_call_target="tpu_custom_call" | custom-call | flops 503316480 | bytes 5242880 | tf_op jit(solution)/shard_map/layer_final/pallas_call | solution.py:373
  152.2 14.5 %all_to_all.10 = bf16[16,24,384]{2,1,0:T(8,128)(2,1)S(1)} all-to-all(bf16[16,24,384]{2,1,0:T(8,128)(2,1)S(1)} %layer_final.1), channel_id=1, replica_groups=mesh['groups'=2,'tm'=4,'chan'=4] {'tm','chan'}, dimensions={0} | all-to-all | bytes 589824 | tf_op jit(solution)/shard_map/all_to_all | solution.py:498
  (52 shorter events, 11.9 us)
Async XLA Ops:
  4.4 34.4 %collective-permute-start.1 = (bf16[1,10,256,256]{3,2,1,0:T(8,128)(2,1)}, bf16[1,10,256,256]{3,2,1,0:T(8,128)(2,1)S(1)}, u32[]{:S(2)}, u32[]{:S(2)}) collective-permute-start(bf16[1,10,256,256]{3,2,1,0:T(8,128)(2,1)} %get-tuple-element.47.refs_1_.refs_3_), channel_id=1, source_target_pairs={{0,8},{4,12},{8,0},{12,4},{1,9},{5,13},{9,1},{13,5},{2,10},{6,14},... | collective-permute-start | bytes 3932168 | tf_op jit(solution)/shard_map/ppermute | solution.py:24
  7.5 31.3 %collective-permute-start = (bf16[1,10,128,256]{3,2,1,0:T(8,128)(2,1)}, bf16[1,10,128,256]{3,2,1,0:T(8,128)(2,1)S(1)}, u32[]{:S(2)}, u32[]{:S(2)}) collective-permute-start(bf16[1,10,128,256]{3,2,1,0:T(8,128)(2,1)} %get-tuple-element.46), channel_id=1, source_target_pairs={{0,2},{1,3},{2,0},{3,1},{4,6},{5,7},{6,4},{7,5},{8,10},{9,11},{10,... | collective-permute-start | bytes 1966088 | tf_op jit(solution)/shard_map/ppermute | solution.py:24
  10.0 51.9 %collective-permute-start.7 = (bf16[1,10,256,256]{3,2,1,0:T(8,128)(2,1)}, bf16[1,10,256,256]{3,2,1,0:T(8,128)(2,1)S(1)}, u32[]{:S(2)}, u32[]{:S(2)}) collective-permute-start(bf16[1,10,256,256]{3,2,1,0:T(8,128)(2,1)} %get-tuple-element.47.refs_1_.refs_3_), channel_id=1, source_target_pairs={{0,4},{4,0},{8,12},{12,8},{1,5},{5,1},{9,13},{13,9},{2,6},{6,2},{1... | collective-permute-start | bytes 3932168 | tf_op jit(solution)/shard_map/ppermute | solution.py:24
  38.8 38.5 %copy-start.2 = (bf16[1,10,128,256]{3,2,1,0:T(8,128)(2,1)}, bf16[1,10,128,256]{3,2,1,0:T(8,128)(2,1)S(1)}, u32[]{:S(2)}) copy-start(bf16[1,10,128,256]{3,2,1,0:T(8,128)(2,1)S(1)} %collective-permute-done.refs_3_.refs_5_) | copy-start | bytes 1966084
  38.8 21.1 %collective-permute-start.3 = (bf16[1,10,128,256]{3,2,1,0:T(8,128)(2,1)S(1)}, bf16[1,10,128,256]{3,2,1,0:T(8,128)(2,1)}, u32[]{:S(2)}, u32[]{:S(2)}) collective-permute-start(bf16[1,10,128,256]{3,2,1,0:T(8,128)(2,1)S(1)} %collective-permute-done.refs_3_.refs_5_), channel_id=1, source_target_pairs={{0,16},{16,0},{1,17},{17,1},{2,18},{18,2},{3,19},{19,3},{4,20},{20... | collective-permute-start | bytes 1966088 | tf_op jit(solution)/shard_map/ppermute | solution.py:24
  40.3 19.6 %collective-permute-start.2 = (bf16[1,10,128,256]{3,2,1,0:T(8,128)(2,1)S(1)}, bf16[1,10,128,256]{3,2,1,0:T(8,128)(2,1)}, u32[]{:S(2)}, u32[]{:S(2)}) collective-permute-start(bf16[1,10,128,256]{3,2,1,0:T(8,128)(2,1)S(1)} %collective-permute-done.refs_3_.refs_5_), channel_id=1, source_target_pairs={{0,8},{4,12},{8,0},{12,4},{1,9},{5,13},{9,1},{13,5},{2,10},{6,14},... | collective-permute-start | bytes 1966088 | tf_op jit(solution)/shard_map/ppermute | solution.py:24
  40.8 19.0 %collective-permute-start.4 = (bf16[1,6,128,256]{3,2,1,0:T(8,128)(2,1)}, bf16[1,6,128,256]{3,2,1,0:T(8,128)(2,1)}, u32[]{:S(2)}, u32[]{:S(2)}) collective-permute-start(bf16[1,6,128,256]{3,2,1,0:T(8,128)(2,1)} %get-tuple-element.51), channel_id=1, source_target_pairs={{0,2},{1,3},{2,0},{3,1},{4,6},{5,7},{6,4},{7,5},{8,10},{9,11},{10,... | collective-permute-start | bytes 1179656 | tf_op jit(solution)/shard_map/ppermute | solution.py:24
  42.3 25.7 %collective-permute-start.9 = (bf16[1,10,128,256]{3,2,1,0:T(8,128)(2,1)S(1)}, bf16[1,10,128,256]{3,2,1,0:T(8,128)(2,1)}, u32[]{:S(2)}, u32[]{:S(2)}) collective-permute-start(bf16[1,10,128,256]{3,2,1,0:T(8,128)(2,1)S(1)} %collective-permute-done.refs_3_.refs_5_), channel_id=1, source_target_pairs={{0,4},{4,0},{8,12},{12,8},{1,5},{5,1},{9,13},{13,9},{2,6},{6,2},{1... | collective-permute-start | bytes 1966088 | tf_op jit(solution)/shard_map/ppermute | solution.py:24
  59.9 21.0 %collective-permute-start.8 = (bf16[1,10,256,256]{3,2,1,0:T(8,128)(2,1)S(1)}, bf16[1,10,256,256]{3,2,1,0:T(8,128)(2,1)}, u32[]{:S(2)}, u32[]{:S(2)}) collective-permute-start(bf16[1,10,256,256]{3,2,1,0:T(8,128)(2,1)S(1)} %collective-permute-done.1.refs_2_.refs_4_), channel_id=1, source_target_pairs={{0,4},{4,0},{8,12},{12,8},{1,5},{5,1},{9,13},{13,9},{2,6},{6,2},{1... | collective-permute-start | bytes 3932168 | tf_op jit(solution)/shard_map/ppermute | solution.py:24
  59.9 17.5 %collective-permute-start.6 = (bf16[1,10,128,256]{3,2,1,0:T(8,128)(2,1)}, bf16[1,10,128,256]{3,2,1,0:T(8,128)(2,1)}, u32[]{:S(2)}, u32[]{:S(2)}) collective-permute-start(bf16[1,10,128,256]{3,2,1,0:T(8,128)(2,1)} %collective-permute-done.2.refs_4_.refs_6_), channel_id=1, source_target_pairs={{0,16},{16,0},{1,17},{17,1},{2,18},{18,2},{3,19},{19,3},{4,20},{20... | collective-permute-start | bytes 1966088 | tf_op jit(solution)/shard_map/ppermute | solution.py:24
  60.4 16.9 %collective-permute-start.5 = (bf16[1,6,128,256]{3,2,1,0:T(8,128)(2,1)}, bf16[1,6,128,256]{3,2,1,0:T(8,128)(2,1)}, u32[]{:S(2)}, u32[]{:S(2)}) collective-permute-start(bf16[1,6,128,256]{3,2,1,0:T(8,128)(2,1)} %collective-permute-done.4.refs_5_.refs_6_), channel_id=1, source_target_pairs={{0,8},{4,12},{8,0},{12,4},{1,9},{5,13},{9,1},{13,5},{2,10},{6,14},... | collective-permute-start | bytes 1179656 | tf_op jit(solution)/shard_map/ppermute | solution.py:24
  62.0 16.9 %collective-permute-start.11 = (bf16[1,10,128,256]{3,2,1,0:T(8,128)(2,1)}, bf16[1,10,128,256]{3,2,1,0:T(8,128)(2,1)}, u32[]{:S(2)}, u32[]{:S(2)}) collective-permute-start(bf16[1,10,128,256]{3,2,1,0:T(8,128)(2,1)} %collective-permute-done.3.refs_5_.refs_7_), channel_id=1, source_target_pairs={{0,4},{4,0},{8,12},{12,8},{1,5},{5,1},{9,13},{13,9},{2,6},{6,2},{1... | collective-permute-start | bytes 1966088 | tf_op jit(solution)/shard_map/ppermute | solution.py:24
  63.8 17.1 %all-to-all-start = ((bf16[16,2,24,256]{3,2,1,0:T(8,128)(2,1)}), bf16[16,2,24,256]{3,2,1,0:T(8,128)(2,1)}, u32[]{:S(2)}, u32[]{:S(2)}) async-start(bf16[16,2,24,256]{3,2,1,0:T(8,128)(2,1)} %bitcast.9), calls=%async_computation | async-start | bytes 786432 | tf_op jit(solution)/shard_map/all_to_all | solution.py:326
  68.0 12.9 %collective-permute-start.10 = (bf16[1,10,128,256]{3,2,1,0:T(8,128)(2,1)}, bf16[1,10,128,256]{3,2,1,0:T(8,128)(2,1)}, u32[]{:S(2)}, u32[]{:S(2)}) collective-permute-start(bf16[1,10,128,256]{3,2,1,0:T(8,128)(2,1)} %collective-permute-done.2.refs_4_.refs_6_), channel_id=1, source_target_pairs={{0,4},{4,0},{8,12},{12,8},{1,5},{5,1},{9,13},{13,9},{2,6},{6,2},{1... | collective-permute-start | bytes 1966088 | tf_op jit(solution)/shard_map/ppermute | solution.py:24
  77.3 3.6 %collective-permute-start.12 = (bf16[1,10,128,256]{3,2,1,0:T(8,128)(2,1)}, bf16[1,10,128,256]{3,2,1,0:T(8,128)(2,1)}, u32[]{:S(2)}, u32[]{:S(2)}) collective-permute-start(bf16[1,10,128,256]{3,2,1,0:T(8,128)(2,1)} %collective-permute-done.6.refs_6_.refs_8_), channel_id=1, source_target_pairs={{0,4},{4,0},{8,12},{12,8},{1,5},{5,1},{9,13},{13,9},{2,6},{6,2},{1... | collective-permute-start | bytes 1966088 | tf_op jit(solution)/shard_map/ppermute | solution.py:24
  77.3 20.2 %collective-permute-start.14 = (bf16[1,6,256,256]{3,2,1,0:T(8,128)(2,1)}, bf16[1,6,256,256]{3,2,1,0:T(8,128)(2,1)S(1)}, u32[]{:S(2)}, u32[]{:S(2)}) collective-permute-start(bf16[1,6,256,256]{3,2,1,0:T(8,128)(2,1)} %get-tuple-element.65.refs_3_.refs_4_), channel_id=1, source_target_pairs={{0,8},{4,12},{8,0},{12,4},{1,9},{5,13},{9,1},{13,5},{2,10},{6,14},... | collective-permute-start | bytes 2359304 | tf_op jit(solution)/shard_map/ppermute | solution.py:24
  78.9 11.5 %collective-permute-start.15 = (bf16[1,6,128,256]{3,2,1,0:T(8,128)(2,1)}, bf16[1,6,128,256]{3,2,1,0:T(8,128)(2,1)}, u32[]{:S(2)}, u32[]{:S(2)}) collective-permute-start(bf16[1,6,128,256]{3,2,1,0:T(8,128)(2,1)} %collective-permute-done.4.refs_5_.refs_6_), channel_id=1, source_target_pairs={{0,16},{16,0},{1,17},{17,1},{2,18},{18,2},{3,19},{19,3},{4,20},{20... | collective-permute-start | bytes 1179656 | tf_op jit(solution)/shard_map/ppermute | solution.py:24
  87.4 10.2 %collective-permute-start.13 = (bf16[96,1024]{1,0:T(8,128)(2,1)S(1)}, bf16[96,1024]{1,0:T(8,128)(2,1)S(1)}, u32[]{:S(2)}, u32[]{:S(2)}) collective-permute-start(bf16[96,1024]{1,0:T(8,128)(2,1)S(1)} %get-tuple-element.58.refs_1_), channel_id=1, source_target_pairs={{0,1},{1,0},{2,3},{3,2},{4,5},{5,4},{6,7},{7,6},{8,9},{9,8},{10,11... | collective-permute-start | bytes 589832 | tf_op jit(solution)/shard_map/ppermute | solution.py:24
  97.6 9.6 %copy-start.1 = (bf16[1,6,256,256]{3,2,1,0:T(8,128)(2,1)S(1)}, bf16[1,6,256,256]{3,2,1,0:T(8,128)(2,1)}, u32[]{:S(2)}) copy-start(bf16[1,6,256,256]{3,2,1,0:T(8,128)(2,1)} %get-tuple-element.65.refs_3_.refs_4_) | copy-start | bytes 2359300
  100.6 6.6 %collective-permute-start.16 = (bf16[96,1024]{1,0:T(8,128)(2,1)S(1)}, bf16[96,1024]{1,0:T(8,128)(2,1)S(1)}, u32[]{:S(2)}, u32[]{:S(2)}) collective-permute-start(bf16[96,1024]{1,0:T(8,128)(2,1)S(1)} %get-tuple-element.64.refs_1_), channel_id=1, source_target_pairs={{0,1},{1,0},{2,3},{3,2},{4,5},{5,4},{6,7},{7,6},{8,9},{9,8},{10,11... | collective-permute-start | bytes 589832 | tf_op jit(solution)/shard_map/ppermute | solution.py:24
  100.7 11.0 %collective-permute-start.17 = (bf16[1,6,128,256]{3,2,1,0:T(8,128)(2,1)}, bf16[1,6,128,256]{3,2,1,0:T(8,128)(2,1)S(1)}, u32[]{:S(2)}, u32[]{:S(2)}) collective-permute-start(bf16[1,6,128,256]{3,2,1,0:T(8,128)(2,1)} %collective-permute-done.5.refs_6_.refs_7_), channel_id=1, source_target_pairs={{0,16},{16,0},{1,17},{17,1},{2,18},{18,2},{3,19},{19,3},{4,20},{20... | collective-permute-start | bytes 1179656 | tf_op jit(solution)/shard_map/ppermute | solution.py:24
  107.2 4.5 %collective-permute-start.20 = (bf16[1,6,128,256]{3,2,1,0:T(8,128)(2,1)}, bf16[1,6,128,256]{3,2,1,0:T(8,128)(2,1)S(1)}, u32[]{:S(2)}, u32[]{:S(2)}) collective-permute-start(bf16[1,6,128,256]{3,2,1,0:T(8,128)(2,1)} %collective-permute-done.4.refs_5_.refs_6_), channel_id=1, source_target_pairs={{0,4},{4,0},{8,12},{12,8},{1,5},{5,1},{9,13},{13,9},{2,6},{6,2},{1... | collective-permute-start | bytes 1179656 | tf_op jit(solution)/shard_map/ppermute | solution.py:24
  107.2 6.9 %collective-permute-start.18 = (bf16[1,6,256,256]{3,2,1,0:T(8,128)(2,1)S(1)}, bf16[1,6,256,256]{3,2,1,0:T(8,128)(2,1)S(1)}, u32[]{:S(2)}, u32[]{:S(2)}) collective-permute-start(bf16[1,6,256,256]{3,2,1,0:T(8,128)(2,1)S(1)} %copy-done.1), channel_id=1, source_target_pairs={{0,4},{4,0},{8,12},{12,8},{1,5},{5,1},{9,13},{13,9},{2,6},{6,2},{1... | collective-permute-start | bytes 2359304 | tf_op jit(solution)/shard_map/ppermute | solution.py:24
  107.7 6.4 %collective-permute-start.19 = (bf16[1,6,256,256]{3,2,1,0:T(8,128)(2,1)S(1)}, bf16[1,6,256,256]{3,2,1,0:T(8,128)(2,1)S(1)}, u32[]{:S(2)}, u32[]{:S(2)}) collective-permute-start(bf16[1,6,256,256]{3,2,1,0:T(8,128)(2,1)S(1)} %collective-permute-done.14.refs_4_.refs_5_), channel_id=1, source_target_pairs={{0,4},{4,0},{8,12},{12,8},{1,5},{5,1},{9,13},{13,9},{2,6},{6,2},{1... | collective-permute-start | bytes 2359304 | tf_op jit(solution)/shard_map/ppermute | solution.py:24
  107.7 4.5 %collective-permute-start.21 = (bf16[1,6,128,256]{3,2,1,0:T(8,128)(2,1)}, bf16[1,6,128,256]{3,2,1,0:T(8,128)(2,1)S(1)}, u32[]{:S(2)}, u32[]{:S(2)}) collective-permute-start(bf16[1,6,128,256]{3,2,1,0:T(8,128)(2,1)} %collective-permute-done.5.refs_6_.refs_7_), channel_id=1, source_target_pairs={{0,4},{4,0},{8,12},{12,8},{1,5},{5,1},{9,13},{13,9},{2,6},{6,2},{1... | collective-permute-start | bytes 1179656 | tf_op jit(solution)/shard_map/ppermute | solution.py:24
  111.7 2.4 %collective-permute-start.22 = (bf16[1,6,128,256]{3,2,1,0:T(8,128)(2,1)}, bf16[1,6,128,256]{3,2,1,0:T(8,128)(2,1)S(1)}, u32[]{:S(2)}, u32[]{:S(2)}) collective-permute-start(bf16[1,6,128,256]{3,2,1,0:T(8,128)(2,1)} %collective-permute-done.15.refs_7_.refs_8_), channel_id=1, source_target_pairs={{0,4},{4,0},{8,12},{12,8},{1,5},{5,1},{9,13},{13,9},{2,6},{6,2},{1... | collective-permute-start | bytes 1179656 | tf_op jit(solution)/shard_map/ppermute | solution.py:24
  111.7 2.4 %collective-permute-start.23 = (bf16[1,6,128,256]{3,2,1,0:T(8,128)(2,1)S(1)}, bf16[1,6,128,256]{3,2,1,0:T(8,128)(2,1)S(1)}, u32[]{:S(2)}, u32[]{:S(2)}) collective-permute-start(bf16[1,6,128,256]{3,2,1,0:T(8,128)(2,1)S(1)} %collective-permute-done.17.refs_8_.refs_9_), channel_id=1, source_target_pairs={{0,4},{4,0},{8,12},{12,8},{1,5},{5,1},{9,13},{13,9},{2,6},{6,2},{1... | collective-permute-start | bytes 1179656 | tf_op jit(solution)/shard_map/ppermute | solution.py:24
  116.6 7.0 %collective-permute-start.24 = (bf16[96,1024]{1,0:T(8,128)(2,1)S(1)}, bf16[96,1024]{1,0:T(8,128)(2,1)S(1)}, u32[]{:S(2)}, u32[]{:S(2)}) collective-permute-start(bf16[96,1024]{1,0:T(8,128)(2,1)S(1)} %get-tuple-element.73.refs_1_), channel_id=1, source_target_pairs={{0,1},{1,0},{2,3},{3,2},{4,5},{5,4},{6,7},{7,6},{8,9},{9,8},{10,11... | collective-permute-start | bytes 589832 | tf_op jit(solution)/shard_map/ppermute | solution.py:24
  127.4 6.2 %collective-permute-start.25 = (bf16[96,1024]{1,0:T(8,128)(2,1)S(1)}, bf16[96,1024]{1,0:T(8,128)(2,1)S(1)}, u32[]{:S(2)}, u32[]{:S(2)}) collective-permute-start(bf16[96,1024]{1,0:T(8,128)(2,1)S(1)} %get-tuple-element.74.refs_1_), channel_id=1, source_target_pairs={{0,1},{1,0},{2,3},{3,2},{4,5},{5,4},{6,7},{7,6},{8,9},{9,8},{10,11... | collective-permute-start | bytes 589832 | tf_op jit(solution)/shard_map/ppermute | solution.py:24
  134.9 7.3 %collective-permute-start.26 = (bf16[96,1024]{1,0:T(8,128)(2,1)S(1)}, bf16[96,1024]{1,0:T(8,128)(2,1)S(1)}, u32[]{:S(2)}, u32[]{:S(2)}) collective-permute-start(bf16[96,1024]{1,0:T(8,128)(2,1)S(1)} %get-tuple-element.79.refs_1_), channel_id=1, source_target_pairs={{0,1},{1,0},{2,3},{3,2},{4,5},{5,4},{6,7},{7,6},{8,9},{9,8},{10,11... | collective-permute-start | bytes 589832 | tf_op jit(solution)/shard_map/ppermute | solution.py:24
  136.7 9.4 %collective-permute-start.28 = (bf16[96,1024]{1,0:T(8,128)(2,1)S(1)}, bf16[96,1024]{1,0:T(8,128)(2,1)S(1)}, u32[]{:S(2)}, u32[]{:S(2)}) collective-permute-start(bf16[96,1024]{1,0:T(8,128)(2,1)S(1)} %get-tuple-element.88.refs_6_), channel_id=1, source_target_pairs={{0,1},{1,0},{2,3},{3,2},{4,5},{5,4},{6,7},{7,6},{8,9},{9,8},{10,11... | collective-permute-start | bytes 589832 | tf_op jit(solution)/shard_map/ppermute | solution.py:24
  144.3 5.7 %collective-permute-start.27 = (bf16[96,1024]{1,0:T(8,128)(2,1)S(1)}, bf16[96,1024]{1,0:T(8,128)(2,1)S(1)}, u32[]{:S(2)}, u32[]{:S(2)}) collective-permute-start(bf16[96,1024]{1,0:T(8,128)(2,1)S(1)} %get-tuple-element.84.refs_1_), channel_id=1, source_target_pairs={{0,1},{1,0},{2,3},{3,2},{4,5},{5,4},{6,7},{7,6},{8,9},{9,8},{10,11... | collective-permute-start | bytes 589832 | tf_op jit(solution)/shard_map/ppermute | solution.py:24
  (2 other events, 2.4 us)

commit v6 on v5

--- a/solution.py
+++ b/solution.py
@@ -131,13 +131,14 @@
         for p in merged(pieces, self.limit):
             self.others[n].append(ordered(p, "groups", 1, "other", after))
 
-    def send(self, exchange_rows):
+    def send(self, exchange_rows, sent):
         def arrays(*lists):
             return [p.array for pieces in lists for p in pieces]
 
         self.along_chan(0)
         self.own_along_tm(0)
-        ended = arrays(self.zs[0], self.ys[0], self.full[0][1:])
+        ended = arrays(self.zs[0], self.ys[0], self.full[0][1:], [self.halves[1]], self.full[1])
+        ended.append(sent)
         self.others_along_tm(0, ended)
         self.along_groups(0, self.zs[0] + self.ys[0], ended)
         self.along_chan(1, ended)
@@ -159,8 +160,7 @@
         return [p.array for p in self.ys[1] + self.full[1][1:] + self.others[1]]
 
     def finish(self, before, after):
-        first = [p.array for p in self.ys[1] + self.full[1][1:] + self.others[1]]
-        self.along_groups(1, self.crossed[1], [*before, *first])
+        self.along_groups(1, self.crossed[1], before)
         return self.stage(1, after)
 
     def stage(self, n, after=()):
@@ -312,7 +312,8 @@
     sources = (filter_weight, gate_weight, mix_source)
     early = (layers + 1) // 2
     stages = [range(early), range(early, layers)]
-    weights = Weights(packed(sources, taps_of, stages), HALVED)
+    packs = [array for stage in stages for array in packed(sources, taps_of, [stage])]
+    weights = Weights(packs, HALVED)
 
     def swap(values):
         return exchange(values, "chan", 1)
@@ -325,7 +326,7 @@
         ready = lax.optimization_barrier((sent, *after))[0]
         return lax.all_to_all(ready, BOTH, split_axis=0, concat_axis=0, tiled=True)
 
-    got, pieces = weights.send(exchange_rows)
+    got, pieces = weights.send(exchange_rows, sent)
     pieces_of = [pieces]
     if not square:
         got = got.reshape(tm_count, chan_count, 2, span, nb).transpose(2, 0, 3, 1, 4)
@@ -433,12 +434,13 @@
         0, first_body, [got], None, [act, act, act, fac, fac], acc, 1, "layer_first"
     )
     weights.own_halves([part])
+    first_part = part
     for layer in range(1, layers - 1):
         arrived = swap(part)
         if layer == 1:
-            arrived = lax.optimization_barrier((arrived, *weights.middle()))[0]
-        if layer == early:
-            pieces_of.append(weights.finish([part], [arrived]))
+            middle = [p.array for p in weights.others[1]]
+            arrived = lax.optimization_barrier((arrived, *middle))[0]
+            pieces_of.append(weights.finish([first_part, *middle], [part]))
         factors.append((fac_f, fac_g))
         helds.append(held)
         sig, part, fac_f, fac_g, held = layer_call(

time: 169 us -> 165 us (0.976)
  starting transfers between devices: 27.8 us -> 23.2 us
  waiting for transfers between devices: 96.7 us -> 99.3 us
  local copies, waits for them, and re-layouts: 3.22 us -> 0.82 us
    ppermute x29, starting transfers between devices: 23.6 us -> 19 us  [exchange(): lax.ppermute(values, axis, [(i, i ^ bit) for i in range(lax.axis_size(axi...]
    ppermute x29, waiting for transfers between devices: 95.3 us -> 99.3 us  [exchange(): lax.ppermute(values, axis, [(i, i ^ bit) for i in range(lax.axis_size(axi...]
    unnamed x8, local copies, waits for them, and re-layouts: 2.4 us -> 0.02 us
    pallas_call x1 -> x2, Pallas kernels: 3.79 us -> 5.48 us  [packed(): pl.pallas_call(kernel, out_shape=[jax.ShapeDtypeStruct(shape, jnp.bfloat1...]
  transfers between devices with their start and end apart: 30 -> 30, of which waited for: 13 -> 16; matrix products, arithmetic and copies ran while one was open for 1% -> 0% of each run, Pallas kernels for 4% -> 7%
where the time goes in v6:
time: 165 us; the launch traced here: 164 us
  waiting for transfers between devices  99.3 us (60%)
  Pallas kernels  24.3 us (15%)
  starting transfers between devices  23.2 us (14%)
  blocking collectives  14.7 us (9%)
    ppermute x29, waiting for transfers between devices, exchange(): lax.ppermute(values, axis, [(i, i ^ bit) for i in range(lax.axis_size(axi...  99.3 us
    ppermute x29, starting transfers between devices, exchange(): lax.ppermute(values, axis, [(i, i ^ bit) for i in range(lax.axis_size(axi...  19 us
    pallas_call x7, Pallas kernels, layer_call(): pl.pallas_call(kernel, out_shape=[*outs, *([jax.ShapeDtypeStruct(shape, b...  18.8 us
    all_to_all x1, blocking collectives, local(): back = lax.all_to_all(back, BOTH, split_axis=0, concat_axis=0, tiled=True)  14.7 us
    pallas_call x2, Pallas kernels, packed(): pl.pallas_call(kernel, out_shape=[jax.ShapeDtypeStruct(shape, jnp.bfloat1...  5.48 us
    all_to_all x1, starting transfers between devices, exchange_rows(): return lax.all_to_all(ready, BOTH, split_axis=0, concat_axis=0, tiled=True)  4.2 us
  transfers between devices with their start and end apart: 30, of which 16 were waited for; matrix products, arithmetic and copies ran while one was open for 0% of the time, Pallas kernels for 7%

profile of v6, /device:TPU:0, one launch (start us, length us, event | category | flops | bytes accessed | tf_op | source)
XLA Modules:
  0.0 164.5 jit_solution(9039549817392451895)
XLA Ops:
  0.6 3.0 %pack.2 = (bf16[1,10,128,256]{3,2,1,0:T(8,128)(2,1)}, bf16[1,10,256,256]{3,2,1,0:T(8,128)(2,1)}) custom-call(bf16[4,2,256,256]{3,2,1,0:T(8,128)(2,1)} %refs_0_.3, bf16[4,2,256,256]{3,2,1,0:T(8,128)(2,1)} %refs_1_.3, bf16[4,256,256]{2,1,0:T(8,128)(2,1)} %refs_2_.3), custom_call_target="tpu_custom_call" | custom-call | tf_op jit(solution)/shard_map/pack/pallas_call | solution.py:84
  3.7 3.0 %collective-permute-start.1 = (bf16[1,10,256,256]{3,2,1,0:T(8,128)(2,1)}, bf16[1,10,256,256]{3,2,1,0:T(8,128)(2,1)S(1)}, u32[]{:S(2)}, u32[]{:S(2)}) collective-permute-start(bf16[1,10,256,256]{3,2,1,0:T(8,128)(2,1)} %get-tuple-element.47.refs_1_.refs_3_), channel_id=1, source_target_pairs={{0,8},{4,12},{8,0},{12,4},{1,9},{5,13},{9,1},{13,5},{2,10},{6,14},... | collective-permute-start | bytes 3932168 | tf_op jit(solution)/shard_map/ppermute | solution.py:24
  6.7 2.6 %collective-permute-start = (bf16[1,10,128,256]{3,2,1,0:T(8,128)(2,1)}, bf16[1,10,128,256]{3,2,1,0:T(8,128)(2,1)}, u32[]{:S(2)}, u32[]{:S(2)}) collective-permute-start(bf16[1,10,128,256]{3,2,1,0:T(8,128)(2,1)} %get-tuple-element.46), channel_id=1, source_target_pairs={{0,2},{1,3},{2,0},{3,1},{4,6},{5,7},{6,4},{7,5},{8,10},{9,11},{10,... | collective-permute-start | bytes 1966088 | tf_op jit(solution)/shard_map/ppermute | solution.py:24
  9.3 2.4 %pack.3 = (bf16[1,6,128,256]{3,2,1,0:T(8,128)(2,1)}, bf16[1,6,256,256]{3,2,1,0:T(8,128)(2,1)}) custom-call(bf16[4,2,256,256]{3,2,1,0:T(8,128)(2,1)} %refs_0_.3, bf16[4,2,256,256]{3,2,1,0:T(8,128)(2,1)} %refs_1_.3, bf16[4,256,256]{2,1,0:T(8,128)(2,1)} %refs_2_.3), custom_call_target="tpu_custom_call" | custom-call | tf_op jit(solution)/shard_map/pack/pallas_call | solution.py:84
  11.9 26.3 %collective-permute-done.refs_3_.refs_5_ = bf16[1,10,128,256]{3,2,1,0:T(8,128)(2,1)} collective-permute-done((bf16[1,10,128,256]{3,2,1,0:T(8,128)(2,1)}, bf16[1,10,128,256]{3,2,1,0:T(8,128)(2,1)}, u32[]{:S(2)}, u32[]{:S(2)}) %collective-permute-start) | collective-permute-done | bytes 655392 | tf_op jit(solution)/shard_map/ppermute | solution.py:24
  39.4 1.5 collective-permute-start.3
  41.0 1.4 collective-permute-start.4
  42.5 19.6 %collective-permute-done.4.refs_5_.refs_6_ = bf16[1,6,128,256]{3,2,1,0:T(8,128)(2,1)} collective-permute-done((bf16[1,6,128,256]{3,2,1,0:T(8,128)(2,1)}, bf16[1,6,128,256]{3,2,1,0:T(8,128)(2,1)}, u32[]{:S(2)}, u32[]{:S(2)}) %collective-permute-start.4) | collective-permute-done | bytes 393248 | tf_op jit(solution)/shard_map/ppermute | solution.py:24
  62.6 1.6 collective-permute-start.5
  64.2 4.2 %all-to-all-start = ((bf16[16,2,24,256]{3,2,1,0:T(8,128)(2,1)}), bf16[16,2,24,256]{3,2,1,0:T(8,128)(2,1)}, u32[]{:S(2)}, u32[]{:S(2)}) async-start(bf16[16,2,24,256]{3,2,1,0:T(8,128)(2,1)} %bitcast.3), calls=%async_computation | async-start | bytes 786432 | tf_op jit(solution)/shard_map/all_to_all | solution.py:327
  68.4 10.4 %collective-permute-done.6.refs_6_.refs_8_ = bf16[1,10,128,256]{3,2,1,0:T(8,128)(2,1)} collective-permute-done((bf16[1,10,128,256]{3,2,1,0:T(8,128)(2,1)}, bf16[1,10,128,256]{3,2,1,0:T(8,128)(2,1)}, u32[]{:S(2)}, u32[]{:S(2)}) %collective-permute-start.6) | collective-permute-done | bytes 655392 | tf_op jit(solution)/shard_map/ppermute | solution.py:24
  78.8 1.5 collective-permute-start.16
  81.5 1.3 collective-permute-done.10.refs_10_.refs_12_
  84.7 4.2 %layer_first.1 = (bf16[96,1024]{1,0:T(8,128)(2,1)S(1)}, bf16[96,1024]{1,0:T(8,128)(2,1)S(1)}, bf16[96,1024]{1,0:T(8,128)(2,1)S(1)}, f32[2,96,256]{2,1,0:T(8,128)...) custom-call(bf16[16,2,24,256]{3,2,1,0:T(8,128)(2,1)} %all-to-all-done.refs_0_, ...), custom_call_target="tpu_custom_call" | custom-call | flops 503316480 | bytes 5242880 | tf_op jit(solution)/shard_map/layer_first/pallas_call | solution.py:374
  88.9 3.8 %collective-permute-done.14.refs_7_.refs_8_ = bf16[1,6,128,256]{3,2,1,0:T(8,128)(2,1)} collective-permute-done((bf16[1,6,128,256]{3,2,1,0:T(8,128)(2,1)}, bf16[1,6,128,256]{3,2,1,0:T(8,128)(2,1)}, u32[]{:S(2)}, u32[]{:S(2)}) %collective-permute-start.14) | collective-permute-done | bytes 393248 | tf_op jit(solution)/shard_map/ppermute | solution.py:24
  93.8 3.9 %collective-permute-done.16.refs_4_.refs_5_ = bf16[1,6,256,256]{3,2,1,0:T(8,128)(2,1)} collective-permute-done((bf16[1,6,256,256]{3,2,1,0:T(8,128)(2,1)}, bf16[1,6,256,256]{3,2,1,0:T(8,128)(2,1)}, u32[]{:S(2)}, u32[]{:S(2)}) %collective-permute-start.16) | collective-permute-done | bytes 786464 | tf_op jit(solution)/shard_map/ppermute | solution.py:24
  97.7 3.0 %layer_forward.2 = (bf16[96,1024]{1,0:T(8,128)(2,1)S(1)}, bf16[96,1024]{1,0:T(8,128)(2,1)S(1)}, f32[2,96,256]{2,1,0:T(8,128)S(1)}, f32[2,96,256]{2,1,0:T(8,128)S(1)}, bf16[8,5,256,256]{3,2,1,0:T(8,128)(2,1)S(1)}) custom-call(bf16[96,1024]{1,0:T(8,128)(2,1)S(1)} %get-tuple-element.58.refs_0_, bf16[96,1024]{1,0:T(8,128)(2,1)S(1)} %get-tuple-element.59.refs_1_, ...), custom_call_target="tpu_custom_call" | custom-call | flops 503316480 | bytes 5242880 | tf_op jit(solution)/shard_map/layer_forward/pallas_call | solution.py:374
  101.1 2.5 %collective-permute-done.17.refs_8_.refs_9_ = bf16[1,6,128,256]{3,2,1,0:T(8,128)(2,1)S(1)} collective-permute-done((bf16[1,6,128,256]{3,2,1,0:T(8,128)(2,1)}, bf16[1,6,128,256]{3,2,1,0:T(8,128)(2,1)S(1)}, u32[]{:S(2)}, u32[]{:S(2)}) %collective-permute-start.17) | collective-permute-done | bytes 393248 | tf_op jit(solution)/shard_map/ppermute | solution.py:24
  103.6 4.5 %collective-permute-done.15.refs_2_ = bf16[96,1024]{1,0:T(8,128)(2,1)S(1)} collective-permute-done((bf16[96,1024]{1,0:T(8,128)(2,1)S(1)}, bf16[96,1024]{1,0:T(8,128)(2,1)S(1)}, u32[]{:S(2)}, u32[]{:S(2)}) %collective-permute-start.15) | collective-permute-done | bytes 196640 | tf_op jit(solution)/shard_map/ppermute | solution.py:24
  108.6 1.9 %collective-permute-done.22.refs_13_.refs_14_ = bf16[1,6,128,256]{3,2,1,0:T(8,128)(2,1)S(1)} collective-permute-done((bf16[1,6,128,256]{3,2,1,0:T(8,128)(2,1)}, bf16[1,6,128,256]{3,2,1,0:T(8,128)(2,1)S(1)}, u32[]{:S(2)}, u32[]{:S(2)}) %collective-permute-start.22) | collective-permute-done | bytes 393248 | tf_op jit(solution)/shard_map/ppermute | solution.py:24
  110.5 2.4 %layer_forward.3 = (bf16[96,1024]{1,0:T(8,128)(2,1)S(1)}, bf16[96,1024]{1,0:T(8,128)(2,1)S(1)}, f32[2,96,256]{2,1,0:T(8,128)S(1)}, f32[2,96,256]{2,1,0:T(8,128)S(1)}, bf16[8,3,256,256]{3,2,1,0:T(8,128)(2,1)S(1)}) custom-call(bf16[96,1024]{1,0:T(8,128)(2,1)S(1)} %get-tuple-element.62.refs_0_, bf16[96,1024]{1,0:T(8,128)(2,1)S(1)} %get-tuple-element.63.refs_1_, ...), custom_call_target="tpu_custom_call" | custom-call | flops 301989888 | bytes 3145728 | tf_op jit(solution)/shard_map/layer_forward/pallas_call | solution.py:374
  113.3 6.7 %collective-permute-done.24.refs_2_ = bf16[96,1024]{1,0:T(8,128)(2,1)S(1)} collective-permute-done((bf16[96,1024]{1,0:T(8,128)(2,1)S(1)}, bf16[96,1024]{1,0:T(8,128)(2,1)S(1)}, u32[]{:S(2)}, u32[]{:S(2)}) %collective-permute-start.24) | collective-permute-done | bytes 196640 | tf_op jit(solution)/shard_map/ppermute | solution.py:24
  119.9 3.7 %layer_last.1 = (bf16[96,1024]{1,0:T(8,128)(2,1)S(1)}, bf16[96,1024]{1,0:T(8,128)(2,1)S(1)}, bf16[96,1024]{1,0:T(8,128)(2,1)S(1)}, bf16[8,3,256,256]{3,2,1,0:T(8,128)(2,1)}) custom-call(bf16[96,1024]{1,0:T(8,128)(2,1)S(1)} %get-tuple-element.72.refs_0_, bf16[96,1024]{1,0:T(8,128)(2,1)S(1)} %get-tuple-element.73.refs_1_, ...), custom_call_target="tpu_custom_call" | custom-call | flops 603979776 | bytes 3145728 | tf_op jit(solution)/shard_map/layer_last/pallas_call | solution.py:374
  124.0 5.8 %collective-permute-done.25.refs_2_ = bf16[96,1024]{1,0:T(8,128)(2,1)S(1)} collective-permute-done((bf16[96,1024]{1,0:T(8,128)(2,1)S(1)}, bf16[96,1024]{1,0:T(8,128)(2,1)S(1)}, u32[]{:S(2)}, u32[]{:S(2)}) %collective-permute-start.25) | collective-permute-done | bytes 196640 | tf_op jit(solution)/shard_map/ppermute | solution.py:24
  129.8 1.4 layer_backward.2
  131.6 1.7 %collective-permute-start.28 = (bf16[96,1024]{1,0:T(8,128)(2,1)S(1)}, bf16[96,1024]{1,0:T(8,128)(2,1)S(1)}, u32[]{:S(2)}, u32[]{:S(2)}) collective-permute-start(bf16[96,1024]{1,0:T(8,128)(2,1)S(1)} %get-tuple-element.88.refs_6_), channel_id=1, source_target_pairs={{0,1},{1,0},{2,3},{3,2},{4,5},{5,4},{6,7},{7,6},{8,9},{9,8},{10,11... | collective-permute-start | bytes 589832 | tf_op jit(solution)/shard_map/ppermute | solution.py:24
  133.3 5.3 %collective-permute-done.26.refs_2_ = bf16[96,1024]{1,0:T(8,128)(2,1)S(1)} collective-permute-done((bf16[96,1024]{1,0:T(8,128)(2,1)S(1)}, bf16[96,1024]{1,0:T(8,128)(2,1)S(1)}, u32[]{:S(2)}, u32[]{:S(2)}) %collective-permute-start.26) | collective-permute-done | bytes 196640 | tf_op jit(solution)/shard_map/ppermute | solution.py:24
  138.6 2.0 %layer_backward.3 = (bf16[96,1024]{1,0:T(8,128)(2,1)S(1)}, bf16[96,1024]{1,0:T(8,128)(2,1)S(1)}) custom-call(bf16[96,1024]{1,0:T(8,128)(2,1)S(1)} %get-tuple-element.78.refs_0_, bf16[96,1024]{1,0:T(8,128)(2,1)S(1)} %get-tuple-element.79.refs_1_, bf16[96,1024]{1,0:T(8,128)(2,1)S(1)} %collective-permute-done.26.refs_2_, ...), custom_call_target="tpu_custom_call" | custom-call | flops 503316480 | bytes 5242880 | tf_op jit(solution)/shard_map/layer_backward/pallas_call | solution.py:374
  141.0 1.4 collective-permute-done.28.refs_7_
  142.4 4.0 %collective-permute-done.27.refs_2_ = bf16[96,1024]{1,0:T(8,128)(2,1)S(1)} collective-permute-done((bf16[96,1024]{1,0:T(8,128)(2,1)S(1)}, bf16[96,1024]{1,0:T(8,128)(2,1)S(1)}, u32[]{:S(2)}, u32[]{:S(2)}) %collective-permute-start.27) | collective-permute-done | bytes 196640 | tf_op jit(solution)/shard_map/ppermute | solution.py:24
  146.4 2.1 %layer_final.1 = bf16[16,24,384]{2,1,0:T(8,128)(2,1)S(1)} custom-call(bf16[96,1024]{1,0:T(8,128)(2,1)S(1)} %get-tuple-element.83.refs_0_, bf16[96,1024]{1,0:T(8,128)(2,1)S(1)} %get-tuple-element.84.refs_1_, bf16[96,1024]{1,0:T(8,128)(2,1)S(1)} %collective-permute-done.27.refs_2_, f32[2,96,256]{2,1,0:T(8,128)S(1)} %get-tuple-element.85.refs_3_, ...), custom_call_target="tpu_custom_call" | custom-call | flops 503316480 | bytes 5242880 | tf_op jit(solution)/shard_map/layer_final/pallas_call | solution.py:374
  148.4 14.7 %all_to_all.10 = bf16[16,24,384]{2,1,0:T(8,128)(2,1)S(1)} all-to-all(bf16[16,24,384]{2,1,0:T(8,128)(2,1)S(1)} %layer_final.1), channel_id=1, replica_groups=mesh['groups'=2,'tm'=4,'chan'=4] {'tm','chan'}, dimensions={0} | all-to-all | bytes 589824 | tf_op jit(solution)/shard_map/all_to_all | solution.py:500
  (53 shorter events, 9.8 us)
Async XLA Ops:
  3.7 37.3 %copy-start = (bf16[1,10,256,256]{3,2,1,0:T(8,128)(2,1)S(1)}, bf16[1,10,256,256]{3,2,1,0:T(8,128)(2,1)}, u32[]{:S(2)}) copy-start(bf16[1,10,256,256]{3,2,1,0:T(8,128)(2,1)} %get-tuple-element.47.refs_1_.refs_3_) | copy-start | bytes 3932164
  3.7 34.5 %collective-permute-start.1 = (bf16[1,10,256,256]{3,2,1,0:T(8,128)(2,1)}, bf16[1,10,256,256]{3,2,1,0:T(8,128)(2,1)S(1)}, u32[]{:S(2)}, u32[]{:S(2)}) collective-permute-start(bf16[1,10,256,256]{3,2,1,0:T(8,128)(2,1)} %get-tuple-element.47.refs_1_.refs_3_), channel_id=1, source_target_pairs={{0,8},{4,12},{8,0},{12,4},{1,9},{5,13},{9,1},{13,5},{2,10},{6,14},... | collective-permute-start | bytes 3932168 | tf_op jit(solution)/shard_map/ppermute | solution.py:24
  6.7 31.5 %collective-permute-start = (bf16[1,10,128,256]{3,2,1,0:T(8,128)(2,1)}, bf16[1,10,128,256]{3,2,1,0:T(8,128)(2,1)}, u32[]{:S(2)}, u32[]{:S(2)}) collective-permute-start(bf16[1,10,128,256]{3,2,1,0:T(8,128)(2,1)} %get-tuple-element.46), channel_id=1, source_target_pairs={{0,2},{1,3},{2,0},{3,1},{4,6},{5,7},{6,4},{7,5},{8,10},{9,11},{10,... | collective-permute-start | bytes 1966088 | tf_op jit(solution)/shard_map/ppermute | solution.py:24
  39.0 23.2 %collective-permute-start.2 = (bf16[1,10,128,256]{3,2,1,0:T(8,128)(2,1)}, bf16[1,10,128,256]{3,2,1,0:T(8,128)(2,1)}, u32[]{:S(2)}, u32[]{:S(2)}) collective-permute-start(bf16[1,10,128,256]{3,2,1,0:T(8,128)(2,1)} %collective-permute-done.refs_3_.refs_5_), channel_id=1, source_target_pairs={{0,8},{4,12},{8,0},{12,4},{1,9},{5,13},{9,1},{13,5},{2,10},{6,14},... | collective-permute-start | bytes 1966088 | tf_op jit(solution)/shard_map/ppermute | solution.py:24
  39.4 22.7 %collective-permute-start.3 = (bf16[1,10,128,256]{3,2,1,0:T(8,128)(2,1)}, bf16[1,10,128,256]{3,2,1,0:T(8,128)(2,1)}, u32[]{:S(2)}, u32[]{:S(2)}) collective-permute-start(bf16[1,10,128,256]{3,2,1,0:T(8,128)(2,1)} %collective-permute-done.refs_3_.refs_5_), channel_id=1, source_target_pairs={{0,16},{16,0},{1,17},{17,1},{2,18},{18,2},{3,19},{19,3},{4,20},{20... | collective-permute-start | bytes 1966088 | tf_op jit(solution)/shard_map/ppermute | solution.py:24
  41.0 39.4 %collective-permute-start.7 = (bf16[1,10,256,256]{3,2,1,0:T(8,128)(2,1)S(1)}, bf16[1,10,256,256]{3,2,1,0:T(8,128)(2,1)}, u32[]{:S(2)}, u32[]{:S(2)}) collective-permute-start(bf16[1,10,256,256]{3,2,1,0:T(8,128)(2,1)S(1)} %copy-done), channel_id=1, source_target_pairs={{0,4},{4,0},{8,12},{12,8},{1,5},{5,1},{9,13},{13,9},{2,6},{6,2},{1... | collective-permute-start | bytes 3932168 | tf_op jit(solution)/shard_map/ppermute | solution.py:24
  41.0 21.2 %collective-permute-start.4 = (bf16[1,6,128,256]{3,2,1,0:T(8,128)(2,1)}, bf16[1,6,128,256]{3,2,1,0:T(8,128)(2,1)}, u32[]{:S(2)}, u32[]{:S(2)}) collective-permute-start(bf16[1,6,128,256]{3,2,1,0:T(8,128)(2,1)} %get-tuple-element.52), channel_id=1, source_target_pairs={{0,2},{1,3},{2,0},{3,1},{4,6},{5,7},{6,4},{7,5},{8,10},{9,11},{10,... | collective-permute-start | bytes 1179656 | tf_op jit(solution)/shard_map/ppermute | solution.py:24
  42.3 38.6 %collective-permute-start.8 = (bf16[1,10,256,256]{3,2,1,0:T(8,128)(2,1)S(1)}, bf16[1,10,256,256]{3,2,1,0:T(8,128)(2,1)}, u32[]{:S(2)}, u32[]{:S(2)}) collective-permute-start(bf16[1,10,256,256]{3,2,1,0:T(8,128)(2,1)S(1)} %collective-permute-done.1.refs_2_.refs_4_), channel_id=1, source_target_pairs={{0,4},{4,0},{8,12},{12,8},{1,5},{5,1},{9,13},{13,9},{2,6},{6,2},{1... | collective-permute-start | bytes 3932168 | tf_op jit(solution)/shard_map/ppermute | solution.py:24
  62.1 16.7 %collective-permute-start.6 = (bf16[1,10,128,256]{3,2,1,0:T(8,128)(2,1)}, bf16[1,10,128,256]{3,2,1,0:T(8,128)(2,1)}, u32[]{:S(2)}, u32[]{:S(2)}) collective-permute-start(bf16[1,10,128,256]{3,2,1,0:T(8,128)(2,1)} %collective-permute-done.2.refs_4_.refs_6_), channel_id=1, source_target_pairs={{0,16},{16,0},{1,17},{17,1},{2,18},{18,2},{3,19},{19,3},{4,20},{20... | collective-permute-start | bytes 1966088 | tf_op jit(solution)/shard_map/ppermute | solution.py:24
  62.6 17.7 %collective-permute-start.9 = (bf16[1,10,128,256]{3,2,1,0:T(8,128)(2,1)}, bf16[1,10,128,256]{3,2,1,0:T(8,128)(2,1)}, u32[]{:S(2)}, u32[]{:S(2)}) collective-permute-start(bf16[1,10,128,256]{3,2,1,0:T(8,128)(2,1)} %collective-permute-done.refs_3_.refs_5_), channel_id=1, source_target_pairs={{0,4},{4,0},{8,12},{12,8},{1,5},{5,1},{9,13},{13,9},{2,6},{6,2},{1... | collective-permute-start | bytes 1966088 | tf_op jit(solution)/shard_map/ppermute | solution.py:24
  62.6 18.2 %collective-permute-start.5 = (bf16[1,6,128,256]{3,2,1,0:T(8,128)(2,1)}, bf16[1,6,128,256]{3,2,1,0:T(8,128)(2,1)}, u32[]{:S(2)}, u32[]{:S(2)}) collective-permute-start(bf16[1,6,128,256]{3,2,1,0:T(8,128)(2,1)} %collective-permute-done.4.refs_5_.refs_6_), channel_id=1, source_target_pairs={{0,8},{4,12},{8,0},{12,4},{1,9},{5,13},{9,1},{13,5},{2,10},{6,14},... | collective-permute-start | bytes 1179656 | tf_op jit(solution)/shard_map/ppermute | solution.py:24
  64.2 17.3 %all-to-all-start = ((bf16[16,2,24,256]{3,2,1,0:T(8,128)(2,1)}), bf16[16,2,24,256]{3,2,1,0:T(8,128)(2,1)}, u32[]{:S(2)}, u32[]{:S(2)}) async-start(bf16[16,2,24,256]{3,2,1,0:T(8,128)(2,1)} %bitcast.3), calls=%async_computation | async-start | bytes 786432 | tf_op jit(solution)/shard_map/all_to_all | solution.py:327
  68.4 24.8 %copy-start.1 = (bf16[1,6,256,256]{3,2,1,0:T(8,128)(2,1)S(1)}, bf16[1,6,256,256]{3,2,1,0:T(8,128)(2,1)}, u32[]{:S(2)}) copy-start(bf16[1,6,256,256]{3,2,1,0:T(8,128)(2,1)} %get-tuple-element.65.refs_3_.refs_4_) | copy-start | bytes 2359300
  78.8 18.9 %collective-permute-start.16 = (bf16[1,6,256,256]{3,2,1,0:T(8,128)(2,1)}, bf16[1,6,256,256]{3,2,1,0:T(8,128)(2,1)}, u32[]{:S(2)}, u32[]{:S(2)}) collective-permute-start(bf16[1,6,256,256]{3,2,1,0:T(8,128)(2,1)} %get-tuple-element.65.refs_3_.refs_4_), channel_id=1, source_target_pairs={{0,8},{4,12},{8,0},{12,4},{1,9},{5,13},{9,1},{13,5},{2,10},{6,14},... | collective-permute-start | bytes 2359304 | tf_op jit(solution)/shard_map/ppermute | solution.py:24
  80.3 2.4 %collective-permute-start.10 = (bf16[1,10,128,256]{3,2,1,0:T(8,128)(2,1)}, bf16[1,10,128,256]{3,2,1,0:T(8,128)(2,1)}, u32[]{:S(2)}, u32[]{:S(2)}) collective-permute-start(bf16[1,10,128,256]{3,2,1,0:T(8,128)(2,1)} %collective-permute-done.2.refs_4_.refs_6_), channel_id=1, source_target_pairs={{0,4},{4,0},{8,12},{12,8},{1,5},{5,1},{9,13},{13,9},{2,6},{6,2},{1... | collective-permute-start | bytes 1966088 | tf_op jit(solution)/shard_map/ppermute | solution.py:24
  80.4 3.4 %collective-permute-start.11 = (bf16[1,10,128,256]{3,2,1,0:T(8,128)(2,1)}, bf16[1,10,128,256]{3,2,1,0:T(8,128)(2,1)}, u32[]{:S(2)}, u32[]{:S(2)}) collective-permute-start(bf16[1,10,128,256]{3,2,1,0:T(8,128)(2,1)} %collective-permute-done.3.refs_5_.refs_7_), channel_id=1, source_target_pairs={{0,4},{4,0},{8,12},{12,8},{1,5},{5,1},{9,13},{13,9},{2,6},{6,2},{1... | collective-permute-start | bytes 1966088 | tf_op jit(solution)/shard_map/ppermute | solution.py:24
  80.9 3.8 %collective-permute-start.12 = (bf16[1,10,128,256]{3,2,1,0:T(8,128)(2,1)}, bf16[1,10,128,256]{3,2,1,0:T(8,128)(2,1)}, u32[]{:S(2)}, u32[]{:S(2)}) collective-permute-start(bf16[1,10,128,256]{3,2,1,0:T(8,128)(2,1)} %collective-permute-done.6.refs_6_.refs_8_), channel_id=1, source_target_pairs={{0,4},{4,0},{8,12},{12,8},{1,5},{5,1},{9,13},{13,9},{2,6},{6,2},{1... | collective-permute-start | bytes 1966088 | tf_op jit(solution)/shard_map/ppermute | solution.py:24
  80.9 11.8 %collective-permute-start.14 = (bf16[1,6,128,256]{3,2,1,0:T(8,128)(2,1)}, bf16[1,6,128,256]{3,2,1,0:T(8,128)(2,1)}, u32[]{:S(2)}, u32[]{:S(2)}) collective-permute-start(bf16[1,6,128,256]{3,2,1,0:T(8,128)(2,1)} %collective-permute-done.4.refs_5_.refs_6_), channel_id=1, source_target_pairs={{0,16},{16,0},{1,17},{17,1},{2,18},{18,2},{3,19},{19,3},{4,20},{20... | collective-permute-start | bytes 1179656 | tf_op jit(solution)/shard_map/ppermute | solution.py:24
  88.8 8.8 %collective-permute-start.13 = (bf16[96,1024]{1,0:T(8,128)(2,1)S(1)}, bf16[96,1024]{1,0:T(8,128)(2,1)S(1)}, u32[]{:S(2)}, u32[]{:S(2)}) collective-permute-start(bf16[96,1024]{1,0:T(8,128)(2,1)S(1)} %get-tuple-element.59.refs_1_), channel_id=1, source_target_pairs={{0,1},{1,0},{2,3},{3,2},{4,5},{5,4},{6,7},{7,6},{8,9},{9,8},{10,11... | collective-permute-start | bytes 589832 | tf_op jit(solution)/shard_map/ppermute | solution.py:24
  92.7 10.9 %collective-permute-start.17 = (bf16[1,6,128,256]{3,2,1,0:T(8,128)(2,1)}, bf16[1,6,128,256]{3,2,1,0:T(8,128)(2,1)S(1)}, u32[]{:S(2)}, u32[]{:S(2)}) collective-permute-start(bf16[1,6,128,256]{3,2,1,0:T(8,128)(2,1)} %collective-permute-done.5.refs_6_.refs_7_), channel_id=1, source_target_pairs={{0,16},{16,0},{1,17},{17,1},{2,18},{18,2},{3,19},{19,3},{4,20},{20... | collective-permute-start | bytes 1179656 | tf_op jit(solution)/shard_map/ppermute | solution.py:24
  93.3 17.3 %collective-permute-start.18 = (bf16[1,6,256,256]{3,2,1,0:T(8,128)(2,1)S(1)}, bf16[1,6,256,256]{3,2,1,0:T(8,128)(2,1)S(1)}, u32[]{:S(2)}, u32[]{:S(2)}) collective-permute-start(bf16[1,6,256,256]{3,2,1,0:T(8,128)(2,1)S(1)} %copy-done.1), channel_id=1, source_target_pairs={{0,4},{4,0},{8,12},{12,8},{1,5},{5,1},{9,13},{13,9},{2,6},{6,2},{1... | collective-permute-start | bytes 2359304 | tf_op jit(solution)/shard_map/ppermute | solution.py:24
  93.3 14.8 %collective-permute-start.20 = (bf16[1,6,128,256]{3,2,1,0:T(8,128)(2,1)}, bf16[1,6,128,256]{3,2,1,0:T(8,128)(2,1)S(1)}, u32[]{:S(2)}, u32[]{:S(2)}) collective-permute-start(bf16[1,6,128,256]{3,2,1,0:T(8,128)(2,1)} %collective-permute-done.4.refs_5_.refs_6_), channel_id=1, source_target_pairs={{0,4},{4,0},{8,12},{12,8},{1,5},{5,1},{9,13},{13,9},{2,6},{6,2},{1... | collective-permute-start | bytes 1179656 | tf_op jit(solution)/shard_map/ppermute | solution.py:24
  97.7 12.8 %collective-permute-start.19 = (bf16[1,6,256,256]{3,2,1,0:T(8,128)(2,1)}, bf16[1,6,256,256]{3,2,1,0:T(8,128)(2,1)S(1)}, u32[]{:S(2)}, u32[]{:S(2)}) collective-permute-start(bf16[1,6,256,256]{3,2,1,0:T(8,128)(2,1)} %collective-permute-done.16.refs_4_.refs_5_), channel_id=1, source_target_pairs={{0,4},{4,0},{8,12},{12,8},{1,5},{5,1},{9,13},{13,9},{2,6},{6,2},{1... | collective-permute-start | bytes 2359304 | tf_op jit(solution)/shard_map/ppermute | solution.py:24
  100.7 7.4 %collective-permute-start.15 = (bf16[96,1024]{1,0:T(8,128)(2,1)S(1)}, bf16[96,1024]{1,0:T(8,128)(2,1)S(1)}, u32[]{:S(2)}, u32[]{:S(2)}) collective-permute-start(bf16[96,1024]{1,0:T(8,128)(2,1)S(1)} %get-tuple-element.63.refs_1_), channel_id=1, source_target_pairs={{0,1},{1,0},{2,3},{3,2},{4,5},{5,4},{6,7},{7,6},{8,9},{9,8},{10,11... | collective-permute-start | bytes 589832 | tf_op jit(solution)/shard_map/ppermute | solution.py:24
  103.6 5.0 %collective-permute-start.21 = (bf16[1,6,128,256]{3,2,1,0:T(8,128)(2,1)}, bf16[1,6,128,256]{3,2,1,0:T(8,128)(2,1)S(1)}, u32[]{:S(2)}, u32[]{:S(2)}) collective-permute-start(bf16[1,6,128,256]{3,2,1,0:T(8,128)(2,1)} %collective-permute-done.5.refs_6_.refs_7_), channel_id=1, source_target_pairs={{0,4},{4,0},{8,12},{12,8},{1,5},{5,1},{9,13},{13,9},{2,6},{6,2},{1... | collective-permute-start | bytes 1179656 | tf_op jit(solution)/shard_map/ppermute | solution.py:24
  108.1 2.4 %collective-permute-start.22 = (bf16[1,6,128,256]{3,2,1,0:T(8,128)(2,1)}, bf16[1,6,128,256]{3,2,1,0:T(8,128)(2,1)S(1)}, u32[]{:S(2)}, u32[]{:S(2)}) collective-permute-start(bf16[1,6,128,256]{3,2,1,0:T(8,128)(2,1)} %collective-permute-done.14.refs_7_.refs_8_), channel_id=1, source_target_pairs={{0,4},{4,0},{8,12},{12,8},{1,5},{5,1},{9,13},{13,9},{2,6},{6,2},{1... | collective-permute-start | bytes 1179656 | tf_op jit(solution)/shard_map/ppermute | solution.py:24
  108.1 2.4 %collective-permute-start.23 = (bf16[1,6,128,256]{3,2,1,0:T(8,128)(2,1)S(1)}, bf16[1,6,128,256]{3,2,1,0:T(8,128)(2,1)S(1)}, u32[]{:S(2)}, u32[]{:S(2)}) collective-permute-start(bf16[1,6,128,256]{3,2,1,0:T(8,128)(2,1)S(1)} %collective-permute-done.17.refs_8_.refs_9_), channel_id=1, source_target_pairs={{0,4},{4,0},{8,12},{12,8},{1,5},{5,1},{9,13},{13,9},{2,6},{6,2},{1... | collective-permute-start | bytes 1179656 | tf_op jit(solution)/shard_map/ppermute | solution.py:24
  112.9 7.0 %collective-permute-start.24 = (bf16[96,1024]{1,0:T(8,128)(2,1)S(1)}, bf16[96,1024]{1,0:T(8,128)(2,1)S(1)}, u32[]{:S(2)}, u32[]{:S(2)}) collective-permute-start(bf16[96,1024]{1,0:T(8,128)(2,1)S(1)} %get-tuple-element.73.refs_1_), channel_id=1, source_target_pairs={{0,1},{1,0},{2,3},{3,2},{4,5},{5,4},{6,7},{7,6},{8,9},{9,8},{10,11... | collective-permute-start | bytes 589832 | tf_op jit(solution)/shard_map/ppermute | solution.py:24
  123.6 6.2 %collective-permute-start.25 = (bf16[96,1024]{1,0:T(8,128)(2,1)S(1)}, bf16[96,1024]{1,0:T(8,128)(2,1)S(1)}, u32[]{:S(2)}, u32[]{:S(2)}) collective-permute-start(bf16[96,1024]{1,0:T(8,128)(2,1)S(1)} %get-tuple-element.74.refs_1_), channel_id=1, source_target_pairs={{0,1},{1,0},{2,3},{3,2},{4,5},{5,4},{6,7},{7,6},{8,9},{9,8},{10,11... | collective-permute-start | bytes 589832 | tf_op jit(solution)/shard_map/ppermute | solution.py:24
  131.2 7.4 %collective-permute-start.26 = (bf16[96,1024]{1,0:T(8,128)(2,1)S(1)}, bf16[96,1024]{1,0:T(8,128)(2,1)S(1)}, u32[]{:S(2)}, u32[]{:S(2)}) collective-permute-start(bf16[96,1024]{1,0:T(8,128)(2,1)S(1)} %get-tuple-element.79.refs_1_), channel_id=1, source_target_pairs={{0,1},{1,0},{2,3},{3,2},{4,5},{5,4},{6,7},{7,6},{8,9},{9,8},{10,11... | collective-permute-start | bytes 589832 | tf_op jit(solution)/shard_map/ppermute | solution.py:24
  131.6 10.8 %collective-permute-start.28 = (bf16[96,1024]{1,0:T(8,128)(2,1)S(1)}, bf16[96,1024]{1,0:T(8,128)(2,1)S(1)}, u32[]{:S(2)}, u32[]{:S(2)}) collective-permute-start(bf16[96,1024]{1,0:T(8,128)(2,1)S(1)} %get-tuple-element.88.refs_6_), channel_id=1, source_target_pairs={{0,1},{1,0},{2,3},{3,2},{4,5},{5,4},{6,7},{7,6},{8,9},{9,8},{10,11... | collective-permute-start | bytes 589832 | tf_op jit(solution)/shard_map/ppermute | solution.py:24
  140.6 5.7 %collective-permute-start.27 = (bf16[96,1024]{1,0:T(8,128)(2,1)S(1)}, bf16[96,1024]{1,0:T(8,128)(2,1)S(1)}, u32[]{:S(2)}, u32[]{:S(2)}) collective-permute-start(bf16[96,1024]{1,0:T(8,128)(2,1)S(1)} %get-tuple-element.84.refs_1_), channel_id=1, source_target_pairs={{0,1},{1,0},{2,3},{3,2},{4,5},{5,4},{6,7},{7,6},{8,9},{9,8},{10,11... | collective-permute-start | bytes 589832 | tf_op jit(solution)/shard_map/ppermute | solution.py:24
  (2 other events, 22.3 us)
